TPU v7x, 32 devices: a whole 2x2x4 slice. The times are simulated.
32 devices in a mesh: groups: 2 (over y), brick: 4 (over z), chan: 2 (over x), sub: 2 (over core).
Axes of the slice: x: 2, y: 2, z: 4, core: 2. Of those that a mesh axis runs over, the one named last changes fastest.
Arguments:
- features: bfloat16 [16384, 256], P(('groups', 'brick', 'chan', 'sub')), parts along dimension 0, may hold values from -6 to 6
- scan_order: int32 [32, 512], P(('groups', 'brick', 'chan', 'sub')), parts along dimension 0, may hold values from 0 to 511, each once within a row
- kernel_map: int32 [256, 27], P(('groups', 'brick', 'sub')), parts along dimension 0, may hold values from 0 to 20, as said below
- halo_send: int32 [32, 2], P(('groups', 'brick', 'sub')), parts along dimension 0, may hold values from 0 to 15, as said below
- down_route: int32 [256, 1], P(('groups', 'brick', 'sub')), parts along dimension 0, may hold values from 0 to 7; in each aligned block of 16 rows (0 to 15, 16 to 31, ...) at most 4 rows name the same one
- conv1_weight: bfloat16 [27, 256, 256], P(None, 'chan'), may hold values from -0.078125 to 0.078125
- conv2_weight: bfloat16 [27, 256, 256], P(None, 'chan'), may hold values from -0.078125 to 0.078125
- down_weight: bfloat16 [8, 256, 256], P(None, 'chan'), may hold values from -0.125 to 0.125
- gain_first: float32 [256], P('chan'), may hold values from 0.1 to 1.9
- bias_first: float32 [256], P('chan'), may hold values from -3 to 3
- gain_second: float32 [256], P('chan'), may hold values from 0.1 to 1.9
- bias_second: float32 [256], P('chan'), may hold values from -3 to 3
- gain_down: float32 [256], P('chan'), may hold values from 0.1 to 1.9
- bias_down: float32 [256], P('chan'), may hold values from -3 to 3
Outputs:
- coarse_out: bfloat16 [16, 256, 256], P(('groups', 'brick', 'sub'), 'chan'), parts along dimension 0
There are 2 independent parts, one for each index of `groups`. A program takes and returns all parts, laid end to end along the dimension named above; an argument that names none is the same for every part. Nothing has to cross between parts.
Inputs may be any that keep to these rules, and one draw needn't show every extreme that they name: `scan_order`: each row is an order of the 512 local rows of one device, each once. `kernel_map`: entries index an owner's extended list: own blocks below 16, then 2 blocks from the previous owner, 2 from the next, and 20 for an absent neighbour block. Offset 13 of block n always names n itself. `halo_send`: row 2 o lists the blocks owner o sends to owner o + 1, row 2 o + 1 those it sends to owner o - 1; each row names 2 distinct blocks. `down_route`: within the 16 rows of one owner no destination is named by more than 4 rows.
All inputs are finite; a program needn't handle non-finite values.
Results may differ from a plain program's by a relative error of at most 0.014.
Values may be sent and summed in bfloat16 or wider, within the bound.
No kernel may reach another device: no remote copies, remote signals or barrier semaphores. Data moves between devices by JAX's collectives and lax.ppermute only.
A program may use at most 64 MiB of HBM per device.

v0:
```python
import jax
import jax.numpy as jnp
from jax import lax
from jax.sharding import PartitionSpec as P

BLK = 64


def from_behind(block, axis, distance):
    devices = range(lax.axis_size(axis))
    route = [(i - distance, i) for i in devices if i - distance in devices]
    return lax.ppermute(block, axis, route)


def neighbours(blocks, step_by):
    return from_behind(blocks, ("brick", "sub"), step_by)


def convolve(extended, weight, kernel_map, pattern):
    block_count = kernel_map.shape[0]
    width_out = weight.shape[1]
    groups = weight.shape[0] // 3
    weight_groups = weight.reshape(groups, 3, width_out, weight.shape[2])
    index_groups = kernel_map.T.reshape(groups, 3, block_count)
    offsets = jnp.arange(3, dtype=jnp.int32)[:, None]

    def one_group(running, inputs):
        group_weight, indices = inputs
        product = jnp.einsum(pattern, group_weight, extended, preferred_element_type=jnp.float32)
        return (running + jnp.sum(product[offsets, :, indices], axis=0), None)

    initial = jnp.zeros((block_count, width_out, BLK), jnp.float32)
    running, _ = lax.scan(one_group, initial, (weight_groups, index_groups))
    return running.transpose(1, 0, 2).reshape(width_out, block_count * BLK)


def body(
    features,
    scan_order,
    kernel_map,
    halo_send,
    down_route,
    conv1_weight,
    conv2_weight,
    down_weight,
    gain_first,
    bias_first,
    gain_second,
    bias_second,
    gain_down,
    bias_down,
):
    owners = lax.axis_size(("brick", "sub"))
    per_owner = features.shape[0] // owners
    channels = features.shape[1]
    width_out = conv1_weight.shape[1]
    block_count = kernel_map.shape[0]
    channel_start = lax.axis_index("chan") * width_out
    ordered = features[scan_order[0]].reshape(owners, per_owner, channels)
    regrouped = lax.all_to_all(ordered, ("brick", "sub"), split_axis=0, concat_axis=0, tiled=True)
    owner_rows = lax.all_gather(regrouped, "chan", axis=1, tiled=True)
    row_blocks = owner_rows.reshape(block_count, BLK, channels)
    from_lower = neighbours(row_blocks[halo_send[0]], 1)
    from_upper = neighbours(row_blocks[halo_send[1]], -1)
    empty_rows = jnp.zeros((1, BLK, channels), jnp.bfloat16)
    extended = jnp.concatenate([row_blocks, from_lower, from_upper, empty_rows], axis=0)
    conv_first = convolve(extended, conv1_weight, kernel_map, "kdc,brc->kdbr")
    hidden = jax.nn.relu(conv_first * gain_first[:, None] + bias_first[:, None]).astype(
        jnp.bfloat16
    )
    hidden_blocks = hidden.reshape(width_out, block_count, BLK)
    empty_cols = jnp.zeros((channels, 1, BLK), jnp.bfloat16)
    all_channels = lax.all_gather(hidden_blocks, "chan", axis=0, tiled=True)
    lower_cols = neighbours(all_channels[:, halo_send[0]], 1)
    upper_cols = neighbours(all_channels[:, halo_send[1]], -1)
    widened_hidden = jnp.concatenate([all_channels, lower_cols, upper_cols, empty_cols], axis=1)
    second = convolve(widened_hidden, conv2_weight, kernel_map, "kdc,cbr->kdbr")
    residual = lax.dynamic_slice_in_dim(
        owner_rows.reshape(block_count * BLK, channels), channel_start, width_out, 1
    )
    refined = jax.nn.relu(
        second * gain_second[:, None] + bias_second[:, None] + residual.T.astype(jnp.float32)
    ).astype(jnp.bfloat16)
    children = refined.reshape(width_out, block_count, 8, 8)
    partial_value = jnp.einsum(
        "oic,inoq->cnq", down_weight, children, preferred_element_type=jnp.float32
    )
    coarse = lax.psum_scatter(
        partial_value.reshape(width_out * lax.axis_size("chan"), block_count * 8).astype(
            jnp.bfloat16
        ),
        "chan",
        scatter_dimension=0,
        tiled=True,
    ).astype(jnp.float32)
    tile_values = jax.nn.relu(coarse * gain_down[:, None] + bias_down[:, None]).astype(jnp.bfloat16)
    tile_values = tile_values.reshape(width_out, block_count, 8)
    capacity = max(2, 2 * block_count // owners)
    destination = down_route[:, 0]
    onehot = (destination[:, None] == jnp.arange(owners, dtype=jnp.int32)[None, :]).astype(
        jnp.int32
    )
    earlier = jnp.sum((jnp.cumsum(onehot, axis=0) - onehot) * onehot, axis=1)
    position = destination * capacity + earlier
    selector = (
        position[None, :] == jnp.arange(owners * capacity, dtype=jnp.int32)[:, None]
    ).astype(jnp.bfloat16)
    outgoing = jnp.einsum(
        "pn,cnq->cpq", selector, tile_values, preferred_element_type=jnp.float32
    ).astype(jnp.bfloat16)
    outgoing = outgoing.reshape(width_out, owners, capacity * 8)
    arrived = lax.all_to_all(outgoing, ("brick", "sub"), split_axis=1, concat_axis=2, tiled=True)
    return arrived.reshape(1, width_out, owners * capacity * 8)


def solution(mesh):
    placed = (
        P(("groups", "brick", "chan", "sub"), None),
        P(("groups", "brick", "chan", "sub"), None),
        P(("groups", "brick", "sub"), None),
        P(("groups", "brick", "sub"), None),
        P(("groups", "brick", "sub"), None),
        P(None, "chan", None),
        P(None, "chan", None),
        P(None, "chan", None),
        P("chan"),
        P("chan"),
        P("chan"),
        P("chan"),
        P("chan"),
        P("chan"),
    )
    return jax.shard_map(
        body,
        mesh=mesh,
        in_specs=placed,
        out_specs=P(("groups", "brick", "sub"), "chan", None),
        check_vma=False,
    )
```

profile of v0, /device:TPU:0, one launch (start us, length us, event | category | flops | bytes accessed | tf_op | source)
XLA Modules:
  0.0 223.3 jit_solution(14736609764272023862)
XLA Ops:
  7.3 3.2 %gather_fusion.2 = bf16[512,256]{1,0:T(8,128)(2,1)} fusion(bf16[512,256]{1,0:T(8,128)(2,1)} %param.18, s32[1024]{0:T(1024)S(1)} %pad_clamp_fusion.2), kind=kCustom, calls=%fused_computation.2 | custom fusion | bytes 526336 | tf_op jit(solution)/shard_map/gather | solution.py:59
  10.5 6.3 %all-to-all-start = ((bf16[8,64,256]{2,1,0:T(8,128)(2,1)}), bf16[8,64,256]{2,1,0:T(8,128)(2,1)S(1)}, u32[]{:S(2)}, u32[]{:S(2)}) async-start(bf16[8,64,256]{2,1,0:T(8,128)(2,1)} %bitcast.4), calls=%async_computation | async-start | bytes 524288 | tf_op jit(solution)/shard_map/all_to_all | solution.py:60
  16.9 9.6 %all-to-all-done = bf16[8,64,256]{2,1,0:T(8,128)(2,1)S(1)} async-done(((bf16[8,64,256]{2,1,0:T(8,128)(2,1)}), bf16[8,64,256]{2,1,0:T(8,128)(2,1)S(1)}, u32[]{:S(2)}, u32[]{:S(2)}) %all-to-all-start) | async-done | bytes 262176 | tf_op jit(solution)/shard_map/all_to_all | solution.py:60
  26.5 8.3 %all_gather.6 = bf16[8,128,256]{2,1,0:T(8,128)(2,1)S(1)} all-gather(bf16[8,64,256]{2,1,0:T(8,128)(2,1)S(1)} %all-to-all-done), channel_id=1, replica_groups=mesh['groups'=2,'brick'=4,'chan'=2,'sub'=2] {'chan'}, dimensions={1}, use_global_device_ids=true | all-gather | bytes 786432 | tf_op jit(solution)/shard_map/all_gather | solution.py:61
  41.0 65.6 %while.22 = (s32[]{:T(128)}, f32[16,128,64]{1,2,0:T(8,128)}, bf16[9,3,128,256]{3,2,1,0:T(8,128)(2,1)}, bf16[21,64,256]{2,1,0:T(8,128)(2,1)S(1)}, s32[9,3,16]{2,0...) while((s32[]{:T(128)}, f32[16,128,64]{1,2,0:T(8,128)}, bf16[9,3,128,256]{3,2,1,0:T(8,128)(2,1)}, ...), condition=%wide.region_2.3_spmd.clone, body=%wide.region_0.2_spmd.clone.sunk | while | flops 264765728 | bytes 9766655 | solution.py:33
  41.0 2.8 %fusion.54 = f32[3,128,21,64]{1,3,2,0:T(8,128)} fusion(bf16[21,64,256]{2,1,0:T(8,128)(2,1)S(1)} %get-tuple-element.234, bf16[9,3,128,256]{3,2,1,0:T(8,128)(2,1)} %get-tuple-element.233, s32[]{:T(128)} %get-tuple-element.223), kind=kOutput, calls=%fused_computation.9.clone.1 | convolution fusion | flops 264241152 | bytes 2949632 | tf_op jit(solution)/shard_map/while/body/eval_jaxpr/kdc,brc->kdbr/dot_general | solution.py:29
  47.4 2.8 %fusion.54 = f32[3,128,21,64]{1,3,2,0:T(8,128)} fusion(bf16[21,64,256]{2,1,0:T(8,128)(2,1)S(1)} %get-tuple-element.234, bf16[9,3,128,256]{3,2,1,0:T(8,128)(2,1)} %get-tuple-element.233, s32[]{:T(128)} %get-tuple-element.223), kind=kOutput, calls=%fused_computation.9.clone.1 | convolution fusion | flops 264241152 | bytes 2949632 | tf_op jit(solution)/shard_map/while/body/eval_jaxpr/kdc,brc->kdbr/dot_general | solution.py:29
  50.4 2.4 %gather_fusion = f32[48,128,64]{1,2,0:T(8,128)S(1)} fusion(f32[3,128,21,64]{1,3,2,0:T(8,128)} %fusion.54, s32[48]{0:T(128)S(1)} %reshape.336), kind=kCustom, calls=%fused_computation.clone.clone.1 | custom fusion | bytes 3146112 | tf_op jit(solution)/shard_map/while/body/eval_jaxpr/gather | solution.py:30
  54.8 2.8 %fusion.54 = f32[3,128,21,64]{1,3,2,0:T(8,128)} fusion(bf16[21,64,256]{2,1,0:T(8,128)(2,1)S(1)} %get-tuple-element.234, bf16[9,3,128,256]{3,2,1,0:T(8,128)(2,1)} %get-tuple-element.233, s32[]{:T(128)} %get-tuple-element.223), kind=kOutput, calls=%fused_computation.9.clone.1 | convolution fusion | flops 264241152 | bytes 2949632 | tf_op jit(solution)/shard_map/while/body/eval_jaxpr/kdc,brc->kdbr/dot_general | solution.py:29
  62.2 2.8 %fusion.54 = f32[3,128,21,64]{1,3,2,0:T(8,128)} fusion(bf16[21,64,256]{2,1,0:T(8,128)(2,1)S(1)} %get-tuple-element.234, bf16[9,3,128,256]{3,2,1,0:T(8,128)(2,1)} %get-tuple-element.233, s32[]{:T(128)} %get-tuple-element.223), kind=kOutput, calls=%fused_computation.9.clone.1 | convolution fusion | flops 264241152 | bytes 2949632 | tf_op jit(solution)/shard_map/while/body/eval_jaxpr/kdc,brc->kdbr/dot_general | solution.py:29
  65.2 2.4 %gather_fusion = f32[48,128,64]{1,2,0:T(8,128)S(1)} fusion(f32[3,128,21,64]{1,3,2,0:T(8,128)} %fusion.54, s32[48]{0:T(128)S(1)} %reshape.336), kind=kCustom, calls=%fused_computation.clone.clone.1 | custom fusion | bytes 3146112 | tf_op jit(solution)/shard_map/while/body/eval_jaxpr/gather | solution.py:30
  69.6 2.8 %fusion.54 = f32[3,128,21,64]{1,3,2,0:T(8,128)} fusion(bf16[21,64,256]{2,1,0:T(8,128)(2,1)S(1)} %get-tuple-element.234, bf16[9,3,128,256]{3,2,1,0:T(8,128)(2,1)} %get-tuple-element.233, s32[]{:T(128)} %get-tuple-element.223), kind=kOutput, calls=%fused_computation.9.clone.1 | convolution fusion | flops 264241152 | bytes 2949632 | tf_op jit(solution)/shard_map/while/body/eval_jaxpr/kdc,brc->kdbr/dot_general | solution.py:29
  72.6 2.4 %gather_fusion = f32[48,128,64]{1,2,0:T(8,128)S(1)} fusion(f32[3,128,21,64]{1,3,2,0:T(8,128)} %fusion.54, s32[48]{0:T(128)S(1)} %reshape.336), kind=kCustom, calls=%fused_computation.clone.clone.1 | custom fusion | bytes 3146112 | tf_op jit(solution)/shard_map/while/body/eval_jaxpr/gather | solution.py:30
  77.0 2.8 %fusion.54 = f32[3,128,21,64]{1,3,2,0:T(8,128)} fusion(bf16[21,64,256]{2,1,0:T(8,128)(2,1)S(1)} %get-tuple-element.234, bf16[9,3,128,256]{3,2,1,0:T(8,128)(2,1)} %get-tuple-element.233, s32[]{:T(128)} %get-tuple-element.223), kind=kOutput, calls=%fused_computation.9.clone.1 | convolution fusion | flops 264241152 | bytes 2949632 | tf_op jit(solution)/shard_map/while/body/eval_jaxpr/kdc,brc->kdbr/dot_general | solution.py:29
  84.4 2.8 %fusion.54 = f32[3,128,21,64]{1,3,2,0:T(8,128)} fusion(bf16[21,64,256]{2,1,0:T(8,128)(2,1)S(1)} %get-tuple-element.234, bf16[9,3,128,256]{3,2,1,0:T(8,128)(2,1)} %get-tuple-element.233, s32[]{:T(128)} %get-tuple-element.223), kind=kOutput, calls=%fused_computation.9.clone.1 | convolution fusion | flops 264241152 | bytes 2949632 | tf_op jit(solution)/shard_map/while/body/eval_jaxpr/kdc,brc->kdbr/dot_general | solution.py:29
  91.8 2.8 %fusion.54 = f32[3,128,21,64]{1,3,2,0:T(8,128)} fusion(bf16[21,64,256]{2,1,0:T(8,128)(2,1)S(1)} %get-tuple-element.234, bf16[9,3,128,256]{3,2,1,0:T(8,128)(2,1)} %get-tuple-element.233, s32[]{:T(128)} %get-tuple-element.223), kind=kOutput, calls=%fused_computation.9.clone.1 | convolution fusion | flops 264241152 | bytes 2949632 | tf_op jit(solution)/shard_map/while/body/eval_jaxpr/kdc,brc->kdbr/dot_general | solution.py:29
  99.2 2.8 %fusion.54 = f32[3,128,21,64]{1,3,2,0:T(8,128)} fusion(bf16[21,64,256]{2,1,0:T(8,128)(2,1)S(1)} %get-tuple-element.234, bf16[9,3,128,256]{3,2,1,0:T(8,128)(2,1)} %get-tuple-element.233, s32[]{:T(128)} %get-tuple-element.223), kind=kOutput, calls=%fused_computation.9.clone.1 | convolution fusion | flops 264241152 | bytes 2949632 | tf_op jit(solution)/shard_map/while/body/eval_jaxpr/kdc,brc->kdbr/dot_general | solution.py:29
  107.8 8.0 %all_gather.7 = bf16[256,16,64]{0,2,1:T(8,128)(2,1)S(1)} all-gather(bf16[128,16,64]{0,2,1:T(8,128)(2,1)S(1)} %fusion.32), channel_id=1, replica_groups=mesh['groups'=2,'brick'=4,'chan'=2,'sub'=2] {'chan'}, dimensions={0}, use_global_device_ids=true | all-gather | bytes 786432 | tf_op jit(solution)/shard_map/all_gather | solution.py:73
  116.9 3.6 %collective-permute-start.2 = (bf16[256,2,64]{0,2,1:T(8,128)(2,1)S(1)}, bf16[256,2,64]{0,2,1:T(8,128)(2,1)S(1)}, u32[]{:S(2)}, u32[]{:S(2)}) collective-permute-start(bf16[256,2,64]{0,2,1:T(8,128)(2,1)S(1)} %bitcast.113), channel_id=1, source_target_pairs={{0,1},{1,4},{4,5},{5,8},{8,9},{9,12},{12,13},{2,3},{3,6},{6,7},{7,... | collective-permute-start | bytes 196616 | tf_op jit(solution)/shard_map/ppermute | solution.py:12
  122.0 3.2 %collective-permute-done.3 = bf16[256,2,64]{0,2,1:T(8,128)(2,1)S(1)} collective-permute-done((bf16[256,2,64]{0,2,1:T(8,128)(2,1)S(1)}, bf16[256,2,64]{0,2,1:T(8,128)(2,1)S(1)}, u32[]{:S(2)}, u32[]{:S(2)}) %collective-permute-start.3) | collective-permute-done | bytes 65568 | tf_op jit(solution)/shard_map/ppermute | solution.py:12
  125.4 65.8 %while.23 = (s32[]{:T(128)}, f32[16,128,64]{1,2,0:T(8,128)}, bf16[9,3,128,256]{3,2,1,0:T(8,128)(2,1)}, bf16[256,21,64]{0,2,1:T(8,128)(2,1)S(1)}, s32[9,3,16]{2,0...) while((s32[]{:T(128)}, f32[16,128,64]{1,2,0:T(8,128)}, bf16[9,3,128,256]{3,2,1,0:T(8,128)(2,1)}, ...), condition=%wide.region_5.6_spmd.clone, body=%wide.region_3.5_spmd.clone.sunk | while | flops 264765728 | bytes 9766655 | solution.py:33
  125.4 2.8 %fusion.59 = f32[3,128,21,64]{1,3,2,0:T(8,128)} fusion(bf16[256,21,64]{0,2,1:T(8,128)(2,1)S(1)} %get-tuple-element.258, bf16[9,3,128,256]{3,2,1,0:T(8,128)(2,1)} %get-tuple-element.257, s32[]{:T(128)} %get-tuple-element.247), kind=kOutput, calls=%fused_computation.22.clone.1 | convolution fusion | flops 264241152 | bytes 2949632 | tf_op jit(solution)/shard_map/while/body/eval_jaxpr/kdc,cbr->kdbr/dot_general | solution.py:29
  131.8 2.8 %fusion.59 = f32[3,128,21,64]{1,3,2,0:T(8,128)} fusion(bf16[256,21,64]{0,2,1:T(8,128)(2,1)S(1)} %get-tuple-element.258, bf16[9,3,128,256]{3,2,1,0:T(8,128)(2,1)} %get-tuple-element.257, s32[]{:T(128)} %get-tuple-element.247), kind=kOutput, calls=%fused_computation.22.clone.1 | convolution fusion | flops 264241152 | bytes 2949632 | tf_op jit(solution)/shard_map/while/body/eval_jaxpr/kdc,cbr->kdbr/dot_general | solution.py:29
  139.2 2.8 %fusion.59 = f32[3,128,21,64]{1,3,2,0:T(8,128)} fusion(bf16[256,21,64]{0,2,1:T(8,128)(2,1)S(1)} %get-tuple-element.258, bf16[9,3,128,256]{3,2,1,0:T(8,128)(2,1)} %get-tuple-element.257, s32[]{:T(128)} %get-tuple-element.247), kind=kOutput, calls=%fused_computation.22.clone.1 | convolution fusion | flops 264241152 | bytes 2949632 | tf_op jit(solution)/shard_map/while/body/eval_jaxpr/kdc,cbr->kdbr/dot_general | solution.py:29
  146.6 2.8 %fusion.59 = f32[3,128,21,64]{1,3,2,0:T(8,128)} fusion(bf16[256,21,64]{0,2,1:T(8,128)(2,1)S(1)} %get-tuple-element.258, bf16[9,3,128,256]{3,2,1,0:T(8,128)(2,1)} %get-tuple-element.257, s32[]{:T(128)} %get-tuple-element.247), kind=kOutput, calls=%fused_computation.22.clone.1 | convolution fusion | flops 264241152 | bytes 2949632 | tf_op jit(solution)/shard_map/while/body/eval_jaxpr/kdc,cbr->kdbr/dot_general | solution.py:29
  154.0 2.8 %fusion.59 = f32[3,128,21,64]{1,3,2,0:T(8,128)} fusion(bf16[256,21,64]{0,2,1:T(8,128)(2,1)S(1)} %get-tuple-element.258, bf16[9,3,128,256]{3,2,1,0:T(8,128)(2,1)} %get-tuple-element.257, s32[]{:T(128)} %get-tuple-element.247), kind=kOutput, calls=%fused_computation.22.clone.1 | convolution fusion | flops 264241152 | bytes 2949632 | tf_op jit(solution)/shard_map/while/body/eval_jaxpr/kdc,cbr->kdbr/dot_general | solution.py:29
  161.4 2.8 %fusion.59 = f32[3,128,21,64]{1,3,2,0:T(8,128)} fusion(bf16[256,21,64]{0,2,1:T(8,128)(2,1)S(1)} %get-tuple-element.258, bf16[9,3,128,256]{3,2,1,0:T(8,128)(2,1)} %get-tuple-element.257, s32[]{:T(128)} %get-tuple-element.247), kind=kOutput, calls=%fused_computation.22.clone.1 | convolution fusion | flops 264241152 | bytes 2949632 | tf_op jit(solution)/shard_map/while/body/eval_jaxpr/kdc,cbr->kdbr/dot_general | solution.py:29
  168.9 2.8 %fusion.59 = f32[3,128,21,64]{1,3,2,0:T(8,128)} fusion(bf16[256,21,64]{0,2,1:T(8,128)(2,1)S(1)} %get-tuple-element.258, bf16[9,3,128,256]{3,2,1,0:T(8,128)(2,1)} %get-tuple-element.257, s32[]{:T(128)} %get-tuple-element.247), kind=kOutput, calls=%fused_computation.22.clone.1 | convolution fusion | flops 264241152 | bytes 2949632 | tf_op jit(solution)/shard_map/while/body/eval_jaxpr/kdc,cbr->kdbr/dot_general | solution.py:29
  176.3 2.8 %fusion.59 = f32[3,128,21,64]{1,3,2,0:T(8,128)} fusion(bf16[256,21,64]{0,2,1:T(8,128)(2,1)S(1)} %get-tuple-element.258, bf16[9,3,128,256]{3,2,1,0:T(8,128)(2,1)} %get-tuple-element.257, s32[]{:T(128)} %get-tuple-element.247), kind=kOutput, calls=%fused_computation.22.clone.1 | convolution fusion | flops 264241152 | bytes 2949632 | tf_op jit(solution)/shard_map/while/body/eval_jaxpr/kdc,cbr->kdbr/dot_general | solution.py:29
  183.7 2.8 %fusion.59 = f32[3,128,21,64]{1,3,2,0:T(8,128)} fusion(bf16[256,21,64]{0,2,1:T(8,128)(2,1)S(1)} %get-tuple-element.258, bf16[9,3,128,256]{3,2,1,0:T(8,128)(2,1)} %get-tuple-element.257, s32[]{:T(128)} %get-tuple-element.247), kind=kOutput, calls=%fused_computation.22.clone.1 | convolution fusion | flops 264241152 | bytes 2949632 | tf_op jit(solution)/shard_map/while/body/eval_jaxpr/kdc,cbr->kdbr/dot_general | solution.py:29
  193.4 10.8 %reduce-scatter.4.cloned.1.call-done = bf16[128,128]{1,0:T(8,128)(2,1)} async-done(((bf16[256,128]{1,0:T(8,128)(2,1)}), bf16[128,128]{1,0:T(8,128)(2,1)}) %reduce-scatter.4.cloned.1.call-update) | async-done | bytes 32784
  205.4 10.3 %all_to_all.14 = bf16[128,8,32]{0,2,1:T(8,128)(2,1)S(1)} all-to-all(bf16[128,8,32]{0,2,1:T(8,128)(2,1)S(1)} %bitcast.114), channel_id=1, replica_groups=mesh['groups'=2,'brick'=4,'chan'=2,'sub'=2] {'brick','sub'}, dimensions={1} | all-to-all | bytes 131072 | tf_op jit(solution)/shard_map/all_to_all | solution.py:112
  (165 shorter events, 88.2 us)
Async XLA Ops:
  6.5 185.8 %copy-start = (bf16[8,128,256]{2,1,0:T(8,128)(2,1)S(1)}, bf16[8,128,256]{2,1,0:T(8,128)(2,1)}, u32[]{:S(2)}) copy-start(bf16[8,128,256]{2,1,0:T(8,128)(2,1)} %param.25) | copy-start | bytes 1572868
  6.5 10.3 %copy-start.4 = (s32[2,2]{1,0:T(2,128)S(1)}, s32[2,2]{1,0:T(2,128)}, u32[]{:S(2)}) copy-start(s32[2,2]{1,0:T(2,128)} %param.21) | copy-start | bytes 52
  6.5 32.1 %copy-start.3 = (s32[16,1]{0,1:T(1,128)S(1)}, s32[16,1]{0,1:T(1,128)}, u32[]{:S(2)}) copy-start(s32[16,1]{0,1:T(1,128)} %param.22) | copy-start | bytes 196
  6.5 32.1 %copy-start.2 = (s32[16,27]{1,0:T(8,128)S(1)}, s32[16,27]{1,0:T(8,128)}, u32[]{:S(2)}) copy-start(s32[16,27]{1,0:T(8,128)} %param.20) | copy-start | bytes 5188
  10.5 16.1 %all-to-all-start = ((bf16[8,64,256]{2,1,0:T(8,128)(2,1)}), bf16[8,64,256]{2,1,0:T(8,128)(2,1)S(1)}, u32[]{:S(2)}, u32[]{:S(2)}) async-start(bf16[8,64,256]{2,1,0:T(8,128)(2,1)} %bitcast.4), calls=%async_computation | async-start | bytes 524288 | tf_op jit(solution)/shard_map/all_to_all | solution.py:60
  16.8 187.4 %reduce-scatter.4.cloned.1.call-start = ((), (), s32[]{:S(2)}) async-start(), calls=%async_computation.3 | async-start | bytes 98304
  34.9 6.1 %copy-start.1 = (bf16[8,128,256]{2,1,0:T(8,128)(2,1)}, bf16[8,128,256]{2,1,0:T(8,128)(2,1)S(1)}, u32[]{:S(2)}) copy-start(bf16[8,128,256]{2,1,0:T(8,128)(2,1)S(1)} %all_gather.6) | copy-start | bytes 1572868
  35.4 3.5 %collective-permute-start = (bf16[2,64,256]{2,1,0:T(8,128)(2,1)S(1)}, bf16[2,64,256]{2,1,0:T(8,128)(2,1)S(1)}, u32[]{:S(2)}, u32[]{:S(2)}) collective-permute-start(bf16[2,64,256]{2,1,0:T(8,128)(2,1)S(1)} %gather_fusion.3), channel_id=1, source_target_pairs={{0,1},{1,4},{4,5},{5,8},{8,9},{9,12},{12,13},{2,3},{3,6},{6,7},{7,... | collective-permute-start | bytes 196616 | tf_op jit(solution)/shard_map/ppermute | solution.py:12
  37.3 3.5 %collective-permute-start.1 = (bf16[2,64,256]{2,1,0:T(8,128)(2,1)S(1)}, bf16[2,64,256]{2,1,0:T(8,128)(2,1)S(1)}, u32[]{:S(2)}, u32[]{:S(2)}) collective-permute-start(bf16[2,64,256]{2,1,0:T(8,128)(2,1)S(1)} %gather_fusion.4), channel_id=1, source_target_pairs={{1,0},{4,1},{5,4},{8,5},{9,8},{12,9},{13,12},{3,2},{6,3},{7,6},{10... | collective-permute-start | bytes 196616 | tf_op jit(solution)/shard_map/ppermute | solution.py:12
  41.0 65.6 %copy-start.5 = (f32[128]{0:T(128)S(1)}, f32[128]{0:T(128)}, u32[]{:S(2)}) copy-start(f32[128]{0:T(128)} %param.27) | copy-start | bytes 1540
  41.0 65.6 %copy-start.6 = (f32[128]{0:T(128)S(1)}, f32[128]{0:T(128)}, u32[]{:S(2)}) copy-start(f32[128]{0:T(128)} %param.26) | copy-start | bytes 1540
  116.9 5.1 %collective-permute-start.2 = (bf16[256,2,64]{0,2,1:T(8,128)(2,1)S(1)}, bf16[256,2,64]{0,2,1:T(8,128)(2,1)S(1)}, u32[]{:S(2)}, u32[]{:S(2)}) collective-permute-start(bf16[256,2,64]{0,2,1:T(8,128)(2,1)S(1)} %bitcast.113), channel_id=1, source_target_pairs={{0,1},{1,4},{4,5},{5,8},{8,9},{9,12},{12,13},{2,3},{3,6},{6,7},{7,... | collective-permute-start | bytes 196616 | tf_op jit(solution)/shard_map/ppermute | solution.py:12
  120.5 4.7 %collective-permute-start.3 = (bf16[256,2,64]{0,2,1:T(8,128)(2,1)S(1)}, bf16[256,2,64]{0,2,1:T(8,128)(2,1)S(1)}, u32[]{:S(2)}, u32[]{:S(2)}) collective-permute-start(bf16[256,2,64]{0,2,1:T(8,128)(2,1)S(1)} %bitcast.112), channel_id=1, source_target_pairs={{1,0},{4,1},{5,4},{8,5},{9,8},{12,9},{13,12},{3,2},{6,3},{7,6},{10... | collective-permute-start | bytes 196616 | tf_op jit(solution)/shard_map/ppermute | solution.py:12
  125.3 65.8 %copy-start.7 = (f32[128]{0:T(128)S(1)}, f32[128]{0:T(128)}, u32[]{:S(2)}) copy-start(f32[128]{0:T(128)} %param.29) | copy-start | bytes 1540
  125.4 65.8 %copy-start.8 = (f32[128]{0:T(128)S(1)}, f32[128]{0:T(128)}, u32[]{:S(2)}) copy-start(f32[128]{0:T(128)} %param.28) | copy-start | bytes 1540
  191.1 14.0 %copy-start.9 = (f32[128]{0:T(128)S(1)}, f32[128]{0:T(128)}, u32[]{:S(2)}) copy-start(f32[128]{0:T(128)} %param.31) | copy-start | bytes 1540
  191.1 14.0 %copy-start.10 = (f32[128]{0:T(128)S(1)}, f32[128]{0:T(128)}, u32[]{:S(2)}) copy-start(f32[128]{0:T(128)} %param.30) | copy-start | bytes 1540
Sparse Core Ops, SparseCore 0:
  193.5 10.6 reduce-scatter.3
where the time goes:
time: 226 us; the launch traced here: 223 us
  local copies, waits for them, and re-layouts  52 us (23%)
  matrix products  51 us (23%)
  other arithmetic  40.1 us (18%)
  blocking collectives  26.7 us (12%)
  waiting for transfers between devices  25.6 us (11%)
  starting transfers between devices  13.9 us (6%)
  between operations  13.6 us (6%)
    dot_general x18, matrix products, one_group(): jnp.einsum(pattern, group_weight, extended, preferred_element_type=jnp.fl...  50.5 us
    gather x18, local copies, waits for them, and re-layouts, one_group(): return (running + jnp.sum(product[offsets, :, indices], axis=0), None)  42.5 us
    add x18, other arithmetic, one_group(): return (running + jnp.sum(product[offsets, :, indices], axis=0), None)  32.2 us
    unnamed x2, waiting for transfers between devices  10.8 us
    all_to_all x1, blocking collectives, body(): lax.all_to_all(outgoing, ('brick', 'sub'), split_axis=1, concat_axis=2, t...  10.3 us
    all_to_all x1, waiting for transfers between devices, body(): lax.all_to_all(ordered, ('brick', 'sub'), split_axis=0, concat_axis=0, ti...  9.65 us
    all_gather x1, blocking collectives, body(): owner_rows = lax.all_gather(regrouped, 'chan', axis=1, tiled=True)  8.34 us
    all_gather x1, blocking collectives, body(): all_channels = lax.all_gather(hidden_blocks, 'chan', axis=0, tiled=True)  8 us
  transfers between devices with their start and end apart: 6, of which 4 were waited for; matrix products, arithmetic and copies ran while one was open for 0% of the time, Pallas kernels for 0%

commit v1 on v0

v1 whole, which is shorter than its diff:
```python
import functools

import jax
import jax.numpy as jnp
from jax import lax
from jax.experimental import pallas as pl
from jax.experimental.pallas import tpu as pltpu
from jax.sharding import PartitionSpec as P

BLK = 64
CHILDREN = 8
F32 = jnp.float32
BF16 = jnp.bfloat16
NT = (((1,), (1,)), ((), ()))
NN = (((1,), (0,)), ((), ()))
VMEM = pl.BlockSpec(memory_space=pltpu.VMEM)
SMEM = pl.BlockSpec(memory_space=pltpu.SMEM)
LIMIT = pltpu.CompilerParams(vmem_limit_bytes=40 * 2**20)


def from_behind(block, axis, distance):
    devices = range(lax.axis_size(axis))
    route = [(i - distance, i) for i in devices if i - distance in devices]
    return lax.ppermute(block, axis, route)


def from_ahead(block, axis, distance):
    n = lax.axis_size(axis)
    return lax.ppermute(block, axis, [((i + distance) % n, i) for i in range(n)])


def to_ahead(block, axis, distance):
    n = lax.axis_size(axis)
    return lax.ppermute(block, axis, [(i, (i + distance) % n) for i in range(n)])


def sort_kernel(bricks, subs, place, order, rows, *outs):
    total = rows.shape[0]
    per = total // (bricks * subs)
    taken = lax.broadcasted_iota(jnp.int32, (total, total), 0) == order[...]
    onehot = jnp.where(taken, 1.0, 0.0).astype(BF16)
    picked = lax.dot_general(
        onehot, rows[...], (((0,), (0,)), ((), ())), preferred_element_type=F32
    ).astype(BF16)
    for b in range(bricks):
        for s in range(subs):
            away = lax.rem(s - place[1] + subs, subs)
            ahead = lax.rem(b - place[0] + bricks, bricks)
            start = (b * subs + s) * per
            for js in range(subs):

                @pl.when(away == js)
                def _(js=js, ahead=ahead, start=start):
                    outs[js][ahead] = picked[start : start + per]


def sort_rows(scan_order, features, place, bricks, subs):
    per = features.shape[0] // (bricks * subs)
    piece = jax.ShapeDtypeStruct((bricks, per, features.shape[1]), BF16)
    return pl.pallas_call(
        functools.partial(sort_kernel, bricks, subs),
        out_shape=[piece] * subs,
        in_specs=[SMEM, VMEM, VMEM],
        out_specs=[VMEM] * subs,
        compiler_params=LIMIT,
        name="sort_rows",
    )(place, scan_order, features)


def assemble_kernel(bricks, subs, chans, place, halo, *refs):
    parts, (rows, up, down) = refs[:-3], refs[-3:]
    split = BLK // parts[0].shape[1]
    for j in range(chans):
        chan = lax.rem(place[2] + j, chans)
        for jb in range(bricks):
            source = lax.rem(place[0] - jb + bricks, bricks)
            for js in range(subs):
                sub = lax.rem(place[1] + js, subs)
                rows[(source * subs + sub) * chans + chan] = parts[j * bricks + jb][js]
    for j in range(halo.shape[1]):
        up[pl.ds(j * split, split)] = rows[pl.ds(halo[0, j] * split, split)]
        down[pl.ds(j * split, split)] = rows[pl.ds(halo[1, j] * split, split)]


def assemble(parts, halo, place, bricks, subs, chans):
    per, channels = parts[0].shape[1:]
    pieces = bricks * subs * chans
    split = BLK // per
    sent = halo.shape[1] * split
    return pl.pallas_call(
        functools.partial(assemble_kernel, bricks, subs, chans),
        out_shape=[
            jax.ShapeDtypeStruct((count, per, channels), BF16) for count in (pieces, sent, sent)
        ],
        in_specs=[SMEM, SMEM] + [VMEM] * len(parts),
        out_specs=[VMEM] * 3,
        compiler_params=LIMIT,
        name="assemble",
    )(place, halo, *parts)


def block_sums(table, extended, weight, total):
    count = table.shape[0]
    group = min(count, 16)
    channels = extended.shape[2]

    def one_group(g, carry):
        first = g * group
        running = None
        for k in range(weight.shape[0]):
            picked = jnp.concatenate(
                [extended[table[first + n, k]] for n in range(group)], axis=0
            )
            product = lax.dot_general(picked, weight[k], NT, preferred_element_type=F32)
            running = product if running is None else running + product
        total[pl.ds(first, group)] = running.reshape(group, BLK, weight.shape[1])
        return carry

    if count == group:
        one_group(0, 0)
    else:
        lax.fori_loop(0, count // group, one_group, 0)


def first_kernel(table, halo, rows, lower, upper, weight, gain, bias, hidden, up, down, extended, total):
    count, reach = table.shape[0], halo.shape[1]
    extended[pl.ds(0, count)] = rows[...]
    extended[pl.ds(count, reach)] = lower[...]
    extended[pl.ds(count + reach, reach)] = upper[...]
    extended[count + 2 * reach] = jnp.zeros(extended.shape[1:], BF16)
    block_sums(table, extended, weight, total)
    value = total[...] * gain[...][None] + bias[...][None]
    hidden[...] = jnp.maximum(value, 0.0).astype(BF16)
    for j in range(reach):
        up[j] = hidden[halo[0, j]]
        down[j] = hidden[halo[1, j]]


def first_conv(table, halo, rows, lower, upper, weight, gain, bias):
    count, reach = table.shape[0], halo.shape[1]
    width, channels = weight.shape[1:]
    return pl.pallas_call(
        first_kernel,
        out_shape=[
            jax.ShapeDtypeStruct((n, BLK, width), BF16) for n in (count, reach, reach)
        ],
        in_specs=[SMEM, SMEM] + [VMEM] * 6,
        out_specs=[VMEM] * 3,
        scratch_shapes=[
            pltpu.VMEM((count + 2 * reach + 1, BLK, channels), BF16),
            pltpu.VMEM((count, BLK, width), F32),
        ],
        compiler_params=LIMIT,
        name="first_conv",
    )(table, halo, rows, lower, upper, weight, gain, bias)


def second_kernel(chans, table, place, rows, weight, down_weight, gain, bias, *refs):
    parts, (out, extended, total) = refs[:-3], refs[-3:]
    count = table.shape[0]
    width, channels = weight.shape[1:]
    reach = parts[1].shape[0]
    for j in range(chans):
        own, lower, upper = parts[3 * j : 3 * j + 3]
        for c in range(chans):

            @pl.when(lax.rem(place[2] + j, chans) == c)
            def _(own=own, lower=lower, upper=upper, c=c):
                lanes = slice(c * width, (c + 1) * width)
                extended[0:count, :, lanes] = own[...]
                extended[count : count + reach, :, lanes] = lower[...]
                extended[count + reach : count + 2 * reach, :, lanes] = upper[...]

    extended[count + 2 * reach] = jnp.zeros(extended.shape[1:], BF16)
    block_sums(table, extended, weight, total)
    for c in range(chans):

        @pl.when(place[2] == c)
        def _(c=c):
            total[...] = (
                total[...] * gain[...][None]
                + bias[...][None]
                + rows[:, :, c * width : (c + 1) * width].astype(F32)
            )

    refined = jnp.maximum(total[...], 0.0).reshape(count, CHILDREN, BLK // CHILDREN, width)
    cells = count * (BLK // CHILDREN)
    coarse = None
    for o in range(CHILDREN):
        child = refined[:, o].reshape(cells, width).astype(BF16)
        product = lax.dot_general(child, down_weight[o], NN, preferred_element_type=F32)
        coarse = product if coarse is None else coarse + product
    for c in range(chans):
        out[lax.rem(c - place[2] + chans, chans)] = coarse[
            :, c * width : (c + 1) * width
        ].astype(BF16)


def second_conv(table, place, rows, weight, down_weight, gain, bias, parts, chans):
    count = table.shape[0]
    reach = parts[1].shape[0]
    width, channels = weight.shape[1:]
    cells = count * (BLK // CHILDREN)
    return pl.pallas_call(
        functools.partial(second_kernel, chans),
        out_shape=jax.ShapeDtypeStruct((chans, cells, width), BF16),
        in_specs=[SMEM, SMEM] + [VMEM] * (5 + len(parts)),
        out_specs=VMEM,
        scratch_shapes=[
            pltpu.VMEM((count + 2 * reach + 1, BLK, channels), BF16),
            pltpu.VMEM((count, BLK, width), F32),
        ],
        compiler_params=LIMIT,
        name="second_conv",
    )(table, place, rows, weight, down_weight, gain, bias, *parts)


def tile_kernel(bricks, subs, capacity, route, place, gain, bias, *refs):
    owners = bricks * subs
    parts, outs, (slots, seen) = refs[: -subs - 2], refs[-subs - 2 : -2], refs[-2:]
    count = route.shape[0]
    coarse = parts[0][...].astype(F32)
    for part in parts[1:]:
        coarse = coarse + part[...].astype(F32)
    tiles = jnp.maximum(coarse * gain[...] + bias[...], 0.0)
    tiles = tiles.reshape(count, BLK // CHILDREN, tiles.shape[1])
    slots[...] = jnp.zeros(slots.shape, F32)
    for owner in range(owners):
        seen[owner] = 0
    for n in range(count):
        owner = route[n, 0]
        slot = seen[owner]
        seen[owner] = slot + 1
        slots[owner * capacity + slot] = tiles[n]
    for b in range(bricks):
        for s in range(subs):
            ahead = lax.rem(b - place[0] + bricks, bricks)
            away = lax.rem(s - place[1] + subs, subs)
            mine = slots[pl.ds((b * subs + s) * capacity, capacity)]
            mine = mine.reshape(capacity * (BLK // CHILDREN), mine.shape[2]).astype(BF16)
            for js in range(subs):

                @pl.when(away == js)
                def _(js=js, ahead=ahead, mine=mine):
                    outs[js][ahead] = mine


def coarse_tiles(route, place, gain, bias, parts, bricks, subs, capacity):
    width = gain.shape[1]
    per = BLK // CHILDREN
    piece = jax.ShapeDtypeStruct((bricks, capacity * per, width), BF16)
    return pl.pallas_call(
        functools.partial(tile_kernel, bricks, subs, capacity),
        out_shape=[piece] * subs,
        in_specs=[SMEM, SMEM] + [VMEM] * (2 + len(parts)),
        out_specs=[VMEM] * subs,
        scratch_shapes=[
            pltpu.VMEM((bricks * subs * capacity, per, width), F32),
            pltpu.SMEM((bricks * subs,), jnp.int32),
        ],
        compiler_params=LIMIT,
        name="coarse_tiles",
    )(route, place, gain, bias, *parts)


def arrive_kernel(bricks, subs, place, *refs):
    parts, out, held = refs[:-2], refs[-2], refs[-1]
    for jb in range(bricks):
        source = lax.rem(place[0] - jb + bricks, bricks)
        for js in range(subs):
            sub = lax.rem(place[1] + js, subs)
            held[source * subs + sub] = parts[jb][js].astype(F32)
    every = held[...].reshape(bricks * subs * held.shape[1], held.shape[2])
    out[0] = every.T.astype(BF16)


def arrived_tiles(place, parts, bricks, subs):
    slots, width = parts[0].shape[1:]
    return pl.pallas_call(
        functools.partial(arrive_kernel, bricks, subs),
        out_shape=jax.ShapeDtypeStruct((1, width, bricks * subs * slots), BF16),
        in_specs=[SMEM] + [VMEM] * len(parts),
        out_specs=VMEM,
        scratch_shapes=[pltpu.VMEM((bricks * subs, slots, width), F32)],
        compiler_params=LIMIT,
        name="arrived_tiles",
    )(place, *parts)


def to_owners(pieces, bricks, subs):
    by_sub = [pieces[0]]
    for js in range(1, subs):
        by_sub.append(to_ahead(pieces[subs - js], "sub", subs - js))
    stacked = [jnp.stack([piece[jb] for piece in by_sub]) for jb in range(bricks)]
    return [stacked[0]] + [to_ahead(stacked[jb], "brick", jb) for jb in range(1, bricks)]


def body(
    features,
    scan_order,
    kernel_map,
    halo_send,
    down_route,
    conv1_weight,
    conv2_weight,
    down_weight,
    gain_first,
    bias_first,
    gain_second,
    bias_second,
    gain_down,
    bias_down,
):
    bricks, subs, chans = (lax.axis_size(axis) for axis in ("brick", "sub", "chan"))
    owners = bricks * subs
    count, reach = kernel_map.shape[0], halo_send.shape[1]
    channels = features.shape[1]
    place = jnp.stack([lax.axis_index(axis) for axis in ("brick", "sub", "chan")])
    place = place.astype(jnp.int32)

    pieces = sort_rows(scan_order, features, place, bricks, subs)
    arrived = to_owners(pieces, bricks, subs)
    parts = arrived + [
        from_ahead(piece, "chan", j) for j in range(1, chans) for piece in arrived
    ]
    rows, up, down = assemble(parts, halo_send, place, bricks, subs, chans)
    lower = from_behind(up, ("brick", "sub"), 1)
    upper = from_behind(down, ("brick", "sub"), -1)
    rows = rows.reshape(count, BLK, channels)
    hidden, up, down = first_conv(
        kernel_map,
        halo_send,
        rows,
        lower.reshape(reach, BLK, channels),
        upper.reshape(reach, BLK, channels),
        conv1_weight,
        gain_first[None],
        bias_first[None],
    )
    lower = from_behind(up, ("brick", "sub"), 1)
    upper = from_behind(down, ("brick", "sub"), -1)
    parts = [hidden, lower, upper]
    for j in range(1, chans):
        parts += [from_ahead(part, "chan", j) for part in (hidden, lower, upper)]
    partial = second_conv(
        kernel_map,
        place,
        rows,
        conv2_weight,
        down_weight,
        gain_second[None],
        bias_second[None],
        parts,
        chans,
    )
    parts = [partial[0]] + [to_ahead(partial[j], "chan", j) for j in range(1, chans)]
    capacity = max(2, 2 * count // owners)
    pieces = coarse_tiles(
        down_route, place, gain_down[None], bias_down[None], parts, bricks, subs, capacity
    )
    return arrived_tiles(place, to_owners(pieces, bricks, subs), bricks, subs)


def solution(mesh):
    placed = (
        P(("groups", "brick", "chan", "sub"), None),
        P(("groups", "brick", "chan", "sub"), None),
        P(("groups", "brick", "sub"), None),
        P(("groups", "brick", "sub"), None),
        P(("groups", "brick", "sub"), None),
        P(None, "chan", None),
        P(None, "chan", None),
        P(None, "chan", None),
        P("chan"),
        P("chan"),
        P("chan"),
        P("chan"),
        P("chan"),
        P("chan"),
    )
    return jax.shard_map(
        body,
        mesh=mesh,
        in_specs=placed,
        out_specs=P(("groups", "brick", "sub"), "chan", None),
        check_vma=False,
    )
```

time: 226 us -> 69 us (0.31); the launches traced: 223 us -> 68.8 us
  matrix products: 51 us -> 0 us
  local copies, waits for them, and re-layouts: 52 us -> 3.9 us
  other arithmetic: 40.1 us -> 0.12 us
  blocking collectives: 26.7 us -> 0 us
  starting transfers between devices: 13.9 us -> 29.9 us
  Pallas kernels: 0 us -> 13.5 us
  between operations: 13.6 us -> 0.22 us
  waiting for transfers between devices: 25.6 us -> 21.1 us
    dot_general x20 -> x0, matrix products: 51 us -> none  [the longest x18 50.5 us: one_group(): jnp.einsum(pattern, group_weight, extended, preferred_element_type=jnp.fl...]
    gather x23 -> x0, local copies, waits for them, and re-layouts: 47.9 us -> none  [the longest x18 42.5 us: one_group(): return (running + jnp.sum(product[offsets, :, indices], axis=0), None)]
    add x19 -> x0, other arithmetic: 32.2 us -> none  [the longest x18 32.2 us: one_group(): return (running + jnp.sum(product[offsets, :, indices], axis=0), None)]
    ppermute x0 -> x16, starting transfers between devices: none -> 21.8 us  [the longest x9 14 us: to_ahead(): lax.ppermute(block, axis, [(i, (i + distance) % n) for i in range(n)])]
    ppermute x0 -> x16, waiting for transfers between devices: none -> 18.5 us  [the longest x9 11.9 us: to_ahead(): lax.ppermute(block, axis, [(i, (i + distance) % n) for i in range(n)])]
    all_gather x2 -> x0, blocking collectives: 16.3 us -> none  [the longest x1 8.34 us: body(): owner_rows = lax.all_gather(regrouped, 'chan', axis=1, tiled=True)]
    pallas_call x0 -> x6, Pallas kernels: none -> 13.5 us  [the longest x1 5.24 us: second_conv(): pl.pallas_call(functools.partial(second_kernel, chans), out_shape=jax.Sha...]
    unnamed x2 -> x0, waiting for transfers between devices: 10.8 us -> none
  transfers between devices with their start and end apart: 6 -> 20, of which waited for: 4 -> 13; matrix products, arithmetic and copies ran while one was open for 0% -> 0% of each run, Pallas kernels for 0% -> 0%
where the time goes in v1:
time: 69 us; the launch traced here: 68.8 us
  starting transfers between devices  29.9 us (43%)
  waiting for transfers between devices  21.1 us (31%)
  Pallas kernels  13.5 us (20%)
  local copies, waits for them, and re-layouts  3.9 us (6%)
    ppermute x9, starting transfers between devices, to_ahead(): lax.ppermute(block, axis, [(i, (i + distance) % n) for i in range(n)])  14 us
    ppermute x9, waiting for transfers between devices, to_ahead(): lax.ppermute(block, axis, [(i, (i + distance) % n) for i in range(n)])  11.9 us
    ppermute x4, starting transfers between devices, from_behind(): return lax.ppermute(block, axis, route)  8.08 us
    ppermute x7, starting transfers between devices, from_ahead(): lax.ppermute(block, axis, [((i + distance) % n, i) for i in range(n)])  7.75 us
    ppermute x7, waiting for transfers between devices, from_ahead(): lax.ppermute(block, axis, [((i + distance) % n, i) for i in range(n)])  6.67 us
    pallas_call x1, Pallas kernels, second_conv(): pl.pallas_call(functools.partial(second_kernel, chans), out_shape=jax.Sha...  5.24 us
    pallas_call x1, Pallas kernels, first_conv(): pl.pallas_call(first_kernel, out_shape=[jax.ShapeDtypeStruct((n, BLK, wid...  4.51 us
    unnamed x29, local copies, waits for them, and re-layouts  3.87 us
  transfers between devices with their start and end apart: 20, of which 13 were waited for; matrix products, arithmetic and copies ran while one was open for 0% of the time, Pallas kernels for 0%

profile of v1, /device:TPU:0, one launch (start us, length us, event | category | flops | bytes accessed | tf_op | source)
XLA Modules:
  0.0 68.8 jit_solution(5741808581840045993)
XLA Ops:
  0.1 1.1 %copy-done.3 = bf16[512,256]{1,0:T(8,128)(2,1)S(1)} copy-done((bf16[512,256]{1,0:T(8,128)(2,1)S(1)}, bf16[512,256]{1,0:T(8,128)(2,1)}, u32[]{:S(2)}) %copy-start.3) | copy-done | bytes 262168
  1.8 1.0 %sort_rows.1 = (bf16[4,64,256]{2,1,0:T(8,128)(2,1)S(1)}, bf16[4,64,256]{2,1,0:T(8,128)(2,1)S(1)}) custom-call(s32[3]{0:T(128)S(1)} %pad_add_fusion.place, s32[1,512]{1,0:T(1,128)S(1)} %copy-done.6, bf16[512,256]{1,0:T(8,128)(2,1)S(1)} %copy-done.3), custom_call_target="tpu_custom_call" | custom-call | tf_op jit(solution)/shard_map/sort_rows/pallas_call | solution.py:60
  3.4 1.0 %collective-permute-done = bf16[4,64,256]{2,1,0:T(8,128)(2,1)S(1)} collective-permute-done((bf16[4,64,256]{2,1,0:T(8,128)(2,1)S(1)}, bf16[4,64,256]{2,1,0:T(8,128)(2,1)S(1)}, u32[]{:S(2)}, u32[]{:S(2)}) %collective-permute-start) | collective-permute-done | bytes 131104 | tf_op jit(solution)/shard_map/ppermute | solution.py:34
  4.4 5.0 %collective-permute-start.3 = (bf16[2,64,256]{2,1,0:T(8,128)(2,1)S(1)}, bf16[2,64,256]{2,1,0:T(8,128)(2,1)S(1)}, u32[]{:S(2)}, u32[]{:S(2)}) collective-permute-start(bf16[2,64,256]{2,1,0:T(8,128)(2,1)S(1)} %pad_maximum_fusion.3), channel_id=1, source_target_pairs={{0,12},{4,0},{8,4},{12,8},{1,13},{5,1},{9,5},{13,9},{2,14},{6,2},{... | collective-permute-start | bytes 196616 | tf_op jit(solution)/shard_map/ppermute | solution.py:34
  9.5 1.0 %collective-permute-start.1 = (bf16[2,64,256]{2,1,0:T(8,128)(2,1)S(1)}, bf16[2,64,256]{2,1,0:T(8,128)(2,1)S(1)}, u32[]{:S(2)}, u32[]{:S(2)}) collective-permute-start(bf16[2,64,256]{2,1,0:T(8,128)(2,1)S(1)} %pad_maximum_fusion.1), channel_id=1, source_target_pairs={{0,4},{4,8},{8,12},{12,0},{1,5},{5,9},{9,13},{13,1},{2,6},{6,10},{... | collective-permute-start | bytes 196616 | tf_op jit(solution)/shard_map/ppermute | solution.py:34
  10.6 1.5 %collective-permute-start.4 = (bf16[2,64,256]{2,1,0:T(8,128)(2,1)S(1)}, bf16[2,64,256]{2,1,0:T(8,128)(2,1)S(1)}, u32[]{:S(2)}, u32[]{:S(2)}) collective-permute-start(bf16[2,64,256]{2,1,0:T(8,128)(2,1)S(1)} %pad_maximum_fusion.refs_0_), channel_id=1, source_target_pairs={{2,0},{0,2},{3,1},{1,3},{6,4},{4,6},{7,5},{5,7},{10,8},{8,10},{11,... | collective-permute-start | bytes 196616 | tf_op jit(solution)/shard_map/ppermute | solution.py:29
  12.1 1.3 %collective-permute-start.7 = (bf16[2,64,256]{2,1,0:T(8,128)(2,1)S(1)}, bf16[2,64,256]{2,1,0:T(8,128)(2,1)S(1)}, u32[]{:S(2)}, u32[]{:S(2)}) collective-permute-start(bf16[2,64,256]{2,1,0:T(8,128)(2,1)S(1)} %collective-permute-done.3.refs_3_), channel_id=1, source_target_pairs={{2,0},{0,2},{3,1},{1,3},{6,4},{4,6},{7,5},{5,7},{10,8},{8,10},{11,... | collective-permute-start | bytes 196616 | tf_op jit(solution)/shard_map/ppermute | solution.py:29
  13.4 2.8 %collective-permute-done.2.refs_2_ = bf16[2,64,256]{2,1,0:T(8,128)(2,1)S(1)} collective-permute-done((bf16[2,64,256]{2,1,0:T(8,128)(2,1)S(1)}, bf16[2,64,256]{2,1,0:T(8,128)(2,1)S(1)}, u32[]{:S(2)}, u32[]{:S(2)}) %collective-permute-start.2) | collective-permute-done | bytes 65568 | tf_op jit(solution)/shard_map/ppermute | solution.py:34
  16.2 1.5 %collective-permute-start.6 = (bf16[2,64,256]{2,1,0:T(8,128)(2,1)S(1)}, bf16[2,64,256]{2,1,0:T(8,128)(2,1)S(1)}, u32[]{:S(2)}, u32[]{:S(2)}) collective-permute-start(bf16[2,64,256]{2,1,0:T(8,128)(2,1)S(1)} %collective-permute-done.2.refs_2_), channel_id=1, source_target_pairs={{2,0},{0,2},{3,1},{1,3},{6,4},{4,6},{7,5},{5,7},{10,8},{8,10},{11,... | collective-permute-start | bytes 196616 | tf_op jit(solution)/shard_map/ppermute | solution.py:29
  18.2 2.8 %collective-permute-done.6.refs_6_ = bf16[2,64,256]{2,1,0:T(8,128)(2,1)S(1)} collective-permute-done((bf16[2,64,256]{2,1,0:T(8,128)(2,1)S(1)}, bf16[2,64,256]{2,1,0:T(8,128)(2,1)S(1)}, u32[]{:S(2)}, u32[]{:S(2)}) %collective-permute-start.6) | collective-permute-done | bytes 65568 | tf_op jit(solution)/shard_map/ppermute | solution.py:29
  21.1 0.9 %collective-permute-done.5.refs_5_ = bf16[2,64,256]{2,1,0:T(8,128)(2,1)S(1)} collective-permute-done((bf16[2,64,256]{2,1,0:T(8,128)(2,1)S(1)}, bf16[2,64,256]{2,1,0:T(8,128)(2,1)S(1)}, u32[]{:S(2)}, u32[]{:S(2)}) %collective-permute-start.5) | collective-permute-done | bytes 65568 | tf_op jit(solution)/shard_map/ppermute | solution.py:29
  23.3 1.3 %collective-permute-start.8 = (bf16[2,64,256]{2,1,0:T(8,128)(2,1)S(1)}, bf16[2,64,256]{2,1,0:T(8,128)(2,1)S(1)}, u32[]{:S(2)}, u32[]{:S(2)}) collective-permute-start(bf16[2,64,256]{2,1,0:T(8,128)(2,1)S(1)} %get-tuple-element.18), channel_id=1, source_target_pairs={{0,1},{1,4},{4,5},{5,8},{8,9},{9,12},{12,13},{2,3},{3,6},{6,7},{7,... | collective-permute-start | bytes 196616 | tf_op jit(solution)/shard_map/ppermute | solution.py:24
  24.6 1.3 %collective-permute-start.9 = (bf16[2,64,256]{2,1,0:T(8,128)(2,1)S(1)}, bf16[2,64,256]{2,1,0:T(8,128)(2,1)S(1)}, u32[]{:S(2)}, u32[]{:S(2)}) collective-permute-start(bf16[2,64,256]{2,1,0:T(8,128)(2,1)S(1)} %get-tuple-element.19), channel_id=1, source_target_pairs={{1,0},{4,1},{5,4},{8,5},{9,8},{12,9},{13,12},{3,2},{6,3},{7,6},{10... | collective-permute-start | bytes 196616 | tf_op jit(solution)/shard_map/ppermute | solution.py:24
  25.9 1.8 %collective-permute-done.9.upper = bf16[2,64,256]{2,1,0:T(8,128)(2,1)S(1)} collective-permute-done((bf16[2,64,256]{2,1,0:T(8,128)(2,1)S(1)}, bf16[2,64,256]{2,1,0:T(8,128)(2,1)S(1)}, u32[]{:S(2)}, u32[]{:S(2)}) %collective-permute-start.9) | collective-permute-done | bytes 65568 | tf_op jit(solution)/shard_map/ppermute | solution.py:24
  29.0 4.5 %first_conv.1 = (bf16[16,64,128]{2,1,0:T(8,128)(2,1)S(1)}, bf16[2,64,128]{2,1,0:T(8,128)(2,1)S(1)}, bf16[2,64,128]{2,1,0:T(8,128)(2,1)S(1)}) custom-call(s32[16,27]{1,0:T(8,128)S(1)} %copy-done.4, s32[2,2]{1,0:T(2,128)S(1)} %copy-done.5, bf16[16,64,256]{2,1,0:T(8,128)(2,1)S(1)} %get-tuple-element.17.rows, ...), custom_call_target="tpu_custom_call" | custom-call | tf_op jit(solution)/shard_map/first_conv/pallas_call | solution.py:142
  33.6 0.9 %collective-permute-start.12 = (bf16[16,64,128]{2,1,0:T(8,128)(2,1)S(1)}, bf16[16,64,128]{2,1,0:T(8,128)(2,1)S(1)}, u32[]{:S(2)}, u32[]{:S(2)}) collective-permute-start(bf16[16,64,128]{2,1,0:T(8,128)(2,1)S(1)} %get-tuple-element.20.refs_0_), channel_id=1, source_target_pairs={{2,0},{0,2},{3,1},{1,3},{6,4},{4,6},{7,5},{5,7},{10,8},{8,10},{11,... | collective-permute-start | bytes 786440 | tf_op jit(solution)/shard_map/ppermute | solution.py:29
  34.4 4.2 %collective-permute-start.10 = (bf16[2,64,128]{2,1,0:T(8,128)(2,1)S(1)}, bf16[2,64,128]{2,1,0:T(8,128)(2,1)S(1)}, u32[]{:S(2)}, u32[]{:S(2)}) collective-permute-start(bf16[2,64,128]{2,1,0:T(8,128)(2,1)S(1)} %get-tuple-element.21), channel_id=1, source_target_pairs={{0,1},{1,4},{4,5},{5,8},{8,9},{9,12},{12,13},{2,3},{3,6},{6,7},{7,... | collective-permute-start | bytes 98312 | tf_op jit(solution)/shard_map/ppermute | solution.py:24
  38.6 1.3 %collective-permute-start.11 = (bf16[2,64,128]{2,1,0:T(8,128)(2,1)S(1)}, bf16[2,64,128]{2,1,0:T(8,128)(2,1)S(1)}, u32[]{:S(2)}, u32[]{:S(2)}) collective-permute-start(bf16[2,64,128]{2,1,0:T(8,128)(2,1)S(1)} %get-tuple-element.22), channel_id=1, source_target_pairs={{1,0},{4,1},{5,4},{8,5},{9,8},{12,9},{13,12},{3,2},{6,3},{7,6},{10... | collective-permute-start | bytes 98312 | tf_op jit(solution)/shard_map/ppermute | solution.py:24
  39.9 1.0 %collective-permute-start.13 = (bf16[2,64,128]{2,1,0:T(8,128)(2,1)S(1)}, bf16[2,64,128]{2,1,0:T(8,128)(2,1)S(1)}, u32[]{:S(2)}, u32[]{:S(2)}) collective-permute-start(bf16[2,64,128]{2,1,0:T(8,128)(2,1)S(1)} %collective-permute-done.10.refs_1_), channel_id=1, source_target_pairs={{2,0},{0,2},{3,1},{1,3},{6,4},{4,6},{7,5},{5,7},{10,8},{8,10},{11,... | collective-permute-start | bytes 98312 | tf_op jit(solution)/shard_map/ppermute | solution.py:29
  41.7 1.0 %collective-permute-start.14 = (bf16[2,64,128]{2,1,0:T(8,128)(2,1)S(1)}, bf16[2,64,128]{2,1,0:T(8,128)(2,1)S(1)}, u32[]{:S(2)}, u32[]{:S(2)}) collective-permute-start(bf16[2,64,128]{2,1,0:T(8,128)(2,1)S(1)} %collective-permute-done.11.refs_2_), channel_id=1, source_target_pairs={{2,0},{0,2},{3,1},{1,3},{6,4},{4,6},{7,5},{5,7},{10,8},{8,10},{11,... | collective-permute-start | bytes 98312 | tf_op jit(solution)/shard_map/ppermute | solution.py:29
  42.7 1.4 %collective-permute-done.13.refs_4_ = bf16[2,64,128]{2,1,0:T(8,128)(2,1)S(1)} collective-permute-done((bf16[2,64,128]{2,1,0:T(8,128)(2,1)S(1)}, bf16[2,64,128]{2,1,0:T(8,128)(2,1)S(1)}, u32[]{:S(2)}, u32[]{:S(2)}) %collective-permute-start.13) | collective-permute-done | bytes 32800 | tf_op jit(solution)/shard_map/ppermute | solution.py:29
  44.1 1.5 %collective-permute-done.14.refs_5_ = bf16[2,64,128]{2,1,0:T(8,128)(2,1)S(1)} collective-permute-done((bf16[2,64,128]{2,1,0:T(8,128)(2,1)S(1)}, bf16[2,64,128]{2,1,0:T(8,128)(2,1)S(1)}, u32[]{:S(2)}, u32[]{:S(2)}) %collective-permute-start.14) | collective-permute-done | bytes 32800 | tf_op jit(solution)/shard_map/ppermute | solution.py:29
  45.7 5.2 %second_conv.1 = bf16[2,128,128]{2,1,0:T(8,128)(2,1)S(1)} custom-call(s32[16,27]{1,0:T(8,128)S(1)} %copy-done.4, s32[3]{0:T(128)S(1)} %pad_add_fusion.place, bf16[16,64,256]{2,1,0:T(8,128)(2,1)S(1)} %get-tuple-element.17.rows, bf16[27,128,256]{2,1,0:T(8,128)(2,1)S(1)} %copy-done.1, bf16[8,128,256]{2,1,0:T(8,128)(2,1)S(1)} %copy-done.2, ...), custom_call_target="tpu_custom_call" | custom-call | tf_op jit(solution)/shard_map/second_conv/pallas_call | solution.py:204
  51.0 1.0 %collective-permute-start.15 = (bf16[128,128]{1,0:T(8,128)(2,1)S(1)}, bf16[128,128]{1,0:T(8,128)(2,1)S(1)}, u32[]{:S(2)}, u32[]{:S(2)}) collective-permute-start(bf16[128,128]{1,0:T(8,128)(2,1)S(1)} %get-tuple-element.33), channel_id=1, source_target_pairs={{0,2},{2,0},{1,3},{3,1},{4,6},{6,4},{5,7},{7,5},{8,10},{10,8},{9,1... | collective-permute-start | bytes 98312 | tf_op jit(solution)/shard_map/ppermute | solution.py:34
  52.1 2.8 %collective-permute-done.15.refs_1_ = bf16[128,128]{1,0:T(8,128)(2,1)S(1)} collective-permute-done((bf16[128,128]{1,0:T(8,128)(2,1)S(1)}, bf16[128,128]{1,0:T(8,128)(2,1)S(1)}, u32[]{:S(2)}, u32[]{:S(2)}) %collective-permute-start.15) | collective-permute-done | bytes 32800 | tf_op jit(solution)/shard_map/ppermute | solution.py:34
  55.0 0.9 %coarse_tiles.1 = (bf16[4,32,128]{2,1,0:T(8,128)(2,1)S(1)}, bf16[4,32,128]{2,1,0:T(8,128)(2,1)S(1)}) custom-call(s32[16,1]{1,0:T(8,128)S(1)} %copy.15.route, s32[3]{0:T(128)S(1)} %pad_add_fusion.place, f32[1,128]{1,0:T(1,128)S(1)} %bitcast.15, f32[1,128]{1,0:T(1,128)S(1)} %bitcast.16, bf16[128,128]{1,0:T(8,128)(2,1)S(1)} %get-tuple-element.34.refs_0_, ...), custom_call_target="tpu_custom_call" | custom-call | tf_op jit(solution)/shard_map/coarse_tiles/pallas_call | solution.py:252
  56.3 0.9 %collective-permute-done.16 = bf16[4,32,128]{2,1,0:T(8,128)(2,1)S(1)} collective-permute-done((bf16[4,32,128]{2,1,0:T(8,128)(2,1)S(1)}, bf16[4,32,128]{2,1,0:T(8,128)(2,1)S(1)}, u32[]{:S(2)}, u32[]{:S(2)}) %collective-permute-start.16) | collective-permute-done | bytes 32800 | tf_op jit(solution)/shard_map/ppermute | solution.py:34
  57.1 4.7 %collective-permute-start.19 = (bf16[2,32,128]{2,1,0:T(8,128)(2,1)S(1)}, bf16[2,32,128]{2,1,0:T(8,128)(2,1)S(1)}, u32[]{:S(2)}, u32[]{:S(2)}) collective-permute-start(bf16[2,32,128]{2,1,0:T(8,128)(2,1)S(1)} %pad_maximum_fusion.7), channel_id=1, source_target_pairs={{0,12},{4,0},{8,4},{12,8},{1,13},{5,1},{9,5},{13,9},{2,14},{6,2},{... | collective-permute-start | bytes 49160 | tf_op jit(solution)/shard_map/ppermute | solution.py:34
  61.9 1.2 %collective-permute-start.17 = (bf16[2,32,128]{2,1,0:T(8,128)(2,1)S(1)}, bf16[2,32,128]{2,1,0:T(8,128)(2,1)S(1)}, u32[]{:S(2)}, u32[]{:S(2)}) collective-permute-start(bf16[2,32,128]{2,1,0:T(8,128)(2,1)S(1)} %pad_maximum_fusion.5), channel_id=1, source_target_pairs={{0,4},{4,8},{8,12},{12,0},{1,5},{5,9},{9,13},{13,1},{2,6},{6,10},{... | collective-permute-start | bytes 49160 | tf_op jit(solution)/shard_map/ppermute | solution.py:34
  63.3 3.2 %collective-permute-done.18.refs_2_ = bf16[2,32,128]{2,1,0:T(8,128)(2,1)S(1)} collective-permute-done((bf16[2,32,128]{2,1,0:T(8,128)(2,1)S(1)}, bf16[2,32,128]{2,1,0:T(8,128)(2,1)S(1)}, u32[]{:S(2)}, u32[]{:S(2)}) %collective-permute-start.18) | collective-permute-done | bytes 16416 | tf_op jit(solution)/shard_map/ppermute | solution.py:34
  66.5 1.0 %collective-permute-done.17.refs_1_ = bf16[2,32,128]{2,1,0:T(8,128)(2,1)S(1)} collective-permute-done((bf16[2,32,128]{2,1,0:T(8,128)(2,1)S(1)}, bf16[2,32,128]{2,1,0:T(8,128)(2,1)S(1)}, u32[]{:S(2)}, u32[]{:S(2)}) %collective-permute-start.17) | collective-permute-done | bytes 16416 | tf_op jit(solution)/shard_map/ppermute | solution.py:34
  67.5 1.3 %arrived_tiles.1 = bf16[1,128,256]{2,1,0:T(8,128)(2,1)} custom-call(s32[3]{0:T(128)S(1)} %pad_add_fusion.place, bf16[2,32,128]{2,1,0:T(8,128)(2,1)S(1)} %pad_maximum_fusion.4.refs_0_, bf16[2,32,128]{2,1,0:T(8,128)(2,1)S(1)} %collective-permute-done.17.refs_1_, bf16[2,32,128]{2,1,0:T(8,128)(2,1)S(1)} %collective-permute-done.18.refs_2_, ...), custom_call_target="tpu_custom_call" | custom-call | tf_op jit(solution)/shard_map/arrived_tiles/pallas_call | solution.py:279
  (57 shorter events, 6.1 us)
Async XLA Ops:
  0.0 27.7 %copy-start = (bf16[27,128,256]{2,1,0:T(8,128)(2,1)S(1)}, bf16[27,128,256]{2,1,0:T(8,128)(2,1)}, u32[]{:S(2)}) copy-start(bf16[27,128,256]{2,1,0:T(8,128)(2,1)} %weight.2) | copy-start | bytes 5308420
  0.1 1.1 %copy-start.3 = (bf16[512,256]{1,0:T(8,128)(2,1)S(1)}, bf16[512,256]{1,0:T(8,128)(2,1)}, u32[]{:S(2)}) copy-start(bf16[512,256]{1,0:T(8,128)(2,1)} %rows.1) | copy-start | bytes 786436
  1.1 0.7 copy-start.6
  1.8 25.9 %copy-start.4 = (s32[16,27]{1,0:T(8,128)S(1)}, s32[16,27]{1,0:T(8,128)}, u32[]{:S(2)}) copy-start(s32[16,27]{1,0:T(8,128)} %table.3) | copy-start | bytes 5188
  2.9 1.5 %collective-permute-start = (bf16[4,64,256]{2,1,0:T(8,128)(2,1)S(1)}, bf16[4,64,256]{2,1,0:T(8,128)(2,1)S(1)}, u32[]{:S(2)}, u32[]{:S(2)}) collective-permute-start(bf16[4,64,256]{2,1,0:T(8,128)(2,1)S(1)} %get-tuple-element.16), channel_id=1, source_target_pairs={{0,1},{1,0},{2,3},{3,2},{4,5},{5,4},{6,7},{7,6},{8,9},{9,8},{10,11... | collective-permute-start | bytes 393224 | tf_op jit(solution)/shard_map/ppermute | solution.py:34
  4.4 41.3 %copy-start.1 = (bf16[27,128,256]{2,1,0:T(8,128)(2,1)S(1)}, bf16[27,128,256]{2,1,0:T(8,128)(2,1)}, u32[]{:S(2)}) copy-start(bf16[27,128,256]{2,1,0:T(8,128)(2,1)} %weight.3) | copy-start | bytes 5308420
  4.4 41.3 %copy-start.2 = (bf16[8,128,256]{2,1,0:T(8,128)(2,1)S(1)}, bf16[8,128,256]{2,1,0:T(8,128)(2,1)}, u32[]{:S(2)}) copy-start(bf16[8,128,256]{2,1,0:T(8,128)(2,1)} %down_weight.1) | copy-start | bytes 1572868
  4.4 7.7 %collective-permute-start.3 = (bf16[2,64,256]{2,1,0:T(8,128)(2,1)S(1)}, bf16[2,64,256]{2,1,0:T(8,128)(2,1)S(1)}, u32[]{:S(2)}, u32[]{:S(2)}) collective-permute-start(bf16[2,64,256]{2,1,0:T(8,128)(2,1)S(1)} %pad_maximum_fusion.3), channel_id=1, source_target_pairs={{0,12},{4,0},{8,4},{12,8},{1,13},{5,1},{9,5},{13,9},{2,14},{6,2},{... | collective-permute-start | bytes 196616 | tf_op jit(solution)/shard_map/ppermute | solution.py:34
  9.4 6.8 %collective-permute-start.2 = (bf16[2,64,256]{2,1,0:T(8,128)(2,1)S(1)}, bf16[2,64,256]{2,1,0:T(8,128)(2,1)S(1)}, u32[]{:S(2)}, u32[]{:S(2)}) collective-permute-start(bf16[2,64,256]{2,1,0:T(8,128)(2,1)S(1)} %pad_maximum_fusion.2), channel_id=1, source_target_pairs={{0,8},{4,12},{8,0},{12,4},{1,9},{5,13},{9,1},{13,5},{2,10},{6,14},... | collective-permute-start | bytes 196616 | tf_op jit(solution)/shard_map/ppermute | solution.py:34
  9.5 8.2 %collective-permute-start.1 = (bf16[2,64,256]{2,1,0:T(8,128)(2,1)S(1)}, bf16[2,64,256]{2,1,0:T(8,128)(2,1)S(1)}, u32[]{:S(2)}, u32[]{:S(2)}) collective-permute-start(bf16[2,64,256]{2,1,0:T(8,128)(2,1)S(1)} %pad_maximum_fusion.1), channel_id=1, source_target_pairs={{0,4},{4,8},{8,12},{12,0},{1,5},{5,9},{9,13},{13,1},{2,6},{6,10},{... | collective-permute-start | bytes 196616 | tf_op jit(solution)/shard_map/ppermute | solution.py:34
  10.6 7.7 %collective-permute-start.4 = (bf16[2,64,256]{2,1,0:T(8,128)(2,1)S(1)}, bf16[2,64,256]{2,1,0:T(8,128)(2,1)S(1)}, u32[]{:S(2)}, u32[]{:S(2)}) collective-permute-start(bf16[2,64,256]{2,1,0:T(8,128)(2,1)S(1)} %pad_maximum_fusion.refs_0_), channel_id=1, source_target_pairs={{2,0},{0,2},{3,1},{1,3},{6,4},{4,6},{7,5},{5,7},{10,8},{8,10},{11,... | collective-permute-start | bytes 196616 | tf_op jit(solution)/shard_map/ppermute | solution.py:29
  12.1 6.1 %collective-permute-start.7 = (bf16[2,64,256]{2,1,0:T(8,128)(2,1)S(1)}, bf16[2,64,256]{2,1,0:T(8,128)(2,1)S(1)}, u32[]{:S(2)}, u32[]{:S(2)}) collective-permute-start(bf16[2,64,256]{2,1,0:T(8,128)(2,1)S(1)} %collective-permute-done.3.refs_3_), channel_id=1, source_target_pairs={{2,0},{0,2},{3,1},{1,3},{6,4},{4,6},{7,5},{5,7},{10,8},{8,10},{11,... | collective-permute-start | bytes 196616 | tf_op jit(solution)/shard_map/ppermute | solution.py:29
  16.2 4.9 %collective-permute-start.6 = (bf16[2,64,256]{2,1,0:T(8,128)(2,1)S(1)}, bf16[2,64,256]{2,1,0:T(8,128)(2,1)S(1)}, u32[]{:S(2)}, u32[]{:S(2)}) collective-permute-start(bf16[2,64,256]{2,1,0:T(8,128)(2,1)S(1)} %collective-permute-done.2.refs_2_), channel_id=1, source_target_pairs={{2,0},{0,2},{3,1},{1,3},{6,4},{4,6},{7,5},{5,7},{10,8},{8,10},{11,... | collective-permute-start | bytes 196616 | tf_op jit(solution)/shard_map/ppermute | solution.py:29
  17.7 4.3 %collective-permute-start.5 = (bf16[2,64,256]{2,1,0:T(8,128)(2,1)S(1)}, bf16[2,64,256]{2,1,0:T(8,128)(2,1)S(1)}, u32[]{:S(2)}, u32[]{:S(2)}) collective-permute-start(bf16[2,64,256]{2,1,0:T(8,128)(2,1)S(1)} %collective-permute-done.1.refs_1_), channel_id=1, source_target_pairs={{2,0},{0,2},{3,1},{1,3},{6,4},{4,6},{7,5},{5,7},{10,8},{8,10},{11,... | collective-permute-start | bytes 196616 | tf_op jit(solution)/shard_map/ppermute | solution.py:29
  22.0 0.7 copy-start.5
  22.6 23.0 %copy-start.7 = (f32[128]{0:T(128)S(1)}, f32[128]{0:T(128)}, u32[]{:S(2)}) copy-start(f32[128]{0:T(128)} %param.24) | copy-start | bytes 1540
  22.6 23.0 %copy-start.8 = (f32[128]{0:T(128)S(1)}, f32[128]{0:T(128)}, u32[]{:S(2)}) copy-start(f32[128]{0:T(128)} %param.25) | copy-start | bytes 1540
  23.3 2.6 %collective-permute-start.8 = (bf16[2,64,256]{2,1,0:T(8,128)(2,1)S(1)}, bf16[2,64,256]{2,1,0:T(8,128)(2,1)S(1)}, u32[]{:S(2)}, u32[]{:S(2)}) collective-permute-start(bf16[2,64,256]{2,1,0:T(8,128)(2,1)S(1)} %get-tuple-element.18), channel_id=1, source_target_pairs={{0,1},{1,4},{4,5},{5,8},{8,9},{9,12},{12,13},{2,3},{3,6},{6,7},{7,... | collective-permute-start | bytes 196616 | tf_op jit(solution)/shard_map/ppermute | solution.py:24
  24.6 3.1 %collective-permute-start.9 = (bf16[2,64,256]{2,1,0:T(8,128)(2,1)S(1)}, bf16[2,64,256]{2,1,0:T(8,128)(2,1)S(1)}, u32[]{:S(2)}, u32[]{:S(2)}) collective-permute-start(bf16[2,64,256]{2,1,0:T(8,128)(2,1)S(1)} %get-tuple-element.19), channel_id=1, source_target_pairs={{1,0},{4,1},{5,4},{8,5},{9,8},{12,9},{13,12},{3,2},{6,3},{7,6},{10... | collective-permute-start | bytes 196616 | tf_op jit(solution)/shard_map/ppermute | solution.py:24
  33.6 12.1 %collective-permute-start.12 = (bf16[16,64,128]{2,1,0:T(8,128)(2,1)S(1)}, bf16[16,64,128]{2,1,0:T(8,128)(2,1)S(1)}, u32[]{:S(2)}, u32[]{:S(2)}) collective-permute-start(bf16[16,64,128]{2,1,0:T(8,128)(2,1)S(1)} %get-tuple-element.20.refs_0_), channel_id=1, source_target_pairs={{2,0},{0,2},{3,1},{1,3},{6,4},{4,6},{7,5},{5,7},{10,8},{8,10},{11,... | collective-permute-start | bytes 786440 | tf_op jit(solution)/shard_map/ppermute | solution.py:29
  34.4 5.5 %collective-permute-start.10 = (bf16[2,64,128]{2,1,0:T(8,128)(2,1)S(1)}, bf16[2,64,128]{2,1,0:T(8,128)(2,1)S(1)}, u32[]{:S(2)}, u32[]{:S(2)}) collective-permute-start(bf16[2,64,128]{2,1,0:T(8,128)(2,1)S(1)} %get-tuple-element.21), channel_id=1, source_target_pairs={{0,1},{1,4},{4,5},{5,8},{8,9},{9,12},{12,13},{2,3},{3,6},{6,7},{7,... | collective-permute-start | bytes 98312 | tf_op jit(solution)/shard_map/ppermute | solution.py:24
  38.6 3.1 %collective-permute-start.11 = (bf16[2,64,128]{2,1,0:T(8,128)(2,1)S(1)}, bf16[2,64,128]{2,1,0:T(8,128)(2,1)S(1)}, u32[]{:S(2)}, u32[]{:S(2)}) collective-permute-start(bf16[2,64,128]{2,1,0:T(8,128)(2,1)S(1)} %get-tuple-element.22), channel_id=1, source_target_pairs={{1,0},{4,1},{5,4},{8,5},{9,8},{12,9},{13,12},{3,2},{6,3},{7,6},{10... | collective-permute-start | bytes 98312 | tf_op jit(solution)/shard_map/ppermute | solution.py:24
  39.9 4.2 %collective-permute-start.13 = (bf16[2,64,128]{2,1,0:T(8,128)(2,1)S(1)}, bf16[2,64,128]{2,1,0:T(8,128)(2,1)S(1)}, u32[]{:S(2)}, u32[]{:S(2)}) collective-permute-start(bf16[2,64,128]{2,1,0:T(8,128)(2,1)S(1)} %collective-permute-done.10.refs_1_), channel_id=1, source_target_pairs={{2,0},{0,2},{3,1},{1,3},{6,4},{4,6},{7,5},{5,7},{10,8},{8,10},{11,... | collective-permute-start | bytes 98312 | tf_op jit(solution)/shard_map/ppermute | solution.py:29
  41.7 3.9 %collective-permute-start.14 = (bf16[2,64,128]{2,1,0:T(8,128)(2,1)S(1)}, bf16[2,64,128]{2,1,0:T(8,128)(2,1)S(1)}, u32[]{:S(2)}, u32[]{:S(2)}) collective-permute-start(bf16[2,64,128]{2,1,0:T(8,128)(2,1)S(1)} %collective-permute-done.11.refs_2_), channel_id=1, source_target_pairs={{2,0},{0,2},{3,1},{1,3},{6,4},{4,6},{7,5},{5,7},{10,8},{8,10},{11,... | collective-permute-start | bytes 98312 | tf_op jit(solution)/shard_map/ppermute | solution.py:29
  45.7 6.3 %copy-start.13 = (s32[16,1]{0,1:T(1,128)S(1)}, s32[16,1]{0,1:T(1,128)}, u32[]{:S(2)}) copy-start(s32[16,1]{0,1:T(1,128)} %param.18) | copy-start | bytes 196
  45.7 9.3 %copy-start.9 = (f32[128]{0:T(128)S(1)}, f32[128]{0:T(128)}, u32[]{:S(2)}) copy-start(f32[128]{0:T(128)} %param.26) | copy-start | bytes 1540
  45.7 9.3 %copy-start.10 = (f32[128]{0:T(128)S(1)}, f32[128]{0:T(128)}, u32[]{:S(2)}) copy-start(f32[128]{0:T(128)} %param.27) | copy-start | bytes 1540
  51.0 4.0 %collective-permute-start.15 = (bf16[128,128]{1,0:T(8,128)(2,1)S(1)}, bf16[128,128]{1,0:T(8,128)(2,1)S(1)}, u32[]{:S(2)}, u32[]{:S(2)}) collective-permute-start(bf16[128,128]{1,0:T(8,128)(2,1)S(1)} %get-tuple-element.33), channel_id=1, source_target_pairs={{0,2},{2,0},{1,3},{3,1},{4,6},{6,4},{5,7},{7,5},{8,10},{10,8},{9,1... | collective-permute-start | bytes 98312 | tf_op jit(solution)/shard_map/ppermute | solution.py:34
  55.8 1.3 %collective-permute-start.16 = (bf16[4,32,128]{2,1,0:T(8,128)(2,1)S(1)}, bf16[4,32,128]{2,1,0:T(8,128)(2,1)S(1)}, u32[]{:S(2)}, u32[]{:S(2)}) collective-permute-start(bf16[4,32,128]{2,1,0:T(8,128)(2,1)S(1)} %get-tuple-element.24), channel_id=1, source_target_pairs={{0,1},{1,0},{2,3},{3,2},{4,5},{5,4},{6,7},{7,6},{8,9},{9,8},{10,11... | collective-permute-start | bytes 98312 | tf_op jit(solution)/shard_map/ppermute | solution.py:34
  57.1 6.2 %collective-permute-start.19 = (bf16[2,32,128]{2,1,0:T(8,128)(2,1)S(1)}, bf16[2,32,128]{2,1,0:T(8,128)(2,1)S(1)}, u32[]{:S(2)}, u32[]{:S(2)}) collective-permute-start(bf16[2,32,128]{2,1,0:T(8,128)(2,1)S(1)} %pad_maximum_fusion.7), channel_id=1, source_target_pairs={{0,12},{4,0},{8,4},{12,8},{1,13},{5,1},{9,5},{13,9},{2,14},{6,2},{... | collective-permute-start | bytes 49160 | tf_op jit(solution)/shard_map/ppermute | solution.py:34
  61.9 4.6 %collective-permute-start.18 = (bf16[2,32,128]{2,1,0:T(8,128)(2,1)S(1)}, bf16[2,32,128]{2,1,0:T(8,128)(2,1)S(1)}, u32[]{:S(2)}, u32[]{:S(2)}) collective-permute-start(bf16[2,32,128]{2,1,0:T(8,128)(2,1)S(1)} %pad_maximum_fusion.6), channel_id=1, source_target_pairs={{0,8},{4,12},{8,0},{12,4},{1,9},{5,13},{9,1},{13,5},{2,10},{6,14},... | collective-permute-start | bytes 49160 | tf_op jit(solution)/shard_map/ppermute | solution.py:34
  61.9 5.6 %collective-permute-start.17 = (bf16[2,32,128]{2,1,0:T(8,128)(2,1)S(1)}, bf16[2,32,128]{2,1,0:T(8,128)(2,1)S(1)}, u32[]{:S(2)}, u32[]{:S(2)}) collective-permute-start(bf16[2,32,128]{2,1,0:T(8,128)(2,1)S(1)} %pad_maximum_fusion.5), channel_id=1, source_target_pairs={{0,4},{4,8},{8,12},{12,0},{1,5},{5,9},{9,13},{13,1},{2,6},{6,10},{... | collective-permute-start | bytes 49160 | tf_op jit(solution)/shard_map/ppermute | solution.py:34
  (2 other events, 1.3 us)

commit v2 on v1

v2 whole, which is shorter than its diff:
```python
import functools

import jax
import jax.numpy as jnp
from jax import lax
from jax.experimental import pallas as pl
from jax.experimental.pallas import tpu as pltpu
from jax.sharding import PartitionSpec as P

BLK = 64
CHILDREN = 8
CELLS = BLK // CHILDREN
ABSENT = -1e30
F32 = jnp.float32
BF16 = jnp.bfloat16
NT = (((1,), (1,)), ((), ()))
NN = (((1,), (0,)), ((), ()))
VMEM = pl.BlockSpec(memory_space=pltpu.VMEM)
SMEM = pl.BlockSpec(memory_space=pltpu.SMEM)
LIMIT = pltpu.CompilerParams(vmem_limit_bytes=40 * 2**20)


class Place:
    def __init__(self, ints, start, reach=0):
        self.ints, self.start, self.reach = ints, start, reach
        self.brick, self.sub, self.chan, self.parity = (ints[0, start + i] for i in range(4))

    def halo(self, direction, j):
        return self.ints[0, self.start + 4 + direction * self.reach + j]

    def route(self, n):
        return self.ints[0, self.start + 4 + 2 * self.reach + n]


def owner_pairs(block, parity, distance=0):
    bricks, subs, chans = (lax.axis_size(axis) for axis in ("brick", "sub", "chan"))

    def device(owner, chan):
        return (owner // subs * chans + chan % chans) * subs + owner % subs

    pairs = [(o, o + 1) for o in range(parity, bricks * subs - 1, 2)]
    pairs += [(b, a) for a, b in pairs]
    route = [(device(a, c + distance), device(b, c)) for a, b in pairs for c in range(chans)]
    return lax.ppermute(block, ("brick", "chan", "sub"), route)


def from_ahead(block, axis, distance):
    n = lax.axis_size(axis)
    return lax.ppermute(block, axis, [((i + distance) % n, i) for i in range(n)])


def to_ahead(block, axis, distance):
    n = lax.axis_size(axis)
    return lax.ppermute(block, axis, [(i, (i + distance) % n) for i in range(n)])


def sort_kernel(bricks, subs, ints, order, rows, *outs):
    total = rows.shape[0]
    place = Place(ints, total)
    per = total // (bricks * subs)
    taken = lax.broadcasted_iota(jnp.int32, (total, total), 0) == order[:, :total]
    onehot = jnp.where(taken, 1.0, 0.0).astype(BF16)
    picked = lax.dot_general(
        onehot, rows[...], (((0,), (0,)), ((), ())), preferred_element_type=F32
    ).astype(BF16)
    for b in range(bricks):
        for s in range(subs):
            away = lax.rem(s - place.sub + subs, subs)
            ahead = lax.rem(b - place.brick + bricks, bricks)
            start = (b * subs + s) * per
            for js in range(subs):

                @pl.when(away == js)
                def _(js=js, ahead=ahead, start=start):
                    outs[js][ahead] = picked[start : start + per]


def sort_rows(ints, features, bricks, subs):
    per = features.shape[0] // (bricks * subs)
    piece = jax.ShapeDtypeStruct((bricks, per, features.shape[1]), BF16)
    return pl.pallas_call(
        functools.partial(sort_kernel, bricks, subs),
        out_shape=[piece] * subs,
        in_specs=[SMEM, VMEM, VMEM],
        out_specs=[VMEM] * subs,
        compiler_params=LIMIT,
        name="sort_rows",
    )(ints, ints, features)


def assemble_kernel(start, reach, bricks, subs, chans, ints, *refs):
    parts, (rows, even, odd) = refs[:-3], refs[-3:]
    place = Place(ints, start, reach)
    split = BLK // parts[0].shape[1]
    for j in range(chans):
        chan = lax.rem(place.chan + j, chans)
        for jb in range(bricks):
            source = lax.rem(place.brick - jb + bricks, bricks)
            for js in range(subs):
                sub = lax.rem(place.sub + js, subs)
                rows[(source * subs + sub) * chans + chan] = parts[j * bricks + jb][js]
    for j in range(reach):
        even[pl.ds(j * split, split)] = rows[pl.ds(place.halo(place.parity, j) * split, split)]
        odd[pl.ds(j * split, split)] = rows[pl.ds(place.halo(1 - place.parity, j) * split, split)]


def assemble(ints, parts, start, reach, bricks, subs, chans):
    per, channels = parts[0].shape[1:]
    pieces = bricks * subs * chans
    split = BLK // per
    sent = reach * split
    return pl.pallas_call(
        functools.partial(assemble_kernel, start, reach, bricks, subs, chans),
        out_shape=[
            jax.ShapeDtypeStruct((count, per, channels), BF16) for count in (pieces, sent, sent)
        ],
        in_specs=[SMEM] + [VMEM] * len(parts),
        out_specs=[VMEM] * 3,
        compiler_params=LIMIT,
        name="assemble",
    )(ints, *parts)


def block_sums(table, blocks, weight, total):
    count = table.shape[0]
    group = min(count, 16)
    lanes = blocks.shape[2]
    offsets = weight.shape[2] // lanes

    def one_group(g, carry):
        first = g * group
        running = None
        for w in range(weight.shape[0]):
            inside = range(w * offsets, min((w + 1) * offsets, table.shape[1]))
            picked = jnp.concatenate(
                [
                    jnp.concatenate(
                        [blocks[jnp.minimum(table[first + n, k], count)] for k in inside], axis=1
                    )
                    for n in range(group)
                ],
                axis=0,
            )
            product = lax.dot_general(
                picked, weight[w, :, : len(inside) * lanes], NT, preferred_element_type=F32
            )
            running = product if running is None else running + product
        total[pl.ds(first, group)] = running.reshape(group, BLK, weight.shape[1])
        return carry

    if count == group:
        one_group(0, 0)
    else:
        lax.fori_loop(0, count // group, one_group, 0)


def rim_blocks(place, even, odd, lanes, rim):
    reach = even.shape[0]
    rim[pl.ds(reach * (1 - place.parity), reach), :, lanes] = even[...]
    rim[pl.ds(reach * place.parity, reach), :, lanes] = odd[...]


def rim_sums(count, table, rim, weight, products, total):
    blocks, offsets = rim.shape[0], table.shape[1]
    width, channels = weight.shape[1:]
    together = max(1, channels // width)
    rows = rim[...].reshape(blocks * BLK, channels)
    for k in range(0, offsets, together):
        size = min(together, offsets - k)
        product = lax.dot_general(
            rows,
            weight[k : k + size].reshape(size * width, channels),
            NT,
            preferred_element_type=F32,
        )
        for i in range(size):
            products[k + i, 0:blocks] = product[:, i * width : (i + 1) * width].reshape(
                blocks, BLK, width
            )
    products[:, blocks : blocks + 1] = jnp.zeros((offsets, 1, BLK, width), F32)

    def one_block(n, carry):
        running = total[n]
        for k in range(offsets):
            index = table[n, k]
            running = running + products[k, jnp.where(index < count, blocks, index - count)]
        total[n] = running
        return carry

    lax.fori_loop(0, count, one_block, 0, unroll=min(count, 16))


def cost(blocks, weight):
    offsets, width, channels = weight.shape
    return pl.CostEstimate(
        flops=4 * blocks * BLK * offsets * width * channels, bytes_accessed=0, transcendentals=0
    )


def own_first_kernel(table, rows, weight, total, blocks):
    count = rows.shape[0]
    blocks[0:count] = rows[...]
    blocks[count] = jnp.zeros(blocks.shape[1:], BF16)
    block_sums(table, blocks, weight, total)


def own_first(table, rows, weight):
    count, channels = rows.shape[0], rows.shape[2]
    return pl.pallas_call(
        own_first_kernel,
        out_shape=jax.ShapeDtypeStruct((count, BLK, weight.shape[1]), F32),
        in_specs=[SMEM, VMEM, VMEM],
        out_specs=VMEM,
        scratch_shapes=[pltpu.VMEM((count + 1, BLK, channels), BF16)],
        compiler_params=LIMIT,
        cost_estimate=cost(count, weight),
        name="own_first",
    )(table, rows, weight)


def rim_first_kernel(start, ints, table, vectors, own, even, odd, weight, hidden, even_out, odd_out, rim, products, total):
    count, reach = table.shape[0], even.shape[0]
    place = Place(ints, start, reach)
    rim_blocks(place, even, odd, slice(None), rim)
    total[...] = own[...]
    rim_sums(count, table, rim, weight, products, total)
    value = total[...] * vectors[0:1][None] + vectors[1:2][None]
    hidden[...] = jnp.maximum(value, 0.0).astype(BF16)
    for j in range(reach):
        even_out[j] = hidden[place.halo(place.parity, j)]
        odd_out[j] = hidden[place.halo(1 - place.parity, j)]


def rim_scratch(count, reach, weight):
    offsets, width, channels = weight.shape
    return [
        pltpu.VMEM((2 * reach, BLK, channels), BF16),
        pltpu.VMEM((offsets, 2 * reach + 1, BLK, width), F32),
        pltpu.VMEM((count, BLK, width), F32),
    ]


def rim_first(ints, table, vectors, own, even, odd, weight, start):
    count, reach, width = table.shape[0], even.shape[0], weight.shape[1]
    return pl.pallas_call(
        functools.partial(rim_first_kernel, start),
        out_shape=[
            jax.ShapeDtypeStruct((n, BLK, width), BF16) for n in (count, reach, reach)
        ],
        in_specs=[SMEM, SMEM] + [VMEM] * 5,
        out_specs=[VMEM] * 3,
        scratch_shapes=rim_scratch(count, reach, weight),
        compiler_params=LIMIT,
        cost_estimate=cost(2 * reach, weight),
        name="rim_first",
    )(ints, table, vectors, own, even, odd, weight)


def own_second_kernel(start, nearest, chans, ints, table, weight, *refs):
    parts, (total, blocks, beside) = refs[:-3], refs[-3:]
    count, width = parts[0].shape[0], parts[0].shape[2]
    place = Place(ints, start)
    lanes = blocks.shape[2]
    offsets = beside.shape[2] // lanes
    for i, part in enumerate(parts):
        blocks[0:count, :, i * width : (i + 1) * width] = part[...]
        for c in range(chans):

            @pl.when(lax.rem(place.chan + nearest + i, chans) == c)
            def _(i=i, c=c):
                for k in range(weight.shape[0]):
                    at = k % offsets * lanes + i * width
                    beside[k // offsets, :, at : at + width] = weight[
                        k, :, c * width : (c + 1) * width
                    ]

    blocks[count] = jnp.zeros(blocks.shape[1:], BF16)
    block_sums(table, blocks, beside, total)


def own_second(ints, table, weight, parts, start, nearest, chans):
    count, width = parts[0].shape[0], parts[0].shape[2]
    lanes = width * len(parts)
    offsets = max(1, weight.shape[2] // lanes)
    groups = -(-weight.shape[0] // offsets)
    return pl.pallas_call(
        functools.partial(own_second_kernel, start, nearest, chans),
        out_shape=jax.ShapeDtypeStruct((count, BLK, width), F32),
        in_specs=[SMEM, SMEM] + [VMEM] * (1 + len(parts)),
        out_specs=VMEM,
        scratch_shapes=[
            pltpu.VMEM((count + 1, BLK, lanes), BF16),
            pltpu.VMEM((groups, width, lanes * offsets), BF16),
        ],
        compiler_params=LIMIT,
        cost_estimate=cost(count // 2, weight),
        name="own_second",
    )(ints, table, weight, *parts)


def rim_second_kernel(start, bricks, subs, chans, owns, ints, table, vectors, rows, weight, down_weight, *refs):
    (even, odd), refs = refs[:2], refs[2:]
    sums, refs = refs[:owns], refs[owns:]
    fars, (out, rim, products, total, slots, seen) = refs[:-6], refs[-6:]
    count, reach = table.shape[0], even.shape[0]
    width = weight.shape[1]
    place = Place(ints, start, reach)
    for j in range(chans):
        near = (even, odd) if j == 0 else (fars[j - 1].at[0:reach], fars[j - 1].at[reach:])
        for c in range(chans):

            @pl.when(lax.rem(place.chan + j, chans) == c)
            def _(near=near, c=c):
                rim_blocks(place, *near, slice(c * width, (c + 1) * width), rim)

    total[...] = sums[0][...]
    for more in sums[1:]:
        total[...] += more[...]
    rim_sums(count, table, rim, weight, products, total)
    for c in range(chans):

        @pl.when(place.chan == c)
        def _(c=c):
            total[...] = (
                total[...] * vectors[2:3][None]
                + vectors[3:4][None]
                + rows[:, :, c * width : (c + 1) * width].astype(F32)
            )

    refined = jnp.maximum(total[...], 0.0).reshape(count, CHILDREN, CELLS, width)
    coarse = None
    for o in range(CHILDREN):
        child = refined[:, o].reshape(count * CELLS, width).astype(BF16)
        product = lax.dot_general(child, down_weight[o], NN, preferred_element_type=F32)
        coarse = product if coarse is None else coarse + product
    slots[...] = jnp.full(slots.shape, ABSENT, F32)
    for owner in range(bricks * subs):
        seen[owner] = 0
    for n in range(count):
        owner = place.route(n)
        slot = seen[owner]
        seen[owner] = slot + 1
        device = owner // subs * (chans * subs) + lax.rem(owner, subs)
        for c in range(chans):
            slots[device + c * subs, pl.ds(pl.multiple_of(slot * CELLS, CELLS), CELLS)] = coarse[
                n * CELLS : (n + 1) * CELLS, c * width : (c + 1) * width
            ]
    out[...] = slots[...].astype(BF16)


def rim_second(ints, table, vectors, rows, weight, down_weight, even, odd, sums, fars, start, bricks, subs, chans, capacity):
    count, reach, width = table.shape[0], even.shape[0], weight.shape[1]
    slots = (bricks * subs * chans, capacity * CELLS, width)
    return pl.pallas_call(
        functools.partial(rim_second_kernel, start, bricks, subs, chans, len(sums)),
        out_shape=jax.ShapeDtypeStruct(slots, BF16),
        in_specs=[SMEM, SMEM] + [VMEM] * (6 + len(sums) + len(fars)),
        out_specs=VMEM,
        scratch_shapes=rim_scratch(count, reach, weight)
        + [pltpu.VMEM(slots, F32), pltpu.SMEM((bricks * subs,), jnp.int32)],
        compiler_params=LIMIT,
        cost_estimate=cost(2 * reach, weight),
        name="rim_second",
    )(ints, table, vectors, rows, weight, down_weight, even, odd, *sums, *fars)


def arrive_kernel(bricks, subs, chans, vectors, parts, out):
    held = []
    for b in range(bricks):
        for s in range(subs):
            coarse = None
            for c in range(chans):
                part = parts[(b * chans + c) * subs + s].astype(F32)
                coarse = part if coarse is None else coarse + part
            held.append(coarse)
    coarse = jnp.concatenate(held, axis=0)
    tiles = jnp.maximum(coarse * vectors[4:5] + vectors[5:6], 0.0)
    tiles = jnp.where(coarse < ABSENT / 2, 0.0, tiles)
    out[0] = tiles.T.astype(BF16)


def arrived_tiles(vectors, parts, bricks, subs, chans):
    slots, width = parts.shape[1:]
    return pl.pallas_call(
        functools.partial(arrive_kernel, bricks, subs, chans),
        out_shape=jax.ShapeDtypeStruct((1, width, bricks * subs * slots), BF16),
        in_specs=[VMEM, VMEM],
        out_specs=VMEM,
        compiler_params=LIMIT,
        name="arrived_tiles",
    )(vectors, parts)


def to_owners(pieces, bricks, subs):
    by_sub = [pieces[0]]
    for js in range(1, subs):
        by_sub.append(to_ahead(pieces[subs - js], "sub", subs - js))
    stacked = [jnp.stack([piece[jb] for piece in by_sub]) for jb in range(bricks)]
    return [stacked[0]] + [to_ahead(stacked[jb], "brick", jb) for jb in range(1, bricks)]


def body(
    features,
    scan_order,
    kernel_map,
    halo_send,
    down_route,
    conv1_weight,
    conv2_weight,
    down_weight,
    gain_first,
    bias_first,
    gain_second,
    bias_second,
    gain_down,
    bias_down,
):
    bricks, subs, chans = (lax.axis_size(axis) for axis in ("brick", "sub", "chan"))
    owners = bricks * subs
    count, reach = kernel_map.shape[0], halo_send.shape[1]
    channels = features.shape[1]
    start = features.shape[0]
    brick, sub, chan = (lax.axis_index(axis) for axis in ("brick", "sub", "chan"))
    place = jnp.stack([brick, sub, chan, lax.rem(brick * subs + sub, 2)]).astype(jnp.int32)
    ints = jnp.concatenate(
        [scan_order, place[None], halo_send.reshape(1, -1), down_route.reshape(1, -1)], axis=1
    )
    vectors = jnp.stack(
        [gain_first, bias_first, gain_second, bias_second, gain_down, bias_down]
    )
    pieces = sort_rows(ints, features, bricks, subs)
    arrived = to_owners(pieces, bricks, subs)
    parts = arrived + [
        from_ahead(piece, "chan", j) for j in range(1, chans) for piece in arrived
    ]
    rows, even, odd = assemble(ints, parts, start, reach, bricks, subs, chans)
    rows = rows.reshape(count, BLK, channels)
    even = owner_pairs(even, 0).reshape(reach, BLK, channels)
    odd = owner_pairs(odd, 1).reshape(reach, BLK, channels)
    own = own_first(kernel_map, rows, conv1_weight)
    hidden, even, odd = rim_first(
        ints, kernel_map, vectors, own, even, odd, conv1_weight, start
    )
    others = [from_ahead(hidden, "chan", j) for j in range(1, chans)]
    even, odd = owner_pairs(even, 0), owner_pairs(odd, 1)
    rim = jnp.concatenate([even, odd], axis=0)
    fars = [from_ahead(rim, "chan", j) for j in range(1, chans)]
    sums = [own_second(ints, kernel_map, conv2_weight, [hidden], start, 0, chans)]
    if others:
        sums.append(own_second(ints, kernel_map, conv2_weight, others, start, 1, chans))
    capacity = max(2, 2 * count // owners)
    partial = rim_second(
        ints,
        kernel_map,
        vectors,
        rows,
        conv2_weight,
        down_weight,
        even,
        odd,
        sums,
        fars,
        start,
        bricks,
        subs,
        chans,
        capacity,
    )
    partial = lax.all_to_all(
        partial, ("brick", "chan", "sub"), split_axis=0, concat_axis=0, tiled=True
    )
    return arrived_tiles(vectors, partial, bricks, subs, chans)


def solution(mesh):
    placed = (
        P(("groups", "brick", "chan", "sub"), None),
        P(("groups", "brick", "chan", "sub"), None),
        P(("groups", "brick", "sub"), None),
        P(("groups", "brick", "sub"), None),
        P(("groups", "brick", "sub"), None),
        P(None, "chan", None),
        P(None, "chan", None),
        P(None, "chan", None),
        P("chan"),
        P("chan"),
        P("chan"),
        P("chan"),
        P("chan"),
        P("chan"),
    )
    return jax.shard_map(
        body,
        mesh=mesh,
        in_specs=placed,
        out_specs=P(("groups", "brick", "sub"), "chan", None),
        check_vma=False,
    )
```

time: 69 us -> 61.2 us (0.89)
  blocking collectives: 0 us -> 15.6 us
  waiting for transfers between devices: 21.1 us -> 7.21 us
  starting transfers between devices: 29.9 us -> 17 us
  Pallas kernels: 13.5 us -> 17.5 us
  local copies, waits for them, and re-layouts: 3.9 us -> 2.51 us
  other arithmetic: 0.12 us -> 0.89 us
    all_to_all x0 -> x1, blocking collectives: none -> 15.6 us  [body(): lax.all_to_all(partial, ('brick', 'chan', 'sub'), split_axis=0, concat_ax...]
    ppermute x9 -> x4, waiting for transfers between devices: 11.9 us -> 2.15 us  [to_ahead(): lax.ppermute(block, axis, [(i, (i + distance) % n) for i in range(n)])]
    ppermute x9 -> x4, starting transfers between devices: 14 us -> 7.55 us  [to_ahead(): lax.ppermute(block, axis, [(i, (i + distance) % n) for i in range(n)])]
    ppermute x4, starting transfers between devices: 8.08 us -> 3.19 us  [owner_pairs(): return lax.ppermute(block, ('brick', 'chan', 'sub'), route)]
    pallas_call x5 -> x7, Pallas kernels: 12.5 us -> 16.5 us  [the longest x2 5.72 us: own_second(): pl.pallas_call(functools.partial(own_second_kernel, start, nearest, chans...]
    unnamed x29 -> x10, local copies, waits for them, and re-layouts: 3.87 us -> 0.97 us
    ppermute x4, waiting for transfers between devices: 2.59 us -> 0.01 us  [owner_pairs(): return lax.ppermute(block, ('brick', 'chan', 'sub'), route)]
    ppermute x7 -> x6, waiting for transfers between devices: 6.67 us -> 5.04 us  [from_ahead(): lax.ppermute(block, axis, [((i + distance) % n, i) for i in range(n)])]
  transfers between devices with their start and end apart: 20 -> 14, of which waited for: 13 -> 5; matrix products, arithmetic and copies ran while one was open for 0% -> 1% of each run, Pallas kernels for 0% -> 17%
where the time goes in v2:
time: 61.2 us; the launch traced here: 60.9 us
  Pallas kernels  17.5 us (29%)
  starting transfers between devices  17 us (28%)
  blocking collectives  15.6 us (25%)
  waiting for transfers between devices  7.21 us (12%)
  local copies, waits for them, and re-layouts  2.51 us (4%)
  other arithmetic  0.89 us (1%)
    all_to_all x1, blocking collectives, body(): lax.all_to_all(partial, ('brick', 'chan', 'sub'), split_axis=0, concat_ax...  15.6 us
    ppermute x4, starting transfers between devices, to_ahead(): lax.ppermute(block, axis, [(i, (i + distance) % n) for i in range(n)])  7.55 us
    ppermute x6, starting transfers between devices, from_ahead(): lax.ppermute(block, axis, [((i + distance) % n, i) for i in range(n)])  6.26 us
    pallas_call x2, Pallas kernels, own_second(): pl.pallas_call(functools.partial(own_second_kernel, start, nearest, chans...  5.72 us
    ppermute x6, waiting for transfers between devices, from_ahead(): lax.ppermute(block, axis, [((i + distance) % n, i) for i in range(n)])  5.04 us
    pallas_call x1, Pallas kernels, own_first(): pl.pallas_call(own_first_kernel, out_shape=jax.ShapeDtypeStruct((count, B...  4.48 us
    ppermute x4, starting transfers between devices, owner_pairs(): return lax.ppermute(block, ('brick', 'chan', 'sub'), route)  3.19 us
    pallas_call x1, Pallas kernels, rim_second(): pl.pallas_call(functools.partial(rim_second_kernel, start, bricks, subs,...  2.73 us
  transfers between devices with their start and end apart: 14, of which 5 were waited for; matrix products, arithmetic and copies ran while one was open for 1% of the time, Pallas kernels for 17%

profile of v2, /device:TPU:0, one launch (start us, length us, event | category | flops | bytes accessed | tf_op | source)
XLA Modules:
  0.0 60.9 jit_solution(404324977109340561)
XLA Ops:
  0.0 0.8 %reshape.6 = s32[1,4]{1,0:T(1,128)S(1)} reshape(s32[2,2]{1,0:T(2,128)} %param.17) | data formatting | bytes 32 | tf_op jit(solution)/shard_map/reshape | solution.py:426
  0.8 0.1 add_bitcast_fusion
  0.9 0.8 %pad_add_fusion.ints.order = s32[1,536]{1,0:T(1,128)S(1)} fusion(s32[1,16]{1,0:T(1,128)} %bitcast.19, s32[1,4]{1,0:T(1,128)S(1)} %reshape.6, s32[1,4]{1,0:T(1,128)S(1)} %add_bitcast_fusion, s32[1,512]{1,0:T(1,128)} %param.15), kind=kLoop, calls=%fused_computation.5 | loop fusion | flops 1608 | bytes 4288 | tf_op jit(solution)/shard_map/concatenate | solution.py:425
  1.6 0.9 %copy-done.2 = bf16[512,256]{1,0:T(8,128)(2,1)S(1)} copy-done((bf16[512,256]{1,0:T(8,128)(2,1)S(1)}, bf16[512,256]{1,0:T(8,128)(2,1)}, u32[]{:S(2)}) %copy-start.2) | copy-done | bytes 262168
  2.6 1.0 %sort_rows.1 = (bf16[4,64,256]{2,1,0:T(8,128)(2,1)S(1)}, bf16[4,64,256]{2,1,0:T(8,128)(2,1)S(1)}) custom-call(s32[1,536]{1,0:T(1,128)S(1)} %pad_add_fusion.ints.order, s32[1,536]{1,0:T(1,128)S(1)} %pad_add_fusion.ints.order, bf16[512,256]{1,0:T(8,128)(2,1)S(1)} %copy-done.2), custom_call_target="tpu_custom_call" | custom-call | tf_op jit(solution)/shard_map/sort_rows/pallas_call | solution.py:81
  3.6 0.5 collective-permute-start
  4.1 1.0 %collective-permute-done = bf16[4,64,256]{2,1,0:T(8,128)(2,1)S(1)} collective-permute-done((bf16[4,64,256]{2,1,0:T(8,128)(2,1)S(1)}, bf16[4,64,256]{2,1,0:T(8,128)(2,1)S(1)}, u32[]{:S(2)}, u32[]{:S(2)}) %collective-permute-start) | collective-permute-done | bytes 131104 | tf_op jit(solution)/shard_map/ppermute | solution.py:54
  5.1 3.0 %collective-permute-start.1 = (bf16[2,64,256]{2,1,0:T(8,128)(2,1)S(1)}, bf16[2,64,256]{2,1,0:T(8,128)(2,1)S(1)}, u32[]{:S(2)}, u32[]{:S(2)}) collective-permute-start(bf16[2,64,256]{2,1,0:T(8,128)(2,1)S(1)} %pad_maximum_fusion.1), channel_id=1, source_target_pairs={{0,4},{4,8},{8,12},{12,0},{1,5},{5,9},{9,13},{13,1},{2,6},{6,10},{... | collective-permute-start | bytes 196616 | tf_op jit(solution)/shard_map/ppermute | solution.py:54
  8.1 2.6 %collective-permute-start.2 = (bf16[2,64,256]{2,1,0:T(8,128)(2,1)S(1)}, bf16[2,64,256]{2,1,0:T(8,128)(2,1)S(1)}, u32[]{:S(2)}, u32[]{:S(2)}) collective-permute-start(bf16[2,64,256]{2,1,0:T(8,128)(2,1)S(1)} %pad_maximum_fusion.2), channel_id=1, source_target_pairs={{0,8},{4,12},{8,0},{12,4},{1,9},{5,13},{9,1},{13,5},{2,10},{6,14},... | collective-permute-start | bytes 196616 | tf_op jit(solution)/shard_map/ppermute | solution.py:54
  10.8 1.4 %collective-permute-start.3 = (bf16[2,64,256]{2,1,0:T(8,128)(2,1)S(1)}, bf16[2,64,256]{2,1,0:T(8,128)(2,1)S(1)}, u32[]{:S(2)}, u32[]{:S(2)}) collective-permute-start(bf16[2,64,256]{2,1,0:T(8,128)(2,1)S(1)} %pad_maximum_fusion.3), channel_id=1, source_target_pairs={{0,12},{4,0},{8,4},{12,8},{1,13},{5,1},{9,5},{13,9},{2,14},{6,2},{... | collective-permute-start | bytes 196616 | tf_op jit(solution)/shard_map/ppermute | solution.py:54
  12.2 1.6 %collective-permute-start.4 = (bf16[2,64,256]{2,1,0:T(8,128)(2,1)S(1)}, bf16[2,64,256]{2,1,0:T(8,128)(2,1)S(1)}, u32[]{:S(2)}, u32[]{:S(2)}) collective-permute-start(bf16[2,64,256]{2,1,0:T(8,128)(2,1)S(1)} %pad_maximum_fusion.refs_0_), channel_id=1, source_target_pairs={{2,0},{0,2},{3,1},{1,3},{6,4},{4,6},{7,5},{5,7},{10,8},{8,10},{11,... | collective-permute-start | bytes 196616 | tf_op jit(solution)/shard_map/ppermute | solution.py:49
  13.7 0.5 collective-permute-start.5
  14.3 1.2 %collective-permute-done.2.refs_2_ = bf16[2,64,256]{2,1,0:T(8,128)(2,1)S(1)} collective-permute-done((bf16[2,64,256]{2,1,0:T(8,128)(2,1)S(1)}, bf16[2,64,256]{2,1,0:T(8,128)(2,1)S(1)}, u32[]{:S(2)}, u32[]{:S(2)}) %collective-permute-start.2) | collective-permute-done | bytes 65568 | tf_op jit(solution)/shard_map/ppermute | solution.py:54
  15.4 1.5 %collective-permute-start.6 = (bf16[2,64,256]{2,1,0:T(8,128)(2,1)S(1)}, bf16[2,64,256]{2,1,0:T(8,128)(2,1)S(1)}, u32[]{:S(2)}, u32[]{:S(2)}) collective-permute-start(bf16[2,64,256]{2,1,0:T(8,128)(2,1)S(1)} %collective-permute-done.2.refs_2_), channel_id=1, source_target_pairs={{2,0},{0,2},{3,1},{1,3},{6,4},{4,6},{7,5},{5,7},{10,8},{8,10},{11,... | collective-permute-start | bytes 196616 | tf_op jit(solution)/shard_map/ppermute | solution.py:49
  16.9 0.5 collective-permute-start.7
  17.5 0.8 %stack.54.vectors = f32[6,128]{1,0:T(8,128)S(1)} concatenate(f32[1,128]{1,0:T(1,128)} %bitcast.13, f32[1,128]{1,0:T(1,128)} %bitcast.14, f32[1,128]{1,0:T(1,128)} %bitcast.15, f32[1,128]{1,0:T(1,128)} %bitcast.16, f32[1,128]{1,0:T(1,128)} %bitcast.17, f32[1,128]{1,0:T(1,128)} %bitcast.18), dimensions={0} | concatenate | bytes 6144 | tf_op jit(solution)/shard_map/stack | solution.py:428
  18.2 2.0 %collective-permute-done.6.refs_6_ = bf16[2,64,256]{2,1,0:T(8,128)(2,1)S(1)} collective-permute-done((bf16[2,64,256]{2,1,0:T(8,128)(2,1)S(1)}, bf16[2,64,256]{2,1,0:T(8,128)(2,1)S(1)}, u32[]{:S(2)}, u32[]{:S(2)}) %collective-permute-start.6) | collective-permute-done | bytes 65568 | tf_op jit(solution)/shard_map/ppermute | solution.py:49
  20.2 1.0 %collective-permute-done.7.refs_7_ = bf16[2,64,256]{2,1,0:T(8,128)(2,1)S(1)} collective-permute-done((bf16[2,64,256]{2,1,0:T(8,128)(2,1)S(1)}, bf16[2,64,256]{2,1,0:T(8,128)(2,1)S(1)}, u32[]{:S(2)}, u32[]{:S(2)}) %collective-permute-start.7) | collective-permute-done | bytes 65568 | tf_op jit(solution)/shard_map/ppermute | solution.py:49
  21.2 0.6 %assemble.1 = (bf16[16,64,256]{2,1,0:T(8,128)(2,1)S(1)}, bf16[2,64,256]{2,1,0:T(8,128)(2,1)S(1)}, bf16[2,64,256]{2,1,0:T(8,128)(2,1)S(1)}) custom-call(s32[1,536]{1,0:T(1,128)S(1)} %pad_add_fusion.ints.order, bf16[2,64,256]{2,1,0:T(8,128)(2,1)S(1)} %pad_maximum_fusion.refs_0_, bf16[2,64,256]{2,1,0:T(8,128)(2,1)S(1)} %collective-permute-done.1.refs_1_, ...), custom_call_target="tpu_custom_call" | custom-call | tf_op jit(solution)/shard_map/assemble/pallas_call | solution.py:112
  21.9 0.7 %collective-permute-start.9 = (bf16[2,64,256]{2,1,0:T(8,128)(2,1)S(1)}, bf16[2,64,256]{2,1,0:T(8,128)(2,1)S(1)}, u32[]{:S(2)}, u32[]{:S(2)}) collective-permute-start(bf16[2,64,256]{2,1,0:T(8,128)(2,1)S(1)} %get-tuple-element.17), channel_id=1, source_target_pairs={{1,4},{3,6},{5,8},{7,10},{9,12},{11,14},{4,1},{6,3},{8,5},{10,7},{... | collective-permute-start | bytes 196616 | tf_op jit(solution)/shard_map/ppermute | solution.py:44
  22.6 4.5 %own_first.1.own = f32[16,64,128]{2,1,0:T(8,128)S(1)} custom-call(s32[16,27]{1,0:T(8,128)S(1)} %copy-done.3, bf16[16,64,256]{2,1,0:T(8,128)(2,1)S(1)} %get-tuple-element.15.rows, bf16[27,128,256]{2,1,0:T(8,128)(2,1)S(1)} %copy-done.4), custom_call_target="tpu_custom_call" | custom-call | flops 3623878656 | tf_op jit(solution)/shard_map/own_first/pallas_call | solution.py:209
  27.1 2.2 %rim_first.1 = (bf16[16,64,128]{2,1,0:T(8,128)(2,1)S(1)}, bf16[2,64,128]{2,1,0:T(8,128)(2,1)S(1)}, bf16[2,64,128]{2,1,0:T(8,128)(2,1)S(1)}) custom-call(s32[1,536]{1,0:T(1,128)S(1)} %pad_add_fusion.ints.order, s32[16,27]{1,0:T(8,128)S(1)} %copy-done.3, f32[6,128]{1,0:T(8,128)S(1)} %stack.54.vectors, f32[16,64,128]{2,1,0:T(8,128)S(1)} %own_first.1.own, ...), custom_call_target="tpu_custom_call" | custom-call | flops 905969664 | tf_op jit(solution)/shard_map/rim_first/pallas_call | solution.py:245
  29.3 1.8 %collective-permute-start.10 = (bf16[2,64,128]{2,1,0:T(8,128)(2,1)S(1)}, bf16[2,64,128]{2,1,0:T(8,128)(2,1)S(1)}, u32[]{:S(2)}, u32[]{:S(2)}) collective-permute-start(bf16[2,64,128]{2,1,0:T(8,128)(2,1)S(1)} %get-tuple-element.18), channel_id=1, source_target_pairs={{0,1},{2,3},{4,5},{6,7},{8,9},{10,11},{12,13},{14,15},{1,0},{3,2},... | collective-permute-start | bytes 98312 | tf_op jit(solution)/shard_map/ppermute | solution.py:44
  31.2 0.7 %collective-permute-start.11 = (bf16[2,64,128]{2,1,0:T(8,128)(2,1)S(1)}, bf16[2,64,128]{2,1,0:T(8,128)(2,1)S(1)}, u32[]{:S(2)}, u32[]{:S(2)}) collective-permute-start(bf16[2,64,128]{2,1,0:T(8,128)(2,1)S(1)} %get-tuple-element.19), channel_id=1, source_target_pairs={{1,4},{3,6},{5,8},{7,10},{9,12},{11,14},{4,1},{6,3},{8,5},{10,7},{... | collective-permute-start | bytes 98312 | tf_op jit(solution)/shard_map/ppermute | solution.py:44
  31.8 1.6 %collective-permute-start.12 = (bf16[16,64,128]{2,1,0:T(8,128)(2,1)S(1)}, bf16[16,64,128]{2,1,0:T(8,128)(2,1)S(1)}, u32[]{:S(2)}, u32[]{:S(2)}) collective-permute-start(bf16[16,64,128]{2,1,0:T(8,128)(2,1)S(1)} %get-tuple-element.20.refs_0_), channel_id=1, source_target_pairs={{2,0},{0,2},{3,1},{1,3},{6,4},{4,6},{7,5},{5,7},{10,8},{8,10},{11,... | collective-permute-start | bytes 786440 | tf_op jit(solution)/shard_map/ppermute | solution.py:49
  33.4 2.9 %own_second.2.refs_2_ = f32[16,64,128]{2,1,0:T(8,128)S(1)} custom-call(s32[1,536]{1,0:T(1,128)S(1)} %pad_add_fusion.ints.order, s32[16,27]{1,0:T(8,128)S(1)} %copy-done.3, bf16[27,128,256]{2,1,0:T(8,128)(2,1)S(1)} %copy-done, bf16[16,64,128]{2,1,0:T(8,128)(2,1)S(1)} %get-tuple-element.20.refs_0_), custom_call_target="tpu_custom_call" | custom-call | flops 1811939328 | tf_op jit(solution)/shard_map/own_second/pallas_call | solution.py:286
  36.3 0.6 collective-permute-start.13
  36.9 2.1 %collective-permute-done.12.refs_0_ = bf16[16,64,128]{2,1,0:T(8,128)(2,1)S(1)} collective-permute-done((bf16[16,64,128]{2,1,0:T(8,128)(2,1)S(1)}, bf16[16,64,128]{2,1,0:T(8,128)(2,1)S(1)}, u32[]{:S(2)}, u32[]{:S(2)}) %collective-permute-start.12) | collective-permute-done | bytes 262176 | tf_op jit(solution)/shard_map/ppermute | solution.py:49
  39.0 2.9 %own_second.3.refs_3_ = f32[16,64,128]{2,1,0:T(8,128)S(1)} custom-call(s32[1,536]{1,0:T(1,128)S(1)} %pad_add_fusion.ints.order, s32[16,27]{1,0:T(8,128)S(1)} %copy-done.3, bf16[27,128,256]{2,1,0:T(8,128)(2,1)S(1)} %copy-done, bf16[16,64,128]{2,1,0:T(8,128)(2,1)S(1)} %collective-permute-done.12.refs_0_), custom_call_target="tpu_custom_call" | custom-call | flops 1811939328 | tf_op jit(solution)/shard_map/own_second/pallas_call | solution.py:286
  41.8 2.7 %rim_second.1 = bf16[16,32,128]{2,1,0:T(8,128)(2,1)S(1)} custom-call(s32[1,536]{1,0:T(1,128)S(1)} %pad_add_fusion.ints.order, s32[16,27]{1,0:T(8,128)S(1)} %copy-done.3, f32[6,128]{1,0:T(8,128)S(1)} %stack.54.vectors, bf16[16,64,256]{2,1,0:T(8,128)(2,1)S(1)} %get-tuple-element.15.rows, bf16[27,128,256]{2,1,0:T(8,128)(2,1)S(1)} %copy-done, ...), custom_call_target="tpu_custom_call" | custom-call | flops 905969664 | tf_op jit(solution)/shard_map/rim_second/pallas_call | solution.py:354
  44.6 15.6 %all_to_all.5.parts = bf16[16,32,128]{2,1,0:T(8,128)(2,1)S(1)} all-to-all(bf16[16,32,128]{2,1,0:T(8,128)(2,1)S(1)} %rim_second.1), channel_id=1, replica_groups=mesh['groups'=2,'brick'=4,'chan'=2,'sub'=2] {'brick','chan','sub'}, dimensions={0} | all-to-all | bytes 262144 | tf_op jit(solution)/shard_map/all_to_all | solution.py:469
  60.2 0.7 %arrived_tiles.1 = bf16[1,128,256]{2,1,0:T(8,128)(2,1)} custom-call(f32[6,128]{1,0:T(8,128)S(1)} %stack.54.vectors, bf16[16,32,128]{2,1,0:T(8,128)(2,1)S(1)} %all_to_all.5.parts), custom_call_target="tpu_custom_call" | custom-call | tf_op jit(solution)/shard_map/arrived_tiles/pallas_call | solution.py:384
  (26 shorter events, 0.2 us)
Async XLA Ops:
  0.0 22.6 %copy-start.3 = (s32[16,27]{1,0:T(8,128)S(1)}, s32[16,27]{1,0:T(8,128)}, u32[]{:S(2)}) copy-start(s32[16,27]{1,0:T(8,128)} %table.9) | copy-start | bytes 5188
  1.6 1.0 %copy-start.2 = (bf16[512,256]{1,0:T(8,128)(2,1)S(1)}, bf16[512,256]{1,0:T(8,128)(2,1)}, u32[]{:S(2)}) copy-start(bf16[512,256]{1,0:T(8,128)(2,1)} %rows.1) | copy-start | bytes 786436
  2.6 20.0 %copy-start.4 = (bf16[27,128,256]{2,1,0:T(8,128)(2,1)S(1)}, bf16[27,128,256]{2,1,0:T(8,128)(2,1)}, u32[]{:S(2)}) copy-start(bf16[27,128,256]{2,1,0:T(8,128)(2,1)} %weight.6) | copy-start | bytes 5308420
  3.6 1.5 %collective-permute-start = (bf16[4,64,256]{2,1,0:T(8,128)(2,1)S(1)}, bf16[4,64,256]{2,1,0:T(8,128)(2,1)S(1)}, u32[]{:S(2)}, u32[]{:S(2)}) collective-permute-start(bf16[4,64,256]{2,1,0:T(8,128)(2,1)S(1)} %get-tuple-element.14), channel_id=1, source_target_pairs={{0,1},{1,0},{2,3},{3,2},{4,5},{5,4},{6,7},{7,6},{8,9},{9,8},{10,11... | collective-permute-start | bytes 393224 | tf_op jit(solution)/shard_map/ppermute | solution.py:54
  5.1 8.6 %collective-permute-start.1 = (bf16[2,64,256]{2,1,0:T(8,128)(2,1)S(1)}, bf16[2,64,256]{2,1,0:T(8,128)(2,1)S(1)}, u32[]{:S(2)}, u32[]{:S(2)}) collective-permute-start(bf16[2,64,256]{2,1,0:T(8,128)(2,1)S(1)} %pad_maximum_fusion.1), channel_id=1, source_target_pairs={{0,4},{4,8},{8,12},{12,0},{1,5},{5,9},{9,13},{13,1},{2,6},{6,10},{... | collective-permute-start | bytes 196616 | tf_op jit(solution)/shard_map/ppermute | solution.py:54
  8.1 7.3 %collective-permute-start.2 = (bf16[2,64,256]{2,1,0:T(8,128)(2,1)S(1)}, bf16[2,64,256]{2,1,0:T(8,128)(2,1)S(1)}, u32[]{:S(2)}, u32[]{:S(2)}) collective-permute-start(bf16[2,64,256]{2,1,0:T(8,128)(2,1)S(1)} %pad_maximum_fusion.2), channel_id=1, source_target_pairs={{0,8},{4,12},{8,0},{12,4},{1,9},{5,13},{9,1},{13,5},{2,10},{6,14},... | collective-permute-start | bytes 196616 | tf_op jit(solution)/shard_map/ppermute | solution.py:54
  10.8 6.2 %collective-permute-start.3 = (bf16[2,64,256]{2,1,0:T(8,128)(2,1)S(1)}, bf16[2,64,256]{2,1,0:T(8,128)(2,1)S(1)}, u32[]{:S(2)}, u32[]{:S(2)}) collective-permute-start(bf16[2,64,256]{2,1,0:T(8,128)(2,1)S(1)} %pad_maximum_fusion.3), channel_id=1, source_target_pairs={{0,12},{4,0},{8,4},{12,8},{1,13},{5,1},{9,5},{13,9},{2,14},{6,2},{... | collective-permute-start | bytes 196616 | tf_op jit(solution)/shard_map/ppermute | solution.py:54
  12.2 6.1 %collective-permute-start.4 = (bf16[2,64,256]{2,1,0:T(8,128)(2,1)S(1)}, bf16[2,64,256]{2,1,0:T(8,128)(2,1)S(1)}, u32[]{:S(2)}, u32[]{:S(2)}) collective-permute-start(bf16[2,64,256]{2,1,0:T(8,128)(2,1)S(1)} %pad_maximum_fusion.refs_0_), channel_id=1, source_target_pairs={{2,0},{0,2},{3,1},{1,3},{6,4},{4,6},{7,5},{5,7},{10,8},{8,10},{11,... | collective-permute-start | bytes 196616 | tf_op jit(solution)/shard_map/ppermute | solution.py:49
  13.7 4.5 %collective-permute-start.5 = (bf16[2,64,256]{2,1,0:T(8,128)(2,1)S(1)}, bf16[2,64,256]{2,1,0:T(8,128)(2,1)S(1)}, u32[]{:S(2)}, u32[]{:S(2)}) collective-permute-start(bf16[2,64,256]{2,1,0:T(8,128)(2,1)S(1)} %collective-permute-done.1.refs_1_), channel_id=1, source_target_pairs={{2,0},{0,2},{3,1},{1,3},{6,4},{4,6},{7,5},{5,7},{10,8},{8,10},{11,... | collective-permute-start | bytes 196616 | tf_op jit(solution)/shard_map/ppermute | solution.py:49
  15.4 4.8 %collective-permute-start.6 = (bf16[2,64,256]{2,1,0:T(8,128)(2,1)S(1)}, bf16[2,64,256]{2,1,0:T(8,128)(2,1)S(1)}, u32[]{:S(2)}, u32[]{:S(2)}) collective-permute-start(bf16[2,64,256]{2,1,0:T(8,128)(2,1)S(1)} %collective-permute-done.2.refs_2_), channel_id=1, source_target_pairs={{2,0},{0,2},{3,1},{1,3},{6,4},{4,6},{7,5},{5,7},{10,8},{8,10},{11,... | collective-permute-start | bytes 196616 | tf_op jit(solution)/shard_map/ppermute | solution.py:49
  16.9 4.3 %collective-permute-start.7 = (bf16[2,64,256]{2,1,0:T(8,128)(2,1)S(1)}, bf16[2,64,256]{2,1,0:T(8,128)(2,1)S(1)}, u32[]{:S(2)}, u32[]{:S(2)}) collective-permute-start(bf16[2,64,256]{2,1,0:T(8,128)(2,1)S(1)} %collective-permute-done.3.refs_3_), channel_id=1, source_target_pairs={{2,0},{0,2},{3,1},{1,3},{6,4},{4,6},{7,5},{5,7},{10,8},{8,10},{11,... | collective-permute-start | bytes 196616 | tf_op jit(solution)/shard_map/ppermute | solution.py:49
  21.9 5.3 %collective-permute-start.8 = (bf16[2,64,256]{2,1,0:T(8,128)(2,1)S(1)}, bf16[2,64,256]{2,1,0:T(8,128)(2,1)S(1)}, u32[]{:S(2)}, u32[]{:S(2)}) collective-permute-start(bf16[2,64,256]{2,1,0:T(8,128)(2,1)S(1)} %get-tuple-element.16), channel_id=1, source_target_pairs={{0,1},{2,3},{4,5},{6,7},{8,9},{10,11},{12,13},{14,15},{1,0},{3,2},... | collective-permute-start | bytes 196616 | tf_op jit(solution)/shard_map/ppermute | solution.py:44
  21.9 5.2 %collective-permute-start.9 = (bf16[2,64,256]{2,1,0:T(8,128)(2,1)S(1)}, bf16[2,64,256]{2,1,0:T(8,128)(2,1)S(1)}, u32[]{:S(2)}, u32[]{:S(2)}) collective-permute-start(bf16[2,64,256]{2,1,0:T(8,128)(2,1)S(1)} %get-tuple-element.17), channel_id=1, source_target_pairs={{1,4},{3,6},{5,8},{7,10},{9,12},{11,14},{4,1},{6,3},{8,5},{10,7},{... | collective-permute-start | bytes 196616 | tf_op jit(solution)/shard_map/ppermute | solution.py:44
  27.1 6.3 %copy-start = (bf16[27,128,256]{2,1,0:T(8,128)(2,1)S(1)}, bf16[27,128,256]{2,1,0:T(8,128)(2,1)}, u32[]{:S(2)}) copy-start(bf16[27,128,256]{2,1,0:T(8,128)(2,1)} %weight.9) | copy-start | bytes 5308420
  29.3 6.9 %collective-permute-start.10 = (bf16[2,64,128]{2,1,0:T(8,128)(2,1)S(1)}, bf16[2,64,128]{2,1,0:T(8,128)(2,1)S(1)}, u32[]{:S(2)}, u32[]{:S(2)}) collective-permute-start(bf16[2,64,128]{2,1,0:T(8,128)(2,1)S(1)} %get-tuple-element.18), channel_id=1, source_target_pairs={{0,1},{2,3},{4,5},{6,7},{8,9},{10,11},{12,13},{14,15},{1,0},{3,2},... | collective-permute-start | bytes 98312 | tf_op jit(solution)/shard_map/ppermute | solution.py:44
  31.2 5.1 %collective-permute-start.11 = (bf16[2,64,128]{2,1,0:T(8,128)(2,1)S(1)}, bf16[2,64,128]{2,1,0:T(8,128)(2,1)S(1)}, u32[]{:S(2)}, u32[]{:S(2)}) collective-permute-start(bf16[2,64,128]{2,1,0:T(8,128)(2,1)S(1)} %get-tuple-element.19), channel_id=1, source_target_pairs={{1,4},{3,6},{5,8},{7,10},{9,12},{11,14},{4,1},{6,3},{8,5},{10,7},{... | collective-permute-start | bytes 98312 | tf_op jit(solution)/shard_map/ppermute | solution.py:44
  31.8 7.1 %collective-permute-start.12 = (bf16[16,64,128]{2,1,0:T(8,128)(2,1)S(1)}, bf16[16,64,128]{2,1,0:T(8,128)(2,1)S(1)}, u32[]{:S(2)}, u32[]{:S(2)}) collective-permute-start(bf16[16,64,128]{2,1,0:T(8,128)(2,1)S(1)} %get-tuple-element.20.refs_0_), channel_id=1, source_target_pairs={{2,0},{0,2},{3,1},{1,3},{6,4},{4,6},{7,5},{5,7},{10,8},{8,10},{11,... | collective-permute-start | bytes 786440 | tf_op jit(solution)/shard_map/ppermute | solution.py:49
  36.3 5.6 %copy-start.1 = (bf16[8,128,256]{2,1,0:T(8,128)(2,1)S(1)}, bf16[8,128,256]{2,1,0:T(8,128)(2,1)}, u32[]{:S(2)}) copy-start(bf16[8,128,256]{2,1,0:T(8,128)(2,1)} %down_weight.1) | copy-start | bytes 1572868
  36.3 5.5 %collective-permute-start.13 = (bf16[4,64,128]{2,1,0:T(8,128)(2,1)S(1)}, bf16[4,64,128]{2,1,0:T(8,128)(2,1)S(1)}, u32[]{:S(2)}, u32[]{:S(2)}) collective-permute-start(bf16[4,64,128]{2,1,0:T(8,128)(2,1)S(1)} %pad_maximum_fusion.4), channel_id=1, source_target_pairs={{2,0},{0,2},{3,1},{1,3},{6,4},{4,6},{7,5},{5,7},{10,8},{8,10},{11,... | collective-permute-start | bytes 196616 | tf_op jit(solution)/shard_map/ppermute | solution.py:49

commit v3 on v2

--- a/solution.py
+++ b/solution.py
@@ -54,63 +54,34 @@
     return lax.ppermute(block, axis, [(i, (i + distance) % n) for i in range(n)])
 
 
-def sort_kernel(bricks, subs, ints, order, rows, *outs):
-    total = rows.shape[0]
-    place = Place(ints, total)
-    per = total // (bricks * subs)
-    taken = lax.broadcasted_iota(jnp.int32, (total, total), 0) == order[:, :total]
-    onehot = jnp.where(taken, 1.0, 0.0).astype(BF16)
-    picked = lax.dot_general(
-        onehot, rows[...], (((0,), (0,)), ((), ())), preferred_element_type=F32
-    ).astype(BF16)
-    for b in range(bricks):
-        for s in range(subs):
-            away = lax.rem(s - place.sub + subs, subs)
-            ahead = lax.rem(b - place.brick + bricks, bricks)
-            start = (b * subs + s) * per
-            for js in range(subs):
-
-                @pl.when(away == js)
-                def _(js=js, ahead=ahead, start=start):
-                    outs[js][ahead] = picked[start : start + per]
-
-
-def sort_rows(ints, features, bricks, subs):
-    per = features.shape[0] // (bricks * subs)
-    piece = jax.ShapeDtypeStruct((bricks, per, features.shape[1]), BF16)
-    return pl.pallas_call(
-        functools.partial(sort_kernel, bricks, subs),
-        out_shape=[piece] * subs,
-        in_specs=[SMEM, VMEM, VMEM],
-        out_specs=[VMEM] * subs,
-        compiler_params=LIMIT,
-        name="sort_rows",
-    )(ints, ints, features)
-
-
-def assemble_kernel(start, reach, bricks, subs, chans, ints, *refs):
-    parts, (rows, even, odd) = refs[:-3], refs[-3:]
+def sorted_rows(scan_order, features):
+    total = features.shape[0]
+    taken = scan_order.reshape(total, 1) == jnp.arange(total, dtype=jnp.int32)[None]
+    return jnp.dot(taken.astype(BF16), features, preferred_element_type=F32).astype(BF16)
+
+
+def assemble_kernel(start, reach, bricks, subs, chans, keys, ints, *refs):
+    parts, (rows, even, odd) = dict(zip(keys, refs[:-3])), refs[-3:]
     place = Place(ints, start, reach)
-    split = BLK // parts[0].shape[1]
-    for j in range(chans):
+    split = BLK // parts[0, 0].shape[1]
+    for (jb, j), part in parts.items():
+        source = lax.rem(place.brick - jb + bricks, bricks)
         chan = lax.rem(place.chan + j, chans)
-        for jb in range(bricks):
-            source = lax.rem(place.brick - jb + bricks, bricks)
-            for js in range(subs):
-                sub = lax.rem(place.sub + js, subs)
-                rows[(source * subs + sub) * chans + chan] = parts[j * bricks + jb][js]
+        for js in range(subs):
+            sub = lax.rem(place.sub + js, subs)
+            rows[(source * subs + sub) * chans + chan] = part[js]
     for j in range(reach):
         even[pl.ds(j * split, split)] = rows[pl.ds(place.halo(place.parity, j) * split, split)]
         odd[pl.ds(j * split, split)] = rows[pl.ds(place.halo(1 - place.parity, j) * split, split)]
 
 
 def assemble(ints, parts, start, reach, bricks, subs, chans):
-    per, channels = parts[0].shape[1:]
+    per, channels = parts[0, 0].shape[1:]
     pieces = bricks * subs * chans
     split = BLK // per
     sent = reach * split
     return pl.pallas_call(
-        functools.partial(assemble_kernel, start, reach, bricks, subs, chans),
+        functools.partial(assemble_kernel, start, reach, bricks, subs, chans, tuple(parts)),
         out_shape=[
             jax.ShapeDtypeStruct((count, per, channels), BF16) for count in (pieces, sent, sent)
         ],
@@ -118,7 +89,7 @@
         out_specs=[VMEM] * 3,
         compiler_params=LIMIT,
         name="assemble",
-    )(ints, *parts)
+    )(ints, *parts.values())
 
 
 def block_sums(table, blocks, weight, total):
@@ -160,11 +131,11 @@
     rim[pl.ds(reach * place.parity, reach), :, lanes] = odd[...]
 
 
-def rim_sums(count, table, rim, weight, products, total):
-    blocks, offsets = rim.shape[0], table.shape[1]
+def named_sums(table, given, weight, products, total):
+    blocks, offsets = given.shape[0], table.shape[1]
     width, channels = weight.shape[1:]
     together = max(1, channels // width)
-    rows = rim[...].reshape(blocks * BLK, channels)
+    rows = given[...].reshape(blocks * BLK, channels)
     for k in range(0, offsets, together):
         size = min(together, offsets - k)
         product = lax.dot_general(
@@ -182,12 +153,11 @@
     def one_block(n, carry):
         running = total[n]
         for k in range(offsets):
-            index = table[n, k]
-            running = running + products[k, jnp.where(index < count, blocks, index - count)]
+            running = running + products[k, table[n, k]]
         total[n] = running
         return carry
 
-    lax.fori_loop(0, count, one_block, 0, unroll=min(count, 16))
+    lax.fori_loop(0, table.shape[0], one_block, 0, unroll=min(table.shape[0], 16))
 
 
 def cost(blocks, weight):
@@ -218,12 +188,46 @@
     )(table, rows, weight)
 
 
+def pieces_first_kernel(bricks, subs, behind, started, ints, table, weight, *refs):
+    parts, (total, held, products) = refs[:-3], refs[-3:]
+    if started:
+        parts, before = parts[:-1], parts[-1]
+    place = Place(ints, 0)
+    for jb, part in zip(behind, parts):
+        source = lax.rem(place.brick - jb + bricks, bricks)
+        for js in range(subs):
+            held[source * subs + lax.rem(place.sub + js, subs)] = part[js]
+    total[...] = before[...] if started else jnp.zeros(total.shape, F32)
+    named_sums(table, held, weight, products, total)
+
+
+def pieces_first(ints, table, weight, parts, before, j, bricks, subs):
+    offsets, width, channels = weight.shape
+    sums = jax.ShapeDtypeStruct((table.shape[0], BLK, width), F32)
+    held = bricks * subs
+    behind = tuple(jb for jb, far in parts if far == j)
+    given = [parts[jb, j] for jb in behind] + ([] if before is None else [before])
+    return pl.pallas_call(
+        functools.partial(pieces_first_kernel, bricks, subs, behind, before is not None),
+        out_shape=sums,
+        in_specs=[SMEM, SMEM] + [VMEM] * (1 + len(given)),
+        out_specs=VMEM,
+        scratch_shapes=[
+            pltpu.VMEM((held, BLK, channels), BF16),
+            pltpu.VMEM((offsets, held + 1, BLK, width), F32),
+        ],
+        compiler_params=LIMIT,
+        cost_estimate=cost(held, weight),
+        name="pieces_first",
+    )(ints, table, weight, *given)
+
+
 def rim_first_kernel(start, ints, table, vectors, own, even, odd, weight, hidden, even_out, odd_out, rim, products, total):
     count, reach = table.shape[0], even.shape[0]
     place = Place(ints, start, reach)
     rim_blocks(place, even, odd, slice(None), rim)
     total[...] = own[...]
-    rim_sums(count, table, rim, weight, products, total)
+    named_sums(table, rim, weight, products, total)
     value = total[...] * vectors[0:1][None] + vectors[1:2][None]
     hidden[...] = jnp.maximum(value, 0.0).astype(BF16)
     for j in range(reach):
@@ -254,6 +258,23 @@
         cost_estimate=cost(2 * reach, weight),
         name="rim_first",
     )(ints, table, vectors, own, even, odd, weight)
+
+
+def pack_kernel(even, odd, *refs):
+    out = refs[-1]
+    out[0 : even.shape[0]] = even[...]
+    out[even.shape[0] :] = odd[...]
+
+
+def pack(even, odd, after):
+    return pl.pallas_call(
+        pack_kernel,
+        out_shape=jax.ShapeDtypeStruct((2 * even.shape[0],) + even.shape[1:], BF16),
+        in_specs=[VMEM, VMEM] + [pl.BlockSpec(memory_space=pl.ANY)] * len(after),
+        out_specs=VMEM,
+        compiler_params=LIMIT,
+        name="pack",
+    )(even, odd, *after)
 
 
 def own_second_kernel(start, nearest, chans, ints, table, weight, *refs):
@@ -316,7 +337,7 @@
     total[...] = sums[0][...]
     for more in sums[1:]:
         total[...] += more[...]
-    rim_sums(count, table, rim, weight, products, total)
+    named_sums(table, rim, weight, products, total)
     for c in range(chans):
 
         @pl.when(place.chan == c)
@@ -391,12 +412,27 @@
     )(vectors, parts)
 
 
-def to_owners(pieces, bricks, subs):
-    by_sub = [pieces[0]]
+def to_owners(ordered, chans):
+    bricks, subs = ordered.shape[:2]
+    brick, sub = lax.axis_index("brick"), lax.axis_index("sub")
+
+    def pieces(js):
+        column = lax.dynamic_index_in_dim(ordered, lax.rem(sub + js, subs), 1, keepdims=False)
+        doubled = jnp.concatenate([column, column], axis=0)
+        return lax.dynamic_slice_in_dim(doubled, brick, bricks, 0)
+
+    by_sub = [pieces(0)]
     for js in range(1, subs):
-        by_sub.append(to_ahead(pieces[subs - js], "sub", subs - js))
+        by_sub.append(to_ahead(pieces(subs - js), "sub", subs - js))
     stacked = [jnp.stack([piece[jb] for piece in by_sub]) for jb in range(bricks)]
-    return [stacked[0]] + [to_ahead(stacked[jb], "brick", jb) for jb in range(1, bricks)]
+    order = sorted(range(1, bricks), key=lambda jb: min(jb, bricks - jb))
+    parts = {(0, 0): stacked[0]}
+    for jb in order:
+        parts[jb, 0] = to_ahead(stacked[jb], "brick", jb)
+    for jb in [0] + order:
+        for j in range(1, chans):
+            parts[jb, j] = from_ahead(parts[jb, 0], "chan", j)
+    return parts
 
 
 def body(
@@ -419,31 +455,37 @@
     owners = bricks * subs
     count, reach = kernel_map.shape[0], halo_send.shape[1]
     channels = features.shape[1]
-    start = features.shape[0]
+    start = 0
     brick, sub, chan = (lax.axis_index(axis) for axis in ("brick", "sub", "chan"))
     place = jnp.stack([brick, sub, chan, lax.rem(brick * subs + sub, 2)]).astype(jnp.int32)
+    ordered = sorted_rows(scan_order, features)
+    ordered = ordered.reshape(bricks, subs, features.shape[0] // owners, channels)
+    parts = to_owners(ordered, chans)
     ints = jnp.concatenate(
-        [scan_order, place[None], halo_send.reshape(1, -1), down_route.reshape(1, -1)], axis=1
+        [place[None], halo_send[0:1], halo_send[1:2], down_route.reshape(1, -1)], axis=1
     )
     vectors = jnp.stack(
         [gain_first, bias_first, gain_second, bias_second, gain_down, bias_down]
     )
-    pieces = sort_rows(ints, features, bricks, subs)
-    arrived = to_owners(pieces, bricks, subs)
-    parts = arrived + [
-        from_ahead(piece, "chan", j) for j in range(1, chans) for piece in arrived
-    ]
     rows, even, odd = assemble(ints, parts, start, reach, bricks, subs, chans)
     rows = rows.reshape(count, BLK, channels)
     even = owner_pairs(even, 0).reshape(reach, BLK, channels)
     odd = owner_pairs(odd, 1).reshape(reach, BLK, channels)
-    own = own_first(kernel_map, rows, conv1_weight)
+    outside = jnp.where(kernel_map < count, 2 * reach, kernel_map - count)
+    if features.shape[0] // owners == BLK:
+        own = None
+        for j in range(chans):
+            here = (kernel_map < count) & (lax.rem(kernel_map, chans) == lax.rem(chan + j, chans))
+            inside = jnp.where(here, lax.div(kernel_map, chans), owners)
+            own = pieces_first(ints, inside, conv1_weight, parts, own, j, bricks, subs)
+    else:
+        own = own_first(kernel_map, rows, conv1_weight)
     hidden, even, odd = rim_first(
-        ints, kernel_map, vectors, own, even, odd, conv1_weight, start
+        ints, outside, vectors, own, even, odd, conv1_weight, start
     )
     others = [from_ahead(hidden, "chan", j) for j in range(1, chans)]
     even, odd = owner_pairs(even, 0), owner_pairs(odd, 1)
-    rim = jnp.concatenate([even, odd], axis=0)
+    rim = pack(even, odd, others)
     fars = [from_ahead(rim, "chan", j) for j in range(1, chans)]
     sums = [own_second(ints, kernel_map, conv2_weight, [hidden], start, 0, chans)]
     if others:
@@ -451,7 +493,7 @@
     capacity = max(2, 2 * count // owners)
     partial = rim_second(
         ints,
-        kernel_map,
+        outside,
         vectors,
         rows,
         conv2_weight,

time: 61.2 us -> 55.1 us (0.900)
  waiting for transfers between devices: 7.21 us -> 2.5 us
  blocking collectives: 15.6 us -> 13.8 us
  starting transfers between devices: 17 us -> 18.5 us
  matrix products: 0 us -> 1.04 us
  Pallas kernels: 17.5 us -> 16.7 us
  local copies, waits for them, and re-layouts: 2.51 us -> 1.74 us
    ppermute x6, waiting for transfers between devices: 5.04 us -> 0.65 us  [from_ahead(): lax.ppermute(block, axis, [((i + distance) % n, i) for i in range(n)])]
    all_to_all x1, blocking collectives: 15.6 us -> 13.8 us  [body(): lax.all_to_all(partial, ('brick', 'chan', 'sub'), split_axis=0, concat_ax...]
    ppermute x6, starting transfers between devices: 6.26 us -> 7.96 us  [from_ahead(): lax.ppermute(block, axis, [((i + distance) % n, i) for i in range(n)])]
    dot_general x0 -> x1, matrix products: none -> 1.04 us  [sorted_rows(): jnp.dot(taken.astype(BF16), features, preferred_element_type=F32)]
    ppermute x4, starting transfers between devices: 7.55 us -> 6.54 us  [to_ahead(): lax.ppermute(block, axis, [(i, (i + distance) % n) for i in range(n)])]
    ppermute x4, starting transfers between devices: 3.19 us -> 3.97 us  [owner_pairs(): return lax.ppermute(block, ('brick', 'chan', 'sub'), route)]
    reshape x1 -> x0, local copies, waits for them, and re-layouts: 0.77 us -> none  [body(): halo_send.reshape(1, -1)]
    slice x0 -> x1, local copies, waits for them, and re-layouts: none -> 0.76 us  [body(): halo_send[0:1]]
  transfers between devices with their start and end apart: 14 -> 14, of which waited for: 5 -> 3; matrix products, arithmetic and copies ran while one was open for 1% -> 2% of each run, Pallas kernels for 17% -> 19%
where the time goes in v3:
time: 55.1 us; the launch traced here: 54.9 us
  starting transfers between devices  18.5 us (34%)
  Pallas kernels  16.7 us (30%)
  blocking collectives  13.8 us (25%)
  waiting for transfers between devices  2.5 us (5%)
  local copies, waits for them, and re-layouts  1.74 us (3%)
  matrix products  1.04 us (2%)
    all_to_all x1, blocking collectives, body(): lax.all_to_all(partial, ('brick', 'chan', 'sub'), split_axis=0, concat_ax...  13.8 us
    ppermute x6, starting transfers between devices, from_ahead(): lax.ppermute(block, axis, [((i + distance) % n, i) for i in range(n)])  7.96 us
    ppermute x4, starting transfers between devices, to_ahead(): lax.ppermute(block, axis, [(i, (i + distance) % n) for i in range(n)])  6.54 us
    pallas_call x2, Pallas kernels, own_second(): pl.pallas_call(functools.partial(own_second_kernel, start, nearest, chans...  5.65 us
    pallas_call x2, Pallas kernels, pieces_first(): pl.pallas_call(functools.partial(pieces_first_kernel, bricks, subs, behin...  4.93 us
    ppermute x4, starting transfers between devices, owner_pairs(): return lax.ppermute(block, ('brick', 'chan', 'sub'), route)  3.97 us
    pallas_call x1, Pallas kernels, rim_second(): pl.pallas_call(functools.partial(rim_second_kernel, start, bricks, subs,...  2.66 us
    pallas_call x1, Pallas kernels, rim_first(): pl.pallas_call(functools.partial(rim_first_kernel, start), out_shape=[jax...  2.07 us
  transfers between devices with their start and end apart: 14, of which 3 were waited for; matrix products, arithmetic and copies ran while one was open for 2% of the time, Pallas kernels for 19%

profile of v3, /device:TPU:0, one launch (start us, length us, event | category | flops | bytes accessed | tf_op | source)
XLA Modules:
  0.0 54.9 jit_solution(4440856211707963413)
XLA Ops:
  0.1 0.9 %copy-done = bf16[512,256]{1,0:T(8,128)(2,1)S(1)} copy-done((bf16[512,256]{1,0:T(8,128)(2,1)S(1)}, bf16[512,256]{1,0:T(8,128)(2,1)}, u32[]{:S(2)}) %copy-start) | copy-done | bytes 262168
  1.0 1.0 %convolution_convert_fusion = bf16[512,256]{1,0:T(8,128)(2,1)S(1)} fusion(bf16[512,256]{1,0:T(8,128)(2,1)S(1)} %copy-done, s32[512]{0:T(512)} %bitcast.32), kind=kOutput, calls=%fused_computation | convolution fusion | flops 134610944 | bytes 526336 | tf_op jit(solution)/shard_map/dot_general | solution.py:60
  2.0 0.1 fusion.1
  2.1 0.5 collective-permute-start
  2.6 0.8 %fusion.5 = (s32[1,2]{1,0:T(1,128)S(1)}, s32[1,2]{1,0:T(1,128)S(1)}) fusion(s32[2,2]{1,0:T(2,128)} %param.17), kind=kLoop, calls=%fused_computation.26 | loop fusion | bytes 32 | tf_op jit(solution)/shard_map/slice | solution.py:465
  3.5 0.1 add_bitcast_fusion
  3.6 0.1 pad_add_fusion.ints
  3.8 2.9 %collective-permute-start.1 = (bf16[2,64,256]{2,1,0:T(8,128)(2,1)S(1)}, bf16[2,64,256]{2,1,0:T(8,128)(2,1)S(1)}, u32[]{:S(2)}, u32[]{:S(2)}) collective-permute-start(bf16[2,64,256]{2,1,0:T(8,128)(2,1)S(1)} %pad_maximum_fusion.1), channel_id=1, source_target_pairs={{0,4},{4,8},{8,12},{12,0},{1,5},{5,9},{9,13},{13,1},{2,6},{6,10},{... | collective-permute-start | bytes 196616 | tf_op jit(solution)/shard_map/ppermute | solution.py:54
  6.6 2.1 %collective-permute-start.2 = (bf16[2,64,256]{2,1,0:T(8,128)(2,1)S(1)}, bf16[2,64,256]{2,1,0:T(8,128)(2,1)S(1)}, u32[]{:S(2)}, u32[]{:S(2)}) collective-permute-start(bf16[2,64,256]{2,1,0:T(8,128)(2,1)S(1)} %pad_maximum_fusion.2), channel_id=1, source_target_pairs={{0,12},{4,0},{8,4},{12,8},{1,13},{5,1},{9,5},{13,9},{2,14},{6,2},{... | collective-permute-start | bytes 196616 | tf_op jit(solution)/shard_map/ppermute | solution.py:54
  8.7 1.0 %collective-permute-start.3 = (bf16[2,64,256]{2,1,0:T(8,128)(2,1)S(1)}, bf16[2,64,256]{2,1,0:T(8,128)(2,1)S(1)}, u32[]{:S(2)}, u32[]{:S(2)}) collective-permute-start(bf16[2,64,256]{2,1,0:T(8,128)(2,1)S(1)} %pad_maximum_fusion.3), channel_id=1, source_target_pairs={{0,8},{4,12},{8,0},{12,4},{1,9},{5,13},{9,1},{13,5},{2,10},{6,14},... | collective-permute-start | bytes 196616 | tf_op jit(solution)/shard_map/ppermute | solution.py:54
  9.8 1.6 %collective-permute-start.4 = (bf16[2,64,256]{2,1,0:T(8,128)(2,1)S(1)}, bf16[2,64,256]{2,1,0:T(8,128)(2,1)S(1)}, u32[]{:S(2)}, u32[]{:S(2)}) collective-permute-start(bf16[2,64,256]{2,1,0:T(8,128)(2,1)S(1)} %pad_maximum_fusion.refs_0_), channel_id=1, source_target_pairs={{2,0},{0,2},{3,1},{1,3},{6,4},{4,6},{7,5},{5,7},{10,8},{8,10},{11,... | collective-permute-start | bytes 196616 | tf_op jit(solution)/shard_map/ppermute | solution.py:49
  11.4 1.5 %collective-permute-start.5 = (bf16[2,64,256]{2,1,0:T(8,128)(2,1)S(1)}, bf16[2,64,256]{2,1,0:T(8,128)(2,1)S(1)}, u32[]{:S(2)}, u32[]{:S(2)}) collective-permute-start(bf16[2,64,256]{2,1,0:T(8,128)(2,1)S(1)} %collective-permute-done.1.refs_1_), channel_id=1, source_target_pairs={{2,0},{0,2},{3,1},{1,3},{6,4},{4,6},{7,5},{5,7},{10,8},{8,10},{11,... | collective-permute-start | bytes 196616 | tf_op jit(solution)/shard_map/ppermute | solution.py:49
  12.8 0.7 %collective-permute-start.6 = (bf16[2,64,256]{2,1,0:T(8,128)(2,1)S(1)}, bf16[2,64,256]{2,1,0:T(8,128)(2,1)S(1)}, u32[]{:S(2)}, u32[]{:S(2)}) collective-permute-start(bf16[2,64,256]{2,1,0:T(8,128)(2,1)S(1)} %collective-permute-done.2.refs_2_), channel_id=1, source_target_pairs={{2,0},{0,2},{3,1},{1,3},{6,4},{4,6},{7,5},{5,7},{10,8},{8,10},{11,... | collective-permute-start | bytes 196616 | tf_op jit(solution)/shard_map/ppermute | solution.py:49
  13.6 1.8 %collective-permute-done.3.refs_3_ = bf16[2,64,256]{2,1,0:T(8,128)(2,1)S(1)} collective-permute-done((bf16[2,64,256]{2,1,0:T(8,128)(2,1)S(1)}, bf16[2,64,256]{2,1,0:T(8,128)(2,1)S(1)}, u32[]{:S(2)}, u32[]{:S(2)}) %collective-permute-start.3) | collective-permute-done | bytes 65568 | tf_op jit(solution)/shard_map/ppermute | solution.py:54
  15.4 1.5 %collective-permute-start.7 = (bf16[2,64,256]{2,1,0:T(8,128)(2,1)S(1)}, bf16[2,64,256]{2,1,0:T(8,128)(2,1)S(1)}, u32[]{:S(2)}, u32[]{:S(2)}) collective-permute-start(bf16[2,64,256]{2,1,0:T(8,128)(2,1)S(1)} %collective-permute-done.3.refs_3_), channel_id=1, source_target_pairs={{2,0},{0,2},{3,1},{1,3},{6,4},{4,6},{7,5},{5,7},{10,8},{8,10},{11,... | collective-permute-start | bytes 196616 | tf_op jit(solution)/shard_map/ppermute | solution.py:49
  16.9 2.4 %pieces_first.2.refs_4_ = f32[16,64,128]{2,1,0:T(8,128)S(1)} custom-call(s32[1,24]{1,0:T(1,128)S(1)} %pad_add_fusion.ints, s32[16,27]{1,0:T(8,128)S(1)} %get-tuple-element.27.table, bf16[27,128,256]{2,1,0:T(8,128)(2,1)S(1)} %copy-done.4, bf16[2,64,256]{2,1,0:T(8,128)(2,1)S(1)} %pad_maximum_fusion.refs_0_, ...), custom_call_target="tpu_custom_call" | custom-call | flops 1811939328 | tf_op jit(solution)/shard_map/pieces_first/pallas_call | solution.py:210
  19.4 0.3 collective-permute-done.7.refs_7_.refs_3_
  19.7 0.6 %assemble.1 = (bf16[16,64,256]{2,1,0:T(8,128)(2,1)S(1)}, bf16[2,64,256]{2,1,0:T(8,128)(2,1)S(1)}, bf16[2,64,256]{2,1,0:T(8,128)(2,1)S(1)}) custom-call(s32[1,24]{1,0:T(1,128)S(1)} %pad_add_fusion.ints, bf16[2,64,256]{2,1,0:T(8,128)(2,1)S(1)} %pad_maximum_fusion.refs_0_, bf16[2,64,256]{2,1,0:T(8,128)(2,1)S(1)} %collective-permute-done.1.refs_1_, ...), custom_call_target="tpu_custom_call" | custom-call | tf_op jit(solution)/shard_map/assemble/pallas_call | solution.py:83
  20.3 0.1 collective-permute-start.8
  20.3 0.7 %collective-permute-start.9 = (bf16[2,64,256]{2,1,0:T(8,128)(2,1)S(1)}, bf16[2,64,256]{2,1,0:T(8,128)(2,1)S(1)}, u32[]{:S(2)}, u32[]{:S(2)}) collective-permute-start(bf16[2,64,256]{2,1,0:T(8,128)(2,1)S(1)} %get-tuple-element.13), channel_id=1, source_target_pairs={{1,4},{3,6},{5,8},{7,10},{9,12},{11,14},{4,1},{6,3},{8,5},{10,7},{... | collective-permute-start | bytes 196616 | tf_op jit(solution)/shard_map/ppermute | solution.py:44
  21.0 2.5 %pieces_first.3.own = f32[16,64,128]{2,1,0:T(8,128)S(1)} custom-call(s32[1,24]{1,0:T(1,128)S(1)} %pad_add_fusion.ints, s32[16,27]{1,0:T(8,128)S(1)} %get-tuple-element.29.table, bf16[27,128,256]{2,1,0:T(8,128)(2,1)S(1)} %copy-done.4, bf16[2,64,256]{2,1,0:T(8,128)(2,1)S(1)} %collective-permute-done.4.refs_4_.refs_0_, ...), custom_call_target="tpu_custom_call" | custom-call | flops 1811939328 | tf_op jit(solution)/shard_map/pieces_first/pallas_call | solution.py:210
  23.5 2.1 %rim_first.1 = (bf16[16,64,128]{2,1,0:T(8,128)(2,1)S(1)}, bf16[2,64,128]{2,1,0:T(8,128)(2,1)S(1)}, bf16[2,64,128]{2,1,0:T(8,128)(2,1)S(1)}) custom-call(s32[1,24]{1,0:T(1,128)S(1)} %pad_add_fusion.ints, s32[16,27]{1,0:T(8,128)S(1)} %get-tuple-element.28.table, f32[6,128]{1,0:T(8,128)S(1)} %stack.54.vectors, f32[16,64,128]{2,1,0:T(8,128)S(1)} %pieces_first.3.own, ...), custom_call_target="tpu_custom_call" | custom-call | flops 905969664 | tf_op jit(solution)/shard_map/rim_first/pallas_call | solution.py:249
  25.6 1.6 %collective-permute-start.12 = (bf16[16,64,128]{2,1,0:T(8,128)(2,1)S(1)}, bf16[16,64,128]{2,1,0:T(8,128)(2,1)S(1)}, u32[]{:S(2)}, u32[]{:S(2)}) collective-permute-start(bf16[16,64,128]{2,1,0:T(8,128)(2,1)S(1)} %get-tuple-element.16.refs_0_), channel_id=1, source_target_pairs={{2,0},{0,2},{3,1},{1,3},{6,4},{4,6},{7,5},{5,7},{10,8},{8,10},{11,... | collective-permute-start | bytes 786440 | tf_op jit(solution)/shard_map/ppermute | solution.py:49
  27.2 2.6 %collective-permute-start.10 = (bf16[2,64,128]{2,1,0:T(8,128)(2,1)S(1)}, bf16[2,64,128]{2,1,0:T(8,128)(2,1)S(1)}, u32[]{:S(2)}, u32[]{:S(2)}) collective-permute-start(bf16[2,64,128]{2,1,0:T(8,128)(2,1)S(1)} %get-tuple-element.14), channel_id=1, source_target_pairs={{0,1},{2,3},{4,5},{6,7},{8,9},{10,11},{12,13},{14,15},{1,0},{3,2},... | collective-permute-start | bytes 98312 | tf_op jit(solution)/shard_map/ppermute | solution.py:44
  29.8 0.7 %collective-permute-start.11 = (bf16[2,64,128]{2,1,0:T(8,128)(2,1)S(1)}, bf16[2,64,128]{2,1,0:T(8,128)(2,1)S(1)}, u32[]{:S(2)}, u32[]{:S(2)}) collective-permute-start(bf16[2,64,128]{2,1,0:T(8,128)(2,1)S(1)} %get-tuple-element.15), channel_id=1, source_target_pairs={{1,4},{3,6},{5,8},{7,10},{9,12},{11,14},{4,1},{6,3},{8,5},{10,7},{... | collective-permute-start | bytes 98312 | tf_op jit(solution)/shard_map/ppermute | solution.py:44
  30.4 2.8 %own_second.2.refs_2_ = f32[16,64,128]{2,1,0:T(8,128)S(1)} custom-call(s32[1,24]{1,0:T(1,128)S(1)} %pad_add_fusion.ints, s32[16,27]{1,0:T(8,128)S(1)} %copy-done.3, bf16[27,128,256]{2,1,0:T(8,128)(2,1)S(1)} %copy-done.1, bf16[16,64,128]{2,1,0:T(8,128)(2,1)S(1)} %get-tuple-element.16.refs_0_), custom_call_target="tpu_custom_call" | custom-call | flops 1811939328 | tf_op jit(solution)/shard_map/own_second/pallas_call | solution.py:307
  33.3 1.2 %collective-permute-start.13 = (bf16[4,64,128]{2,1,0:T(8,128)(2,1)S(1)}, bf16[4,64,128]{2,1,0:T(8,128)(2,1)S(1)}, u32[]{:S(2)}, u32[]{:S(2)}) collective-permute-start(bf16[4,64,128]{2,1,0:T(8,128)(2,1)S(1)} %pack.1), channel_id=1, source_target_pairs={{2,0},{0,2},{3,1},{1,3},{6,4},{4,6},{7,5},{5,7},{10,8},{8,10},{11,... | collective-permute-start | bytes 196616 | tf_op jit(solution)/shard_map/ppermute | solution.py:49
  34.5 2.8 %own_second.3.refs_3_ = f32[16,64,128]{2,1,0:T(8,128)S(1)} custom-call(s32[1,24]{1,0:T(1,128)S(1)} %pad_add_fusion.ints, s32[16,27]{1,0:T(8,128)S(1)} %copy-done.3, bf16[27,128,256]{2,1,0:T(8,128)(2,1)S(1)} %copy-done.1, bf16[16,64,128]{2,1,0:T(8,128)(2,1)S(1)} %collective-permute-done.12.refs_0_), custom_call_target="tpu_custom_call" | custom-call | flops 1811939328 | tf_op jit(solution)/shard_map/own_second/pallas_call | solution.py:307
  37.3 0.3 collective-permute-done.13.refs_4_
  37.7 2.7 %rim_second.1 = bf16[16,32,128]{2,1,0:T(8,128)(2,1)S(1)} custom-call(s32[1,24]{1,0:T(1,128)S(1)} %pad_add_fusion.ints, s32[16,27]{1,0:T(8,128)S(1)} %get-tuple-element.28.table, f32[6,128]{1,0:T(8,128)S(1)} %stack.54.vectors, bf16[16,64,256]{2,1,0:T(8,128)(2,1)S(1)} %get-tuple-element.11.rows, bf16[27,128,256]{2,1,0:T(8,128)(2,1)S(1)} %copy-done.1, ...), custom_call_target="tpu_custom_call" | custom-call | flops 905969664 | tf_op jit(solution)/shard_map/rim_second/pallas_call | solution.py:375
  40.3 13.8 %all_to_all.5.parts = bf16[16,32,128]{2,1,0:T(8,128)(2,1)S(1)} all-to-all(bf16[16,32,128]{2,1,0:T(8,128)(2,1)S(1)} %rim_second.1), channel_id=1, replica_groups=mesh['groups'=2,'brick'=4,'chan'=2,'sub'=2] {'brick','chan','sub'}, dimensions={0} | all-to-all | bytes 262144 | tf_op jit(solution)/shard_map/all_to_all | solution.py:511
  54.1 0.7 %arrived_tiles.1 = bf16[1,128,256]{2,1,0:T(8,128)(2,1)} custom-call(f32[6,128]{1,0:T(8,128)S(1)} %stack.54.vectors, bf16[16,32,128]{2,1,0:T(8,128)(2,1)S(1)} %all_to_all.5.parts), custom_call_target="tpu_custom_call" | custom-call | tf_op jit(solution)/shard_map/arrived_tiles/pallas_call | solution.py:405
  (45 shorter events, 0.3 us)
Async XLA Ops:
  0.0 1.0 %copy-start = (bf16[512,256]{1,0:T(8,128)(2,1)S(1)}, bf16[512,256]{1,0:T(8,128)(2,1)}, u32[]{:S(2)}) copy-start(bf16[512,256]{1,0:T(8,128)(2,1)} %param.14) | copy-start | bytes 786436
  0.0 3.5 %copy-start.3 = (s32[16,27]{1,0:T(8,128)S(1)}, s32[16,27]{1,0:T(8,128)}, u32[]{:S(2)}) copy-start(s32[16,27]{1,0:T(8,128)} %table.3) | copy-start | bytes 5188
  0.0 3.6 %copy-start.10 = (f32[128]{0:T(128)S(1)}, f32[128]{0:T(128)}, u32[]{:S(2)}) copy-start(f32[128]{0:T(128)} %param.27) | copy-start | bytes 1540
  0.0 3.6 %copy-start.9 = (f32[128]{0:T(128)S(1)}, f32[128]{0:T(128)}, u32[]{:S(2)}) copy-start(f32[128]{0:T(128)} %param.26) | copy-start | bytes 1540
  0.0 3.6 %copy-start.8 = (f32[128]{0:T(128)S(1)}, f32[128]{0:T(128)}, u32[]{:S(2)}) copy-start(f32[128]{0:T(128)} %param.25) | copy-start | bytes 1540
  0.0 3.6 %copy-start.7 = (f32[128]{0:T(128)S(1)}, f32[128]{0:T(128)}, u32[]{:S(2)}) copy-start(f32[128]{0:T(128)} %param.24) | copy-start | bytes 1540
  0.0 3.6 %copy-start.6 = (f32[128]{0:T(128)S(1)}, f32[128]{0:T(128)}, u32[]{:S(2)}) copy-start(f32[128]{0:T(128)} %param.23) | copy-start | bytes 1540
  0.0 3.6 %copy-start.5 = (f32[128]{0:T(128)S(1)}, f32[128]{0:T(128)}, u32[]{:S(2)}) copy-start(f32[128]{0:T(128)} %param.22) | copy-start | bytes 1540
  0.1 3.6 %copy-start.11 = (s32[16,1]{0,1:T(1,128)S(1)}, s32[16,1]{0,1:T(1,128)}, u32[]{:S(2)}) copy-start(s32[16,1]{0,1:T(1,128)} %param.18) | copy-start | bytes 196
  0.1 16.8 %copy-start.4 = (bf16[27,128,256]{2,1,0:T(8,128)(2,1)S(1)}, bf16[27,128,256]{2,1,0:T(8,128)(2,1)}, u32[]{:S(2)}) copy-start(bf16[27,128,256]{2,1,0:T(8,128)(2,1)} %weight.8) | copy-start | bytes 5308420
  2.1 1.6 %collective-permute-start = (bf16[4,64,256]{2,1,0:T(8,128)(2,1)S(1)}, bf16[4,64,256]{2,1,0:T(8,128)(2,1)S(1)}, u32[]{:S(2)}, u32[]{:S(2)}) collective-permute-start(bf16[4,64,256]{2,1,0:T(8,128)(2,1)S(1)} %fusion.1), channel_id=1, source_target_pairs={{0,1},{1,0},{2,3},{3,2},{4,5},{5,4},{6,7},{7,6},{8,9},{9,8},{10,11... | collective-permute-start | bytes 393224 | tf_op jit(solution)/shard_map/ppermute | solution.py:54
  3.8 7.6 %collective-permute-start.1 = (bf16[2,64,256]{2,1,0:T(8,128)(2,1)S(1)}, bf16[2,64,256]{2,1,0:T(8,128)(2,1)S(1)}, u32[]{:S(2)}, u32[]{:S(2)}) collective-permute-start(bf16[2,64,256]{2,1,0:T(8,128)(2,1)S(1)} %pad_maximum_fusion.1), channel_id=1, source_target_pairs={{0,4},{4,8},{8,12},{12,0},{1,5},{5,9},{9,13},{13,1},{2,6},{6,10},{... | collective-permute-start | bytes 196616 | tf_op jit(solution)/shard_map/ppermute | solution.py:54
  6.6 6.2 %collective-permute-start.2 = (bf16[2,64,256]{2,1,0:T(8,128)(2,1)S(1)}, bf16[2,64,256]{2,1,0:T(8,128)(2,1)S(1)}, u32[]{:S(2)}, u32[]{:S(2)}) collective-permute-start(bf16[2,64,256]{2,1,0:T(8,128)(2,1)S(1)} %pad_maximum_fusion.2), channel_id=1, source_target_pairs={{0,12},{4,0},{8,4},{12,8},{1,13},{5,1},{9,5},{13,9},{2,14},{6,2},{... | collective-permute-start | bytes 196616 | tf_op jit(solution)/shard_map/ppermute | solution.py:54
  8.7 6.6 %collective-permute-start.3 = (bf16[2,64,256]{2,1,0:T(8,128)(2,1)S(1)}, bf16[2,64,256]{2,1,0:T(8,128)(2,1)S(1)}, u32[]{:S(2)}, u32[]{:S(2)}) collective-permute-start(bf16[2,64,256]{2,1,0:T(8,128)(2,1)S(1)} %pad_maximum_fusion.3), channel_id=1, source_target_pairs={{0,8},{4,12},{8,0},{12,4},{1,9},{5,13},{9,1},{13,5},{2,10},{6,14},... | collective-permute-start | bytes 196616 | tf_op jit(solution)/shard_map/ppermute | solution.py:54
  9.8 9.5 %collective-permute-start.4 = (bf16[2,64,256]{2,1,0:T(8,128)(2,1)S(1)}, bf16[2,64,256]{2,1,0:T(8,128)(2,1)S(1)}, u32[]{:S(2)}, u32[]{:S(2)}) collective-permute-start(bf16[2,64,256]{2,1,0:T(8,128)(2,1)S(1)} %pad_maximum_fusion.refs_0_), channel_id=1, source_target_pairs={{2,0},{0,2},{3,1},{1,3},{6,4},{4,6},{7,5},{5,7},{10,8},{8,10},{11,... | collective-permute-start | bytes 196616 | tf_op jit(solution)/shard_map/ppermute | solution.py:49
  11.4 8.0 %collective-permute-start.5 = (bf16[2,64,256]{2,1,0:T(8,128)(2,1)S(1)}, bf16[2,64,256]{2,1,0:T(8,128)(2,1)S(1)}, u32[]{:S(2)}, u32[]{:S(2)}) collective-permute-start(bf16[2,64,256]{2,1,0:T(8,128)(2,1)S(1)} %collective-permute-done.1.refs_1_), channel_id=1, source_target_pairs={{2,0},{0,2},{3,1},{1,3},{6,4},{4,6},{7,5},{5,7},{10,8},{8,10},{11,... | collective-permute-start | bytes 196616 | tf_op jit(solution)/shard_map/ppermute | solution.py:49
  12.8 6.5 %collective-permute-start.6 = (bf16[2,64,256]{2,1,0:T(8,128)(2,1)S(1)}, bf16[2,64,256]{2,1,0:T(8,128)(2,1)S(1)}, u32[]{:S(2)}, u32[]{:S(2)}) collective-permute-start(bf16[2,64,256]{2,1,0:T(8,128)(2,1)S(1)} %collective-permute-done.2.refs_2_), channel_id=1, source_target_pairs={{2,0},{0,2},{3,1},{1,3},{6,4},{4,6},{7,5},{5,7},{10,8},{8,10},{11,... | collective-permute-start | bytes 196616 | tf_op jit(solution)/shard_map/ppermute | solution.py:49
  15.4 4.3 %collective-permute-start.7 = (bf16[2,64,256]{2,1,0:T(8,128)(2,1)S(1)}, bf16[2,64,256]{2,1,0:T(8,128)(2,1)S(1)}, u32[]{:S(2)}, u32[]{:S(2)}) collective-permute-start(bf16[2,64,256]{2,1,0:T(8,128)(2,1)S(1)} %collective-permute-done.3.refs_3_), channel_id=1, source_target_pairs={{2,0},{0,2},{3,1},{1,3},{6,4},{4,6},{7,5},{5,7},{10,8},{8,10},{11,... | collective-permute-start | bytes 196616 | tf_op jit(solution)/shard_map/ppermute | solution.py:49
  20.3 3.3 %collective-permute-start.8 = (bf16[2,64,256]{2,1,0:T(8,128)(2,1)S(1)}, bf16[2,64,256]{2,1,0:T(8,128)(2,1)S(1)}, u32[]{:S(2)}, u32[]{:S(2)}) collective-permute-start(bf16[2,64,256]{2,1,0:T(8,128)(2,1)S(1)} %get-tuple-element.12), channel_id=1, source_target_pairs={{0,1},{2,3},{4,5},{6,7},{8,9},{10,11},{12,13},{14,15},{1,0},{3,2},... | collective-permute-start | bytes 196616 | tf_op jit(solution)/shard_map/ppermute | solution.py:44
  20.3 3.2 %collective-permute-start.9 = (bf16[2,64,256]{2,1,0:T(8,128)(2,1)S(1)}, bf16[2,64,256]{2,1,0:T(8,128)(2,1)S(1)}, u32[]{:S(2)}, u32[]{:S(2)}) collective-permute-start(bf16[2,64,256]{2,1,0:T(8,128)(2,1)S(1)} %get-tuple-element.13), channel_id=1, source_target_pairs={{1,4},{3,6},{5,8},{7,10},{9,12},{11,14},{4,1},{6,3},{8,5},{10,7},{... | collective-permute-start | bytes 196616 | tf_op jit(solution)/shard_map/ppermute | solution.py:44
  23.5 6.9 %copy-start.1 = (bf16[27,128,256]{2,1,0:T(8,128)(2,1)S(1)}, bf16[27,128,256]{2,1,0:T(8,128)(2,1)}, u32[]{:S(2)}) copy-start(bf16[27,128,256]{2,1,0:T(8,128)(2,1)} %weight.11) | copy-start | bytes 5308420
  25.6 7.7 %collective-permute-start.12 = (bf16[16,64,128]{2,1,0:T(8,128)(2,1)S(1)}, bf16[16,64,128]{2,1,0:T(8,128)(2,1)S(1)}, u32[]{:S(2)}, u32[]{:S(2)}) collective-permute-start(bf16[16,64,128]{2,1,0:T(8,128)(2,1)S(1)} %get-tuple-element.16.refs_0_), channel_id=1, source_target_pairs={{2,0},{0,2},{3,1},{1,3},{6,4},{4,6},{7,5},{5,7},{10,8},{8,10},{11,... | collective-permute-start | bytes 786440 | tf_op jit(solution)/shard_map/ppermute | solution.py:49
  27.2 6.1 %collective-permute-start.10 = (bf16[2,64,128]{2,1,0:T(8,128)(2,1)S(1)}, bf16[2,64,128]{2,1,0:T(8,128)(2,1)S(1)}, u32[]{:S(2)}, u32[]{:S(2)}) collective-permute-start(bf16[2,64,128]{2,1,0:T(8,128)(2,1)S(1)} %get-tuple-element.14), channel_id=1, source_target_pairs={{0,1},{2,3},{4,5},{6,7},{8,9},{10,11},{12,13},{14,15},{1,0},{3,2},... | collective-permute-start | bytes 98312 | tf_op jit(solution)/shard_map/ppermute | solution.py:44
  29.8 3.5 %collective-permute-start.11 = (bf16[2,64,128]{2,1,0:T(8,128)(2,1)S(1)}, bf16[2,64,128]{2,1,0:T(8,128)(2,1)S(1)}, u32[]{:S(2)}, u32[]{:S(2)}) collective-permute-start(bf16[2,64,128]{2,1,0:T(8,128)(2,1)S(1)} %get-tuple-element.15), channel_id=1, source_target_pairs={{1,4},{3,6},{5,8},{7,10},{9,12},{11,14},{4,1},{6,3},{8,5},{10,7},{... | collective-permute-start | bytes 98312 | tf_op jit(solution)/shard_map/ppermute | solution.py:44
  33.3 4.3 %copy-start.2 = (bf16[8,128,256]{2,1,0:T(8,128)(2,1)S(1)}, bf16[8,128,256]{2,1,0:T(8,128)(2,1)}, u32[]{:S(2)}) copy-start(bf16[8,128,256]{2,1,0:T(8,128)(2,1)} %down_weight.1) | copy-start | bytes 1572868
  33.3 4.3 %collective-permute-start.13 = (bf16[4,64,128]{2,1,0:T(8,128)(2,1)S(1)}, bf16[4,64,128]{2,1,0:T(8,128)(2,1)S(1)}, u32[]{:S(2)}, u32[]{:S(2)}) collective-permute-start(bf16[4,64,128]{2,1,0:T(8,128)(2,1)S(1)} %pack.1), channel_id=1, source_target_pairs={{2,0},{0,2},{3,1},{1,3},{6,4},{4,6},{7,5},{5,7},{10,8},{8,10},{11,... | collective-permute-start | bytes 196616 | tf_op jit(solution)/shard_map/ppermute | solution.py:49

commit v4 on v3

--- a/solution.py
+++ b/solution.py
@@ -16,20 +16,33 @@
 NT = (((1,), (1,)), ((), ()))
 NN = (((1,), (0,)), ((), ()))
 VMEM = pl.BlockSpec(memory_space=pltpu.VMEM)
-SMEM = pl.BlockSpec(memory_space=pltpu.SMEM)
 LIMIT = pltpu.CompilerParams(vmem_limit_bytes=40 * 2**20)
 
 
 class Place:
-    def __init__(self, ints, start, reach=0):
-        self.ints, self.start, self.reach = ints, start, reach
-        self.brick, self.sub, self.chan, self.parity = (ints[0, start + i] for i in range(4))
-
-    def halo(self, direction, j):
-        return self.ints[0, self.start + 4 + direction * self.reach + j]
-
-    def route(self, n):
-        return self.ints[0, self.start + 4 + 2 * self.reach + n]
+    def __init__(self):
+        self.brick, self.sub, self.chan = (lax.axis_index(a) for a in ("brick", "sub", "chan"))
+        self.parity = lax.rem(self.brick * lax.axis_size("sub") + self.sub, 2)
+
+
+class Scalars:
+    def __init__(self, given, held, semaphore):
+        self.copies = [
+            pltpu.make_async_copy(source, target, semaphore.at[i])
+            for i, (source, target) in enumerate(zip(given, held))
+        ]
+        for copy in self.copies:
+            copy.start()
+
+    def wait(self):
+        for copy in self.copies:
+            copy.wait()
+
+
+def scalar_scratch(*arrays):
+    return [pltpu.SMEM(x.shape, jnp.int32) for x in arrays] + [
+        pltpu.SemaphoreType.DMA((len(arrays),))
+    ]
 
 
 def owner_pairs(block, parity, distance=0):
@@ -60,9 +73,11 @@
     return jnp.dot(taken.astype(BF16), features, preferred_element_type=F32).astype(BF16)
 
 
-def assemble_kernel(start, reach, bricks, subs, chans, keys, ints, *refs):
-    parts, (rows, even, odd) = dict(zip(keys, refs[:-3])), refs[-3:]
-    place = Place(ints, start, reach)
+def assemble_kernel(bricks, subs, chans, keys, halo_near, *refs):
+    parts, (rows, even, odd, halo, semaphore) = dict(zip(keys, refs[:-5])), refs[-5:]
+    reach = halo.shape[1]
+    scalars = Scalars([halo_near], [halo], semaphore)
+    place = Place()
     split = BLK // parts[0, 0].shape[1]
     for (jb, j), part in parts.items():
         source = lax.rem(place.brick - jb + bricks, bricks)
@@ -70,26 +85,28 @@
         for js in range(subs):
             sub = lax.rem(place.sub + js, subs)
             rows[(source * subs + sub) * chans + chan] = part[js]
+    scalars.wait()
     for j in range(reach):
-        even[pl.ds(j * split, split)] = rows[pl.ds(place.halo(place.parity, j) * split, split)]
-        odd[pl.ds(j * split, split)] = rows[pl.ds(place.halo(1 - place.parity, j) * split, split)]
-
-
-def assemble(ints, parts, start, reach, bricks, subs, chans):
+        even[pl.ds(j * split, split)] = rows[pl.ds(halo[place.parity, j] * split, split)]
+        odd[pl.ds(j * split, split)] = rows[pl.ds(halo[1 - place.parity, j] * split, split)]
+
+
+def assemble(halo, parts, bricks, subs, chans):
     per, channels = parts[0, 0].shape[1:]
     pieces = bricks * subs * chans
     split = BLK // per
-    sent = reach * split
-    return pl.pallas_call(
-        functools.partial(assemble_kernel, start, reach, bricks, subs, chans, tuple(parts)),
+    sent = halo.shape[1] * split
+    return pl.pallas_call(
+        functools.partial(assemble_kernel, bricks, subs, chans, tuple(parts)),
         out_shape=[
             jax.ShapeDtypeStruct((count, per, channels), BF16) for count in (pieces, sent, sent)
         ],
-        in_specs=[SMEM] + [VMEM] * len(parts),
+        in_specs=[VMEM] * (1 + len(parts)),
         out_specs=[VMEM] * 3,
+        scratch_shapes=scalar_scratch(halo),
         compiler_params=LIMIT,
         name="assemble",
-    )(ints, *parts.values())
+    )(halo, *parts.values())
 
 
 def block_sums(table, blocks, weight, total):
@@ -131,7 +148,7 @@
     rim[pl.ds(reach * place.parity, reach), :, lanes] = odd[...]
 
 
-def named_sums(table, given, weight, products, total):
+def named_sums(table, scalars, given, weight, products, total):
     blocks, offsets = given.shape[0], table.shape[1]
     width, channels = weight.shape[1:]
     together = max(1, channels // width)
@@ -149,6 +166,7 @@
                 blocks, BLK, width
             )
     products[:, blocks : blocks + 1] = jnp.zeros((offsets, 1, BLK, width), F32)
+    scalars.wait()
 
     def one_block(n, carry):
         running = total[n]
@@ -167,10 +185,12 @@
     )
 
 
-def own_first_kernel(table, rows, weight, total, blocks):
+def own_first_kernel(table_near, rows, weight, total, blocks, table, semaphore):
+    scalars = Scalars([table_near], [table], semaphore)
     count = rows.shape[0]
     blocks[0:count] = rows[...]
     blocks[count] = jnp.zeros(blocks.shape[1:], BF16)
+    scalars.wait()
     block_sums(table, blocks, weight, total)
 
 
@@ -179,29 +199,30 @@
     return pl.pallas_call(
         own_first_kernel,
         out_shape=jax.ShapeDtypeStruct((count, BLK, weight.shape[1]), F32),
-        in_specs=[SMEM, VMEM, VMEM],
+        in_specs=[VMEM] * 3,
         out_specs=VMEM,
-        scratch_shapes=[pltpu.VMEM((count + 1, BLK, channels), BF16)],
+        scratch_shapes=[pltpu.VMEM((count + 1, BLK, channels), BF16)] + scalar_scratch(table),
         compiler_params=LIMIT,
         cost_estimate=cost(count, weight),
         name="own_first",
     )(table, rows, weight)
 
 
-def pieces_first_kernel(bricks, subs, behind, started, ints, table, weight, *refs):
-    parts, (total, held, products) = refs[:-3], refs[-3:]
+def pieces_first_kernel(bricks, subs, behind, started, table_near, weight, *refs):
+    parts, (total, held, products, table, semaphore) = refs[:-5], refs[-5:]
+    scalars = Scalars([table_near], [table], semaphore)
     if started:
         parts, before = parts[:-1], parts[-1]
-    place = Place(ints, 0)
+    place = Place()
     for jb, part in zip(behind, parts):
         source = lax.rem(place.brick - jb + bricks, bricks)
         for js in range(subs):
             held[source * subs + lax.rem(place.sub + js, subs)] = part[js]
     total[...] = before[...] if started else jnp.zeros(total.shape, F32)
-    named_sums(table, held, weight, products, total)
-
-
-def pieces_first(ints, table, weight, parts, before, j, bricks, subs):
+    named_sums(table, scalars, held, weight, products, total)
+
+
+def pieces_first(table, weight, parts, before, j, bricks, subs):
     offsets, width, channels = weight.shape
     sums = jax.ShapeDtypeStruct((table.shape[0], BLK, width), F32)
     held = bricks * subs
@@ -210,29 +231,32 @@
     return pl.pallas_call(
         functools.partial(pieces_first_kernel, bricks, subs, behind, before is not None),
         out_shape=sums,
-        in_specs=[SMEM, SMEM] + [VMEM] * (1 + len(given)),
+        in_specs=[VMEM] * (2 + len(given)),
         out_specs=VMEM,
         scratch_shapes=[
             pltpu.VMEM((held, BLK, channels), BF16),
             pltpu.VMEM((offsets, held + 1, BLK, width), F32),
-        ],
+        ]
+        + scalar_scratch(table),
         compiler_params=LIMIT,
         cost_estimate=cost(held, weight),
         name="pieces_first",
-    )(ints, table, weight, *given)
-
-
-def rim_first_kernel(start, ints, table, vectors, own, even, odd, weight, hidden, even_out, odd_out, rim, products, total):
-    count, reach = table.shape[0], even.shape[0]
-    place = Place(ints, start, reach)
+    )(table, weight, *given)
+
+
+def rim_first_kernel(halo_near, table_near, vectors, own, even, odd, weight, *refs):
+    hidden, even_out, odd_out, rim, products, total, halo, table, semaphore = refs
+    scalars = Scalars([halo_near, table_near], [halo, table], semaphore)
+    reach = even.shape[0]
+    place = Place()
     rim_blocks(place, even, odd, slice(None), rim)
     total[...] = own[...]
-    named_sums(table, rim, weight, products, total)
+    named_sums(table, scalars, rim, weight, products, total)
     value = total[...] * vectors[0:1][None] + vectors[1:2][None]
     hidden[...] = jnp.maximum(value, 0.0).astype(BF16)
     for j in range(reach):
-        even_out[j] = hidden[place.halo(place.parity, j)]
-        odd_out[j] = hidden[place.halo(1 - place.parity, j)]
+        even_out[j] = hidden[halo[place.parity, j]]
+        odd_out[j] = hidden[halo[1 - place.parity, j]]
 
 
 def rim_scratch(count, reach, weight):
@@ -244,20 +268,20 @@
     ]
 
 
-def rim_first(ints, table, vectors, own, even, odd, weight, start):
+def rim_first(halo, table, vectors, own, even, odd, weight):
     count, reach, width = table.shape[0], even.shape[0], weight.shape[1]
     return pl.pallas_call(
-        functools.partial(rim_first_kernel, start),
+        rim_first_kernel,
         out_shape=[
             jax.ShapeDtypeStruct((n, BLK, width), BF16) for n in (count, reach, reach)
         ],
-        in_specs=[SMEM, SMEM] + [VMEM] * 5,
+        in_specs=[VMEM] * 7,
         out_specs=[VMEM] * 3,
-        scratch_shapes=rim_scratch(count, reach, weight),
+        scratch_shapes=rim_scratch(count, reach, weight) + scalar_scratch(halo, table),
         compiler_params=LIMIT,
         cost_estimate=cost(2 * reach, weight),
         name="rim_first",
-    )(ints, table, vectors, own, even, odd, weight)
+    )(halo, table, vectors, own, even, odd, weight)
 
 
 def pack_kernel(even, odd, *refs):
@@ -277,10 +301,11 @@
     )(even, odd, *after)
 
 
-def own_second_kernel(start, nearest, chans, ints, table, weight, *refs):
-    parts, (total, blocks, beside) = refs[:-3], refs[-3:]
+def own_second_kernel(nearest, chans, table_near, weight, *refs):
+    parts, (total, blocks, beside, table, semaphore) = refs[:-5], refs[-5:]
+    scalars = Scalars([table_near], [table], semaphore)
     count, width = parts[0].shape[0], parts[0].shape[2]
-    place = Place(ints, start)
+    place = Place()
     lanes = blocks.shape[2]
     offsets = beside.shape[2] // lanes
     for i, part in enumerate(parts):
@@ -296,36 +321,39 @@
                     ]
 
     blocks[count] = jnp.zeros(blocks.shape[1:], BF16)
+    scalars.wait()
     block_sums(table, blocks, beside, total)
 
 
-def own_second(ints, table, weight, parts, start, nearest, chans):
+def own_second(table, weight, parts, nearest, chans):
     count, width = parts[0].shape[0], parts[0].shape[2]
     lanes = width * len(parts)
     offsets = max(1, weight.shape[2] // lanes)
     groups = -(-weight.shape[0] // offsets)
     return pl.pallas_call(
-        functools.partial(own_second_kernel, start, nearest, chans),
+        functools.partial(own_second_kernel, nearest, chans),
         out_shape=jax.ShapeDtypeStruct((count, BLK, width), F32),
-        in_specs=[SMEM, SMEM] + [VMEM] * (1 + len(parts)),
+        in_specs=[VMEM] * (2 + len(parts)),
         out_specs=VMEM,
         scratch_shapes=[
             pltpu.VMEM((count + 1, BLK, lanes), BF16),
             pltpu.VMEM((groups, width, lanes * offsets), BF16),
-        ],
+        ]
+        + scalar_scratch(table),
         compiler_params=LIMIT,
         cost_estimate=cost(count // 2, weight),
         name="own_second",
-    )(ints, table, weight, *parts)
-
-
-def rim_second_kernel(start, bricks, subs, chans, owns, ints, table, vectors, rows, weight, down_weight, *refs):
+    )(table, weight, *parts)
+
+
+def rim_second_kernel(bricks, subs, chans, owns, route_near, table_near, vectors, rows, weight, down_weight, *refs):
     (even, odd), refs = refs[:2], refs[2:]
     sums, refs = refs[:owns], refs[owns:]
-    fars, (out, rim, products, total, slots, seen) = refs[:-6], refs[-6:]
+    fars, (out, rim, products, total, slots, seen, route, table, semaphore) = refs[:-9], refs[-9:]
+    scalars = Scalars([route_near, table_near], [route, table], semaphore)
     count, reach = table.shape[0], even.shape[0]
     width = weight.shape[1]
-    place = Place(ints, start, reach)
+    place = Place()
     for j in range(chans):
         near = (even, odd) if j == 0 else (fars[j - 1].at[0:reach], fars[j - 1].at[reach:])
         for c in range(chans):
@@ -337,7 +365,7 @@
     total[...] = sums[0][...]
     for more in sums[1:]:
         total[...] += more[...]
-    named_sums(table, rim, weight, products, total)
+    named_sums(table, scalars, rim, weight, products, total)
     for c in range(chans):
 
         @pl.when(place.chan == c)
@@ -358,7 +386,7 @@
     for owner in range(bricks * subs):
         seen[owner] = 0
     for n in range(count):
-        owner = place.route(n)
+        owner = route[0, n]
         slot = seen[owner]
         seen[owner] = slot + 1
         device = owner // subs * (chans * subs) + lax.rem(owner, subs)
@@ -369,20 +397,21 @@
     out[...] = slots[...].astype(BF16)
 
 
-def rim_second(ints, table, vectors, rows, weight, down_weight, even, odd, sums, fars, start, bricks, subs, chans, capacity):
+def rim_second(route, table, vectors, rows, weight, down_weight, even, odd, sums, fars, bricks, subs, chans, capacity):
     count, reach, width = table.shape[0], even.shape[0], weight.shape[1]
     slots = (bricks * subs * chans, capacity * CELLS, width)
     return pl.pallas_call(
-        functools.partial(rim_second_kernel, start, bricks, subs, chans, len(sums)),
+        functools.partial(rim_second_kernel, bricks, subs, chans, len(sums)),
         out_shape=jax.ShapeDtypeStruct(slots, BF16),
-        in_specs=[SMEM, SMEM] + [VMEM] * (6 + len(sums) + len(fars)),
+        in_specs=[VMEM] * (8 + len(sums) + len(fars)),
         out_specs=VMEM,
         scratch_shapes=rim_scratch(count, reach, weight)
-        + [pltpu.VMEM(slots, F32), pltpu.SMEM((bricks * subs,), jnp.int32)],
+        + [pltpu.VMEM(slots, F32), pltpu.SMEM((bricks * subs,), jnp.int32)]
+        + scalar_scratch(route, table),
         compiler_params=LIMIT,
         cost_estimate=cost(2 * reach, weight),
         name="rim_second",
-    )(ints, table, vectors, rows, weight, down_weight, even, odd, *sums, *fars)
+    )(route, table, vectors, rows, weight, down_weight, even, odd, *sums, *fars)
 
 
 def arrive_kernel(bricks, subs, chans, vectors, parts, out):
@@ -455,19 +484,15 @@
     owners = bricks * subs
     count, reach = kernel_map.shape[0], halo_send.shape[1]
     channels = features.shape[1]
-    start = 0
-    brick, sub, chan = (lax.axis_index(axis) for axis in ("brick", "sub", "chan"))
-    place = jnp.stack([brick, sub, chan, lax.rem(brick * subs + sub, 2)]).astype(jnp.int32)
     ordered = sorted_rows(scan_order, features)
     ordered = ordered.reshape(bricks, subs, features.shape[0] // owners, channels)
     parts = to_owners(ordered, chans)
-    ints = jnp.concatenate(
-        [place[None], halo_send[0:1], halo_send[1:2], down_route.reshape(1, -1)], axis=1
-    )
+    chan = lax.axis_index("chan")
+    down_route = down_route.reshape(1, count)
     vectors = jnp.stack(
         [gain_first, bias_first, gain_second, bias_second, gain_down, bias_down]
     )
-    rows, even, odd = assemble(ints, parts, start, reach, bricks, subs, chans)
+    rows, even, odd = assemble(halo_send, parts, bricks, subs, chans)
     rows = rows.reshape(count, BLK, channels)
     even = owner_pairs(even, 0).reshape(reach, BLK, channels)
     odd = owner_pairs(odd, 1).reshape(reach, BLK, channels)
@@ -477,22 +502,20 @@
         for j in range(chans):
             here = (kernel_map < count) & (lax.rem(kernel_map, chans) == lax.rem(chan + j, chans))
             inside = jnp.where(here, lax.div(kernel_map, chans), owners)
-            own = pieces_first(ints, inside, conv1_weight, parts, own, j, bricks, subs)
+            own = pieces_first(inside, conv1_weight, parts, own, j, bricks, subs)
     else:
         own = own_first(kernel_map, rows, conv1_weight)
-    hidden, even, odd = rim_first(
-        ints, outside, vectors, own, even, odd, conv1_weight, start
-    )
+    hidden, even, odd = rim_first(halo_send, outside, vectors, own, even, odd, conv1_weight)
     others = [from_ahead(hidden, "chan", j) for j in range(1, chans)]
     even, odd = owner_pairs(even, 0), owner_pairs(odd, 1)
-    rim = pack(even, odd, others)
+    sums = [own_second(kernel_map, conv2_weight, [hidden], 0, chans)]
+    rim = pack(even, odd, sums)
     fars = [from_ahead(rim, "chan", j) for j in range(1, chans)]
-    sums = [own_second(ints, kernel_map, conv2_weight, [hidden], start, 0, chans)]
     if others:
-        sums.append(own_second(ints, kernel_map, conv2_weight, others, start, 1, chans))
+        sums.append(own_second(kernel_map, conv2_weight, others, 1, chans))
     capacity = max(2, 2 * count // owners)
     partial = rim_second(
-        ints,
+        down_route,
         outside,
         vectors,
         rows,
@@ -502,7 +525,6 @@
         odd,
         sums,
         fars,
-        start,
         bricks,
         subs,
         chans,

time: 55.1 us -> 52.8 us (0.958)
  Pallas kernels: 16.7 us -> 14.1 us
  waiting for transfers between devices: 2.5 us -> 4.5 us
  blocking collectives: 13.8 us -> 13 us
  local copies, waits for them, and re-layouts: 1.74 us -> 1 us
    pallas_call x5, Pallas kernels: 11 us -> 9.44 us  [the longest x2 5.33 us: own_second(): pl.pallas_call(functools.partial(own_second_kernel, nearest, chans), out_...]
    ppermute x6, waiting for transfers between devices: 0.65 us -> 1.86 us  [from_ahead(): lax.ppermute(block, axis, [((i + distance) % n, i) for i in range(n)])]
    pallas_call x2, Pallas kernels: 4.93 us -> 3.87 us  [pieces_first(): pl.pallas_call(functools.partial(pieces_first_kernel, bricks, subs, behin...]
    all_to_all x1, blocking collectives: 13.8 us -> 13 us  [body(): lax.all_to_all(partial, ('brick', 'chan', 'sub'), split_axis=0, concat_ax...]
    ppermute x4, waiting for transfers between devices: 1.83 us -> 2.63 us  [to_ahead(): lax.ppermute(block, axis, [(i, (i + distance) % n) for i in range(n)])]
    slice x1 -> x0, local copies, waits for them, and re-layouts: 0.76 us -> none  [body(): halo_send[0:1]]
    ppermute x6, starting transfers between devices: 7.96 us -> 7.29 us  [from_ahead(): lax.ppermute(block, axis, [((i + distance) % n, i) for i in range(n)])]
    ppermute x4, starting transfers between devices: 3.97 us -> 4.52 us  [owner_pairs(): return lax.ppermute(block, ('brick', 'chan', 'sub'), route)]
  transfers between devices with their start and end apart: 14 -> 14, of which waited for: 3 -> 4; matrix products, arithmetic and copies ran while one was open for 2% -> 0% of each run, Pallas kernels for 19% -> 17%
where the time goes in v4:
time: 52.8 us; the launch traced here: 52.6 us
  starting transfers between devices  18.5 us (35%)
  Pallas kernels  14.1 us (27%)
  blocking collectives  13 us (25%)
  waiting for transfers between devices  4.5 us (9%)
  matrix products  1.04 us (2%)
  local copies, waits for them, and re-layouts  1 us (2%)
    all_to_all x1, blocking collectives, body(): lax.all_to_all(partial, ('brick', 'chan', 'sub'), split_axis=0, concat_ax...  13 us
    ppermute x6, starting transfers between devices, from_ahead(): lax.ppermute(block, axis, [((i + distance) % n, i) for i in range(n)])  7.29 us
    ppermute x4, starting transfers between devices, to_ahead(): lax.ppermute(block, axis, [(i, (i + distance) % n) for i in range(n)])  6.65 us
    pallas_call x2, Pallas kernels, own_second(): pl.pallas_call(functools.partial(own_second_kernel, nearest, chans), out_...  5.33 us
    ppermute x4, starting transfers between devices, owner_pairs(): return lax.ppermute(block, ('brick', 'chan', 'sub'), route)  4.52 us
    pallas_call x2, Pallas kernels, pieces_first(): pl.pallas_call(functools.partial(pieces_first_kernel, bricks, subs, behin...  3.87 us
    ppermute x4, waiting for transfers between devices, to_ahead(): lax.ppermute(block, axis, [(i, (i + distance) % n) for i in range(n)])  2.63 us
    pallas_call x1, Pallas kernels, rim_second(): pl.pallas_call(functools.partial(rim_second_kernel, bricks, subs, chans,...  2.07 us
  transfers between devices with their start and end apart: 14, of which 4 were waited for; matrix products, arithmetic and copies ran while one was open for 0% of the time, Pallas kernels for 17%

profile of v4, /device:TPU:0, one launch (start us, length us, event | category | flops | bytes accessed | tf_op | source)
XLA Modules:
  0.0 52.6 jit_solution(15464353693125433104)
XLA Ops:
  0.1 0.9 %copy-done = bf16[512,256]{1,0:T(8,128)(2,1)S(1)} copy-done((bf16[512,256]{1,0:T(8,128)(2,1)S(1)}, bf16[512,256]{1,0:T(8,128)(2,1)}, u32[]{:S(2)}) %copy-start) | copy-done | bytes 262168
  1.0 1.0 %convolution_convert_fusion = bf16[512,256]{1,0:T(8,128)(2,1)S(1)} fusion(bf16[512,256]{1,0:T(8,128)(2,1)S(1)} %copy-done, s32[512]{0:T(512)} %bitcast.26), kind=kOutput, calls=%fused_computation | convolution fusion | flops 134610944 | bytes 526336 | tf_op jit(solution)/shard_map/dot_general | solution.py:73
  2.0 0.1 fusion.1
  2.1 0.5 collective-permute-start
  2.6 0.1 fusion.2
  2.8 0.8 %collective-permute-done = bf16[4,64,256]{2,1,0:T(8,128)(2,1)S(1)} collective-permute-done((bf16[4,64,256]{2,1,0:T(8,128)(2,1)S(1)}, bf16[4,64,256]{2,1,0:T(8,128)(2,1)S(1)}, u32[]{:S(2)}, u32[]{:S(2)}) %collective-permute-start) | collective-permute-done | bytes 131104 | tf_op jit(solution)/shard_map/ppermute | solution.py:67
  3.6 3.0 %collective-permute-start.1 = (bf16[2,64,256]{2,1,0:T(8,128)(2,1)S(1)}, bf16[2,64,256]{2,1,0:T(8,128)(2,1)S(1)}, u32[]{:S(2)}, u32[]{:S(2)}) collective-permute-start(bf16[2,64,256]{2,1,0:T(8,128)(2,1)S(1)} %pad_maximum_fusion.1), channel_id=1, source_target_pairs={{0,4},{4,8},{8,12},{12,0},{1,5},{5,9},{9,13},{13,1},{2,6},{6,10},{... | collective-permute-start | bytes 196616 | tf_op jit(solution)/shard_map/ppermute | solution.py:67
  6.6 2.1 %collective-permute-start.2 = (bf16[2,64,256]{2,1,0:T(8,128)(2,1)S(1)}, bf16[2,64,256]{2,1,0:T(8,128)(2,1)S(1)}, u32[]{:S(2)}, u32[]{:S(2)}) collective-permute-start(bf16[2,64,256]{2,1,0:T(8,128)(2,1)S(1)} %pad_maximum_fusion.2), channel_id=1, source_target_pairs={{0,12},{4,0},{8,4},{12,8},{1,13},{5,1},{9,5},{13,9},{2,14},{6,2},{... | collective-permute-start | bytes 196616 | tf_op jit(solution)/shard_map/ppermute | solution.py:67
  8.7 1.0 %collective-permute-start.3 = (bf16[2,64,256]{2,1,0:T(8,128)(2,1)S(1)}, bf16[2,64,256]{2,1,0:T(8,128)(2,1)S(1)}, u32[]{:S(2)}, u32[]{:S(2)}) collective-permute-start(bf16[2,64,256]{2,1,0:T(8,128)(2,1)S(1)} %pad_maximum_fusion.3), channel_id=1, source_target_pairs={{0,8},{4,12},{8,0},{12,4},{1,9},{5,13},{9,1},{13,5},{2,10},{6,14},... | collective-permute-start | bytes 196616 | tf_op jit(solution)/shard_map/ppermute | solution.py:67
  9.8 1.6 %collective-permute-start.4 = (bf16[2,64,256]{2,1,0:T(8,128)(2,1)S(1)}, bf16[2,64,256]{2,1,0:T(8,128)(2,1)S(1)}, u32[]{:S(2)}, u32[]{:S(2)}) collective-permute-start(bf16[2,64,256]{2,1,0:T(8,128)(2,1)S(1)} %pad_maximum_fusion.refs_0_), channel_id=1, source_target_pairs={{2,0},{0,2},{3,1},{1,3},{6,4},{4,6},{7,5},{5,7},{10,8},{8,10},{11,... | collective-permute-start | bytes 196616 | tf_op jit(solution)/shard_map/ppermute | solution.py:62
  11.4 1.4 %collective-permute-start.5 = (bf16[2,64,256]{2,1,0:T(8,128)(2,1)S(1)}, bf16[2,64,256]{2,1,0:T(8,128)(2,1)S(1)}, u32[]{:S(2)}, u32[]{:S(2)}) collective-permute-start(bf16[2,64,256]{2,1,0:T(8,128)(2,1)S(1)} %collective-permute-done.1.refs_1_), channel_id=1, source_target_pairs={{2,0},{0,2},{3,1},{1,3},{6,4},{4,6},{7,5},{5,7},{10,8},{8,10},{11,... | collective-permute-start | bytes 196616 | tf_op jit(solution)/shard_map/ppermute | solution.py:62
  12.7 0.7 %collective-permute-start.6 = (bf16[2,64,256]{2,1,0:T(8,128)(2,1)S(1)}, bf16[2,64,256]{2,1,0:T(8,128)(2,1)S(1)}, u32[]{:S(2)}, u32[]{:S(2)}) collective-permute-start(bf16[2,64,256]{2,1,0:T(8,128)(2,1)S(1)} %collective-permute-done.2.refs_2_), channel_id=1, source_target_pairs={{2,0},{0,2},{3,1},{1,3},{6,4},{4,6},{7,5},{5,7},{10,8},{8,10},{11,... | collective-permute-start | bytes 196616 | tf_op jit(solution)/shard_map/ppermute | solution.py:62
  13.4 1.8 %collective-permute-done.3.refs_3_ = bf16[2,64,256]{2,1,0:T(8,128)(2,1)S(1)} collective-permute-done((bf16[2,64,256]{2,1,0:T(8,128)(2,1)S(1)}, bf16[2,64,256]{2,1,0:T(8,128)(2,1)S(1)}, u32[]{:S(2)}, u32[]{:S(2)}) %collective-permute-start.3) | collective-permute-done | bytes 65568 | tf_op jit(solution)/shard_map/ppermute | solution.py:67
  15.3 1.5 %collective-permute-start.7 = (bf16[2,64,256]{2,1,0:T(8,128)(2,1)S(1)}, bf16[2,64,256]{2,1,0:T(8,128)(2,1)S(1)}, u32[]{:S(2)}, u32[]{:S(2)}) collective-permute-start(bf16[2,64,256]{2,1,0:T(8,128)(2,1)S(1)} %collective-permute-done.3.refs_3_), channel_id=1, source_target_pairs={{2,0},{0,2},{3,1},{1,3},{6,4},{4,6},{7,5},{5,7},{10,8},{8,10},{11,... | collective-permute-start | bytes 196616 | tf_op jit(solution)/shard_map/ppermute | solution.py:62
  16.8 1.9 %pieces_first.2.refs_4_ = f32[16,64,128]{2,1,0:T(8,128)S(1)} custom-call(s32[16,27]{1,0:T(8,128)S(1)} %get-tuple-element.27.table_near, bf16[27,128,256]{2,1,0:T(8,128)(2,1)S(1)} %copy-done.6, bf16[2,64,256]{2,1,0:T(8,128)(2,1)S(1)} %pad_maximum_fusion.refs_0_, bf16[2,64,256]{2,1,0:T(8,128)(2,1)S(1)} %collective-permute-done.1.refs_1_, ...), custom_call_target="tpu_custom_call" | custom-call | flops 1811939328 | tf_op jit(solution)/shard_map/pieces_first/pallas_call | solution.py:231
  18.7 0.8 %collective-permute-done.7.refs_7_.refs_3_ = bf16[2,64,256]{2,1,0:T(8,128)(2,1)S(1)} collective-permute-done((bf16[2,64,256]{2,1,0:T(8,128)(2,1)S(1)}, bf16[2,64,256]{2,1,0:T(8,128)(2,1)S(1)}, u32[]{:S(2)}, u32[]{:S(2)}) %collective-permute-start.7) | collective-permute-done | bytes 65568 | tf_op jit(solution)/shard_map/ppermute | solution.py:62
  19.5 0.6 %assemble.1 = (bf16[16,64,256]{2,1,0:T(8,128)(2,1)S(1)}, bf16[2,64,256]{2,1,0:T(8,128)(2,1)S(1)}, bf16[2,64,256]{2,1,0:T(8,128)(2,1)S(1)}) custom-call(s32[2,2]{1,0:T(2,128)S(1)} %copy-done.4, bf16[2,64,256]{2,1,0:T(8,128)(2,1)S(1)} %pad_maximum_fusion.refs_0_, bf16[2,64,256]{2,1,0:T(8,128)(2,1)S(1)} %collective-permute-done.1.refs_1_, ...), custom_call_target="tpu_custom_call" | custom-call | tf_op jit(solution)/shard_map/assemble/pallas_call | solution.py:99
  20.1 0.1 collective-permute-start.8
  20.2 0.7 %collective-permute-start.9 = (bf16[2,64,256]{2,1,0:T(8,128)(2,1)S(1)}, bf16[2,64,256]{2,1,0:T(8,128)(2,1)S(1)}, u32[]{:S(2)}, u32[]{:S(2)}) collective-permute-start(bf16[2,64,256]{2,1,0:T(8,128)(2,1)S(1)} %get-tuple-element.13), channel_id=1, source_target_pairs={{1,4},{3,6},{5,8},{7,10},{9,12},{11,14},{4,1},{6,3},{8,5},{10,7},{... | collective-permute-start | bytes 196616 | tf_op jit(solution)/shard_map/ppermute | solution.py:57
  20.9 1.9 %pieces_first.3.own = f32[16,64,128]{2,1,0:T(8,128)S(1)} custom-call(s32[16,27]{1,0:T(8,128)S(1)} %get-tuple-element.29.table_near, bf16[27,128,256]{2,1,0:T(8,128)(2,1)S(1)} %copy-done.6, bf16[2,64,256]{2,1,0:T(8,128)(2,1)S(1)} %collective-permute-done.4.refs_4_.refs_0_, bf16[2,64,256]{2,1,0:T(8,128)(2,1)S(1)} %collective-permute-done.5.refs_5_.refs_1_, ...), custom_call_target="tpu_custom_call" | custom-call | flops 1811939328 | tf_op jit(solution)/shard_map/pieces_first/pallas_call | solution.py:231
  22.8 1.5 %rim_first.1 = (bf16[16,64,128]{2,1,0:T(8,128)(2,1)S(1)}, bf16[2,64,128]{2,1,0:T(8,128)(2,1)S(1)}, bf16[2,64,128]{2,1,0:T(8,128)(2,1)S(1)}) custom-call(s32[2,2]{1,0:T(2,128)S(1)} %copy-done.4, s32[16,27]{1,0:T(8,128)S(1)} %get-tuple-element.28.table_near, f32[6,128]{1,0:T(8,128)S(1)} %stack.39.vectors, f32[16,64,128]{2,1,0:T(8,128)S(1)} %pieces_first.3.own, ...), custom_call_target="tpu_custom_call" | custom-call | flops 905969664 | tf_op jit(solution)/shard_map/rim_first/pallas_call | solution.py:273
  24.3 1.6 %collective-permute-start.12 = (bf16[16,64,128]{2,1,0:T(8,128)(2,1)S(1)}, bf16[16,64,128]{2,1,0:T(8,128)(2,1)S(1)}, u32[]{:S(2)}, u32[]{:S(2)}) collective-permute-start(bf16[16,64,128]{2,1,0:T(8,128)(2,1)S(1)} %get-tuple-element.16.refs_0_), channel_id=1, source_target_pairs={{2,0},{0,2},{3,1},{1,3},{6,4},{4,6},{7,5},{5,7},{10,8},{8,10},{11,... | collective-permute-start | bytes 786440 | tf_op jit(solution)/shard_map/ppermute | solution.py:62
  25.9 3.1 %collective-permute-start.10 = (bf16[2,64,128]{2,1,0:T(8,128)(2,1)S(1)}, bf16[2,64,128]{2,1,0:T(8,128)(2,1)S(1)}, u32[]{:S(2)}, u32[]{:S(2)}) collective-permute-start(bf16[2,64,128]{2,1,0:T(8,128)(2,1)S(1)} %get-tuple-element.14), channel_id=1, source_target_pairs={{0,1},{2,3},{4,5},{6,7},{8,9},{10,11},{12,13},{14,15},{1,0},{3,2},... | collective-permute-start | bytes 98312 | tf_op jit(solution)/shard_map/ppermute | solution.py:57
  29.0 0.7 %collective-permute-start.11 = (bf16[2,64,128]{2,1,0:T(8,128)(2,1)S(1)}, bf16[2,64,128]{2,1,0:T(8,128)(2,1)S(1)}, u32[]{:S(2)}, u32[]{:S(2)}) collective-permute-start(bf16[2,64,128]{2,1,0:T(8,128)(2,1)S(1)} %get-tuple-element.15), channel_id=1, source_target_pairs={{1,4},{3,6},{5,8},{7,10},{9,12},{11,14},{4,1},{6,3},{8,5},{10,7},{... | collective-permute-start | bytes 98312 | tf_op jit(solution)/shard_map/ppermute | solution.py:57
  29.7 2.7 %own_second.2.refs_0_.refs_2_ = f32[16,64,128]{2,1,0:T(8,128)S(1)} custom-call(s32[16,27]{1,0:T(8,128)S(1)} %copy-done.3, bf16[27,128,256]{2,1,0:T(8,128)(2,1)S(1)} %copy-done.1, bf16[16,64,128]{2,1,0:T(8,128)(2,1)S(1)} %get-tuple-element.16.refs_0_), custom_call_target="tpu_custom_call" | custom-call | flops 1811939328 | tf_op jit(solution)/shard_map/own_second/pallas_call | solution.py:333
  32.4 0.0 copy-start.5
  32.4 0.6 %collective-permute-start.13 = (bf16[4,64,128]{2,1,0:T(8,128)(2,1)S(1)}, bf16[4,64,128]{2,1,0:T(8,128)(2,1)S(1)}, u32[]{:S(2)}, u32[]{:S(2)}) collective-permute-start(bf16[4,64,128]{2,1,0:T(8,128)(2,1)S(1)} %pack.1), channel_id=1, source_target_pairs={{2,0},{0,2},{3,1},{1,3},{6,4},{4,6},{7,5},{5,7},{10,8},{8,10},{11,... | collective-permute-start | bytes 196616 | tf_op jit(solution)/shard_map/ppermute | solution.py:62
  33.0 2.7 %own_second.3.refs_3_ = f32[16,64,128]{2,1,0:T(8,128)S(1)} custom-call(s32[16,27]{1,0:T(8,128)S(1)} %copy-done.3, bf16[27,128,256]{2,1,0:T(8,128)(2,1)S(1)} %copy-done.1, bf16[16,64,128]{2,1,0:T(8,128)(2,1)S(1)} %collective-permute-done.12.refs_0_), custom_call_target="tpu_custom_call" | custom-call | flops 1811939328 | tf_op jit(solution)/shard_map/own_second/pallas_call | solution.py:333
  35.7 1.1 %collective-permute-done.13.refs_4_ = bf16[4,64,128]{2,1,0:T(8,128)(2,1)S(1)} collective-permute-done((bf16[4,64,128]{2,1,0:T(8,128)(2,1)S(1)}, bf16[4,64,128]{2,1,0:T(8,128)(2,1)S(1)}, u32[]{:S(2)}, u32[]{:S(2)}) %collective-permute-start.13) | collective-permute-done | bytes 65568 | tf_op jit(solution)/shard_map/ppermute | solution.py:62
  36.8 2.1 %rim_second.1 = bf16[16,32,128]{2,1,0:T(8,128)(2,1)S(1)} custom-call(s32[1,16]{1,0:T(1,128)S(1)} %bitcast.18, s32[16,27]{1,0:T(8,128)S(1)} %get-tuple-element.28.table_near, f32[6,128]{1,0:T(8,128)S(1)} %stack.39.vectors, bf16[16,64,256]{2,1,0:T(8,128)(2,1)S(1)} %get-tuple-element.11.rows, bf16[27,128,256]{2,1,0:T(8,128)(2,1)S(1)} %copy-done.1, ...), custom_call_target="tpu_custom_call" | custom-call | flops 905969664 | tf_op jit(solution)/shard_map/rim_second/pallas_call | solution.py:403
  38.8 13.0 %all_to_all.5.parts = bf16[16,32,128]{2,1,0:T(8,128)(2,1)S(1)} all-to-all(bf16[16,32,128]{2,1,0:T(8,128)(2,1)S(1)} %rim_second.1), channel_id=1, replica_groups=mesh['groups'=2,'brick'=4,'chan'=2,'sub'=2] {'brick','chan','sub'}, dimensions={0} | all-to-all | bytes 262144 | tf_op jit(solution)/shard_map/all_to_all | solution.py:533
  51.8 0.7 %arrived_tiles.1 = bf16[1,128,256]{2,1,0:T(8,128)(2,1)} custom-call(f32[6,128]{1,0:T(8,128)S(1)} %stack.39.vectors, bf16[16,32,128]{2,1,0:T(8,128)(2,1)S(1)} %all_to_all.5.parts), custom_call_target="tpu_custom_call" | custom-call | tf_op jit(solution)/shard_map/arrived_tiles/pallas_call | solution.py:434
  (44 shorter events, 0.2 us)
Async XLA Ops:
  0.0 1.0 %copy-start = (bf16[512,256]{1,0:T(8,128)(2,1)S(1)}, bf16[512,256]{1,0:T(8,128)(2,1)}, u32[]{:S(2)}) copy-start(bf16[512,256]{1,0:T(8,128)(2,1)} %param.14) | copy-start | bytes 786436
  0.0 2.7 %copy-start.12 = (f32[128]{0:T(128)S(1)}, f32[128]{0:T(128)}, u32[]{:S(2)}) copy-start(f32[128]{0:T(128)} %param.27) | copy-start | bytes 1540
  0.0 2.7 %copy-start.11 = (f32[128]{0:T(128)S(1)}, f32[128]{0:T(128)}, u32[]{:S(2)}) copy-start(f32[128]{0:T(128)} %param.26) | copy-start | bytes 1540
  0.0 2.7 %copy-start.10 = (f32[128]{0:T(128)S(1)}, f32[128]{0:T(128)}, u32[]{:S(2)}) copy-start(f32[128]{0:T(128)} %param.25) | copy-start | bytes 1540
  0.0 2.7 %copy-start.9 = (f32[128]{0:T(128)S(1)}, f32[128]{0:T(128)}, u32[]{:S(2)}) copy-start(f32[128]{0:T(128)} %param.24) | copy-start | bytes 1540
  0.0 2.7 %copy-start.8 = (f32[128]{0:T(128)S(1)}, f32[128]{0:T(128)}, u32[]{:S(2)}) copy-start(f32[128]{0:T(128)} %param.23) | copy-start | bytes 1540
  0.0 2.7 %copy-start.7 = (f32[128]{0:T(128)S(1)}, f32[128]{0:T(128)}, u32[]{:S(2)}) copy-start(f32[128]{0:T(128)} %param.22) | copy-start | bytes 1540
  0.0 2.7 %copy-start.3 = (s32[16,27]{1,0:T(8,128)S(1)}, s32[16,27]{1,0:T(8,128)}, u32[]{:S(2)}) copy-start(s32[16,27]{1,0:T(8,128)} %table_near.3) | copy-start | bytes 5188
  0.1 16.7 %copy-start.6 = (bf16[27,128,256]{2,1,0:T(8,128)(2,1)S(1)}, bf16[27,128,256]{2,1,0:T(8,128)(2,1)}, u32[]{:S(2)}) copy-start(bf16[27,128,256]{2,1,0:T(8,128)(2,1)} %weight.8) | copy-start | bytes 5308420
  2.1 1.5 %collective-permute-start = (bf16[4,64,256]{2,1,0:T(8,128)(2,1)S(1)}, bf16[4,64,256]{2,1,0:T(8,128)(2,1)S(1)}, u32[]{:S(2)}, u32[]{:S(2)}) collective-permute-start(bf16[4,64,256]{2,1,0:T(8,128)(2,1)S(1)} %fusion.1), channel_id=1, source_target_pairs={{0,1},{1,0},{2,3},{3,2},{4,5},{5,4},{6,7},{7,6},{8,9},{9,8},{10,11... | collective-permute-start | bytes 393224 | tf_op jit(solution)/shard_map/ppermute | solution.py:67
  3.6 7.7 %collective-permute-start.1 = (bf16[2,64,256]{2,1,0:T(8,128)(2,1)S(1)}, bf16[2,64,256]{2,1,0:T(8,128)(2,1)S(1)}, u32[]{:S(2)}, u32[]{:S(2)}) collective-permute-start(bf16[2,64,256]{2,1,0:T(8,128)(2,1)S(1)} %pad_maximum_fusion.1), channel_id=1, source_target_pairs={{0,4},{4,8},{8,12},{12,0},{1,5},{5,9},{9,13},{13,1},{2,6},{6,10},{... | collective-permute-start | bytes 196616 | tf_op jit(solution)/shard_map/ppermute | solution.py:67
  6.6 6.1 %collective-permute-start.2 = (bf16[2,64,256]{2,1,0:T(8,128)(2,1)S(1)}, bf16[2,64,256]{2,1,0:T(8,128)(2,1)S(1)}, u32[]{:S(2)}, u32[]{:S(2)}) collective-permute-start(bf16[2,64,256]{2,1,0:T(8,128)(2,1)S(1)} %pad_maximum_fusion.2), channel_id=1, source_target_pairs={{0,12},{4,0},{8,4},{12,8},{1,13},{5,1},{9,5},{13,9},{2,14},{6,2},{... | collective-permute-start | bytes 196616 | tf_op jit(solution)/shard_map/ppermute | solution.py:67
  8.7 6.5 %collective-permute-start.3 = (bf16[2,64,256]{2,1,0:T(8,128)(2,1)S(1)}, bf16[2,64,256]{2,1,0:T(8,128)(2,1)S(1)}, u32[]{:S(2)}, u32[]{:S(2)}) collective-permute-start(bf16[2,64,256]{2,1,0:T(8,128)(2,1)S(1)} %pad_maximum_fusion.3), channel_id=1, source_target_pairs={{0,8},{4,12},{8,0},{12,4},{1,9},{5,13},{9,1},{13,5},{2,10},{6,14},... | collective-permute-start | bytes 196616 | tf_op jit(solution)/shard_map/ppermute | solution.py:67
  9.8 8.9 %collective-permute-start.4 = (bf16[2,64,256]{2,1,0:T(8,128)(2,1)S(1)}, bf16[2,64,256]{2,1,0:T(8,128)(2,1)S(1)}, u32[]{:S(2)}, u32[]{:S(2)}) collective-permute-start(bf16[2,64,256]{2,1,0:T(8,128)(2,1)S(1)} %pad_maximum_fusion.refs_0_), channel_id=1, source_target_pairs={{2,0},{0,2},{3,1},{1,3},{6,4},{4,6},{7,5},{5,7},{10,8},{8,10},{11,... | collective-permute-start | bytes 196616 | tf_op jit(solution)/shard_map/ppermute | solution.py:62
  11.4 7.4 %collective-permute-start.5 = (bf16[2,64,256]{2,1,0:T(8,128)(2,1)S(1)}, bf16[2,64,256]{2,1,0:T(8,128)(2,1)S(1)}, u32[]{:S(2)}, u32[]{:S(2)}) collective-permute-start(bf16[2,64,256]{2,1,0:T(8,128)(2,1)S(1)} %collective-permute-done.1.refs_1_), channel_id=1, source_target_pairs={{2,0},{0,2},{3,1},{1,3},{6,4},{4,6},{7,5},{5,7},{10,8},{8,10},{11,... | collective-permute-start | bytes 196616 | tf_op jit(solution)/shard_map/ppermute | solution.py:62
  12.7 6.0 %collective-permute-start.6 = (bf16[2,64,256]{2,1,0:T(8,128)(2,1)S(1)}, bf16[2,64,256]{2,1,0:T(8,128)(2,1)S(1)}, u32[]{:S(2)}, u32[]{:S(2)}) collective-permute-start(bf16[2,64,256]{2,1,0:T(8,128)(2,1)S(1)} %collective-permute-done.2.refs_2_), channel_id=1, source_target_pairs={{2,0},{0,2},{3,1},{1,3},{6,4},{4,6},{7,5},{5,7},{10,8},{8,10},{11,... | collective-permute-start | bytes 196616 | tf_op jit(solution)/shard_map/ppermute | solution.py:62
  15.3 4.3 %collective-permute-start.7 = (bf16[2,64,256]{2,1,0:T(8,128)(2,1)S(1)}, bf16[2,64,256]{2,1,0:T(8,128)(2,1)S(1)}, u32[]{:S(2)}, u32[]{:S(2)}) collective-permute-start(bf16[2,64,256]{2,1,0:T(8,128)(2,1)S(1)} %collective-permute-done.3.refs_3_), channel_id=1, source_target_pairs={{2,0},{0,2},{3,1},{1,3},{6,4},{4,6},{7,5},{5,7},{10,8},{8,10},{11,... | collective-permute-start | bytes 196616 | tf_op jit(solution)/shard_map/ppermute | solution.py:62
  16.8 2.8 %copy-start.4 = (s32[2,2]{1,0:T(2,128)S(1)}, s32[2,2]{1,0:T(2,128)}, u32[]{:S(2)}) copy-start(s32[2,2]{1,0:T(2,128)} %halo_near.3) | copy-start | bytes 52
  20.1 2.7 %collective-permute-start.8 = (bf16[2,64,256]{2,1,0:T(8,128)(2,1)S(1)}, bf16[2,64,256]{2,1,0:T(8,128)(2,1)S(1)}, u32[]{:S(2)}, u32[]{:S(2)}) collective-permute-start(bf16[2,64,256]{2,1,0:T(8,128)(2,1)S(1)} %get-tuple-element.12), channel_id=1, source_target_pairs={{0,1},{2,3},{4,5},{6,7},{8,9},{10,11},{12,13},{14,15},{1,0},{3,2},... | collective-permute-start | bytes 196616 | tf_op jit(solution)/shard_map/ppermute | solution.py:57
  20.2 2.6 %collective-permute-start.9 = (bf16[2,64,256]{2,1,0:T(8,128)(2,1)S(1)}, bf16[2,64,256]{2,1,0:T(8,128)(2,1)S(1)}, u32[]{:S(2)}, u32[]{:S(2)}) collective-permute-start(bf16[2,64,256]{2,1,0:T(8,128)(2,1)S(1)} %get-tuple-element.13), channel_id=1, source_target_pairs={{1,4},{3,6},{5,8},{7,10},{9,12},{11,14},{4,1},{6,3},{8,5},{10,7},{... | collective-permute-start | bytes 196616 | tf_op jit(solution)/shard_map/ppermute | solution.py:57
  22.8 6.9 %copy-start.1 = (bf16[27,128,256]{2,1,0:T(8,128)(2,1)S(1)}, bf16[27,128,256]{2,1,0:T(8,128)(2,1)}, u32[]{:S(2)}) copy-start(bf16[27,128,256]{2,1,0:T(8,128)(2,1)} %weight.11) | copy-start | bytes 5308420
  24.3 8.7 %collective-permute-start.12 = (bf16[16,64,128]{2,1,0:T(8,128)(2,1)S(1)}, bf16[16,64,128]{2,1,0:T(8,128)(2,1)S(1)}, u32[]{:S(2)}, u32[]{:S(2)}) collective-permute-start(bf16[16,64,128]{2,1,0:T(8,128)(2,1)S(1)} %get-tuple-element.16.refs_0_), channel_id=1, source_target_pairs={{2,0},{0,2},{3,1},{1,3},{6,4},{4,6},{7,5},{5,7},{10,8},{8,10},{11,... | collective-permute-start | bytes 786440 | tf_op jit(solution)/shard_map/ppermute | solution.py:62
  25.9 6.5 %collective-permute-start.10 = (bf16[2,64,128]{2,1,0:T(8,128)(2,1)S(1)}, bf16[2,64,128]{2,1,0:T(8,128)(2,1)S(1)}, u32[]{:S(2)}, u32[]{:S(2)}) collective-permute-start(bf16[2,64,128]{2,1,0:T(8,128)(2,1)S(1)} %get-tuple-element.14), channel_id=1, source_target_pairs={{0,1},{2,3},{4,5},{6,7},{8,9},{10,11},{12,13},{14,15},{1,0},{3,2},... | collective-permute-start | bytes 98312 | tf_op jit(solution)/shard_map/ppermute | solution.py:57
  29.0 3.4 %collective-permute-start.11 = (bf16[2,64,128]{2,1,0:T(8,128)(2,1)S(1)}, bf16[2,64,128]{2,1,0:T(8,128)(2,1)S(1)}, u32[]{:S(2)}, u32[]{:S(2)}) collective-permute-start(bf16[2,64,128]{2,1,0:T(8,128)(2,1)S(1)} %get-tuple-element.15), channel_id=1, source_target_pairs={{1,4},{3,6},{5,8},{7,10},{9,12},{11,14},{4,1},{6,3},{8,5},{10,7},{... | collective-permute-start | bytes 98312 | tf_op jit(solution)/shard_map/ppermute | solution.py:57
  32.4 4.4 %copy-start.2 = (bf16[8,128,256]{2,1,0:T(8,128)(2,1)S(1)}, bf16[8,128,256]{2,1,0:T(8,128)(2,1)}, u32[]{:S(2)}) copy-start(bf16[8,128,256]{2,1,0:T(8,128)(2,1)} %down_weight.1) | copy-start | bytes 1572868
  32.4 4.3 %copy-start.5 = (s32[16,1]{0,1:T(1,128)S(1)}, s32[16,1]{0,1:T(1,128)}, u32[]{:S(2)}) copy-start(s32[16,1]{0,1:T(1,128)} %param.18) | copy-start | bytes 196
  32.4 4.3 %collective-permute-start.13 = (bf16[4,64,128]{2,1,0:T(8,128)(2,1)S(1)}, bf16[4,64,128]{2,1,0:T(8,128)(2,1)S(1)}, u32[]{:S(2)}, u32[]{:S(2)}) collective-permute-start(bf16[4,64,128]{2,1,0:T(8,128)(2,1)S(1)} %pack.1), channel_id=1, source_target_pairs={{2,0},{0,2},{3,1},{1,3},{6,4},{4,6},{7,5},{5,7},{10,8},{8,10},{11,... | collective-permute-start | bytes 196616 | tf_op jit(solution)/shard_map/ppermute | solution.py:62

commit v5 on v4

--- a/solution.py
+++ b/solution.py
@@ -45,21 +45,35 @@
     ]
 
 
-def owner_pairs(block, parity, distance=0):
-    bricks, subs, chans = (lax.axis_size(axis) for axis in ("brick", "sub", "chan"))
-
-    def device(owner, chan):
-        return (owner // subs * chans + chan % chans) * subs + owner % subs
-
-    pairs = [(o, o + 1) for o in range(parity, bricks * subs - 1, 2)]
-    pairs += [(b, a) for a, b in pairs]
-    route = [(device(a, c + distance), device(b, c)) for a, b in pairs for c in range(chans)]
-    return lax.ppermute(block, ("brick", "chan", "sub"), route)
+def owner_pairs(block, parity):
+    owners = lax.axis_size("brick") * lax.axis_size("sub")
+    pairs = [(o, o + 1) for o in range(parity, owners - 1, 2)]
+    if parity == 1 and owners % 2 == 0:
+        pairs.append((0, owners - 1))
+    return lax.ppermute(block, ("brick", "sub"), pairs + [(b, a) for a, b in pairs])
+
+
+def named(place, odd):
+    owners = lax.axis_size("brick") * lax.axis_size("sub")
+    owner = place.brick * lax.axis_size("sub") + place.sub
+    inside = (owner > 0) & ((owner < owners - 1) | (place.parity == 0))
+    return jnp.where(inside, odd, jnp.zeros_like(odd))
 
 
 def from_ahead(block, axis, distance):
     n = lax.axis_size(axis)
     return lax.ppermute(block, axis, [((i + distance) % n, i) for i in range(n)])
+
+
+def other(brick, step, bricks, way=1):
+    if bricks & (bricks - 1) == 0:
+        return brick ^ step
+    return (brick + way * step + bricks) % bricks
+
+
+def across(block, step):
+    bricks = lax.axis_size("brick")
+    return lax.ppermute(block, "brick", [(b, other(b, step, bricks)) for b in range(bricks)])
 
 
 def to_ahead(block, axis, distance):
@@ -80,7 +94,7 @@
     place = Place()
     split = BLK // parts[0, 0].shape[1]
     for (jb, j), part in parts.items():
-        source = lax.rem(place.brick - jb + bricks, bricks)
+        source = other(place.brick, jb, bricks, -1)
         chan = lax.rem(place.chan + j, chans)
         for js in range(subs):
             sub = lax.rem(place.sub + js, subs)
@@ -145,7 +159,7 @@
 def rim_blocks(place, even, odd, lanes, rim):
     reach = even.shape[0]
     rim[pl.ds(reach * (1 - place.parity), reach), :, lanes] = even[...]
-    rim[pl.ds(reach * place.parity, reach), :, lanes] = odd[...]
+    rim[pl.ds(reach * place.parity, reach), :, lanes] = named(place, odd[...])
 
 
 def named_sums(table, scalars, given, weight, products, total):
@@ -215,7 +229,7 @@
         parts, before = parts[:-1], parts[-1]
     place = Place()
     for jb, part in zip(behind, parts):
-        source = lax.rem(place.brick - jb + bricks, bricks)
+        source = other(place.brick, jb, bricks, -1)
         for js in range(subs):
             held[source * subs + lax.rem(place.sub + js, subs)] = part[js]
     total[...] = before[...] if started else jnp.zeros(total.shape, F32)
@@ -244,7 +258,7 @@
     )(table, weight, *given)
 
 
-def rim_first_kernel(halo_near, table_near, vectors, own, even, odd, weight, *refs):
+def rim_first_kernel(odd, even, halo_near, table_near, vectors, own, weight, *refs):
     hidden, even_out, odd_out, rim, products, total, halo, table, semaphore = refs
     scalars = Scalars([halo_near, table_near], [halo, table], semaphore)
     reach = even.shape[0]
@@ -281,7 +295,7 @@
         compiler_params=LIMIT,
         cost_estimate=cost(2 * reach, weight),
         name="rim_first",
-    )(halo, table, vectors, own, even, odd, weight)
+    )(odd, even, halo, table, vectors, own, weight)
 
 
 def pack_kernel(even, odd, *refs):
@@ -447,17 +461,21 @@
 
     def pieces(js):
         column = lax.dynamic_index_in_dim(ordered, lax.rem(sub + js, subs), 1, keepdims=False)
-        doubled = jnp.concatenate([column, column], axis=0)
-        return lax.dynamic_slice_in_dim(doubled, brick, bricks, 0)
+        return jnp.stack(
+            [
+                lax.dynamic_index_in_dim(column, other(brick, jb, bricks), 0, keepdims=False)
+                for jb in range(bricks)
+            ]
+        )
 
     by_sub = [pieces(0)]
     for js in range(1, subs):
         by_sub.append(to_ahead(pieces(subs - js), "sub", subs - js))
     stacked = [jnp.stack([piece[jb] for piece in by_sub]) for jb in range(bricks)]
-    order = sorted(range(1, bricks), key=lambda jb: min(jb, bricks - jb))
+    order = sorted(range(1, bricks), key=lambda jb: (jb % 2 == 0, -jb))
     parts = {(0, 0): stacked[0]}
     for jb in order:
-        parts[jb, 0] = to_ahead(stacked[jb], "brick", jb)
+        parts[jb, 0] = across(stacked[jb], jb)
     for jb in [0] + order:
         for j in range(1, chans):
             parts[jb, j] = from_ahead(parts[jb, 0], "chan", j)

time: 52.8 us -> 51.9 us (0.983)
  blocking collectives: 13 us -> 11 us
  waiting for transfers between devices: 4.5 us -> 6.21 us
  starting transfers between devices: 18.5 us -> 17.3 us
  local copies, waits for them, and re-layouts: 1 us -> 1.77 us
    ppermute x4 -> x1, starting transfers between devices: 6.65 us -> 0.52 us  [to_ahead(): lax.ppermute(block, axis, [(i, (i + distance) % n) for i in range(n)])]
    ppermute x4 -> x7, starting transfers between devices: 4.52 us -> 8.62 us  [the longest x3 5.72 us: across(): lax.ppermute(block, 'brick', [(b, other(b, step, bricks)) for b in range(...]
    ppermute x4 -> x7, waiting for transfers between devices: 0.01 us -> 3.95 us  [the longest x4 3.16 us: owner_pairs(): lax.ppermute(block, ('brick', 'sub'), pairs + [(b, a) for a, b in pairs])]
    ppermute x4 -> x1, waiting for transfers between devices: 2.63 us -> 0.21 us  [to_ahead(): lax.ppermute(block, axis, [(i, (i + distance) % n) for i in range(n)])]
    all_to_all x1, blocking collectives: 13 us -> 11 us  [body(): lax.all_to_all(partial, ('brick', 'chan', 'sub'), split_axis=0, concat_ax...]
    ppermute x6, starting transfers between devices: 7.29 us -> 8.15 us  [from_ahead(): lax.ppermute(block, axis, [((i + distance) % n, i) for i in range(n)])]
    another operation x1, local copies, waits for them, and re-layouts: 0.03 us -> 0.75 us  [body(): jnp.stack([gain_first, bias_first, gain_second, bias_second, gain_down, b...]
  transfers between devices with their start and end apart: 14 -> 14, of which waited for: 4 -> 7; matrix products, arithmetic and copies ran while one was open for 0% -> 2% of each run, Pallas kernels for 17% -> 18%
where the time goes in v5:
time: 51.9 us; the launch traced here: 51.6 us
  starting transfers between devices  17.3 us (33%)
  Pallas kernels  14.1 us (27%)
  blocking collectives  11 us (21%)
  waiting for transfers between devices  6.21 us (12%)
  local copies, waits for them, and re-layouts  1.77 us (3%)
  matrix products  1.04 us (2%)
    all_to_all x1, blocking collectives, body(): lax.all_to_all(partial, ('brick', 'chan', 'sub'), split_axis=0, concat_ax...  11 us
    ppermute x6, starting transfers between devices, from_ahead(): lax.ppermute(block, axis, [((i + distance) % n, i) for i in range(n)])  8.15 us
    ppermute x3, starting transfers between devices, across(): lax.ppermute(block, 'brick', [(b, other(b, step, bricks)) for b in range(...  5.72 us
    pallas_call x2, Pallas kernels, own_second(): pl.pallas_call(functools.partial(own_second_kernel, nearest, chans), out_...  5.32 us
    pallas_call x2, Pallas kernels, pieces_first(): pl.pallas_call(functools.partial(pieces_first_kernel, bricks, subs, behin...  3.87 us
    ppermute x4, waiting for transfers between devices, owner_pairs(): lax.ppermute(block, ('brick', 'sub'), pairs + [(b, a) for a, b in pairs])  3.16 us
    ppermute x4, starting transfers between devices, owner_pairs(): lax.ppermute(block, ('brick', 'sub'), pairs + [(b, a) for a, b in pairs])  2.9 us
    pallas_call x1, Pallas kernels, rim_second(): pl.pallas_call(functools.partial(rim_second_kernel, bricks, subs, chans,...  2.07 us
  transfers between devices with their start and end apart: 14, of which 7 were waited for; matrix products, arithmetic and copies ran while one was open for 2% of the time, Pallas kernels for 18%

profile of v5, /device:TPU:0, one launch (start us, length us, event | category | flops | bytes accessed | tf_op | source)
XLA Modules:
  0.0 51.6 jit_solution(5853832144009082155)
XLA Ops:
  0.0 0.9 %copy-done = bf16[512,256]{1,0:T(8,128)(2,1)S(1)} copy-done((bf16[512,256]{1,0:T(8,128)(2,1)S(1)}, bf16[512,256]{1,0:T(8,128)(2,1)}, u32[]{:S(2)}) %copy-start) | copy-done | bytes 262168
  1.0 1.0 %convolution_convert_fusion = bf16[512,256]{1,0:T(8,128)(2,1)S(1)} fusion(bf16[512,256]{1,0:T(8,128)(2,1)S(1)} %copy-done, s32[512]{0:T(512)} %bitcast.34), kind=kOutput, calls=%fused_computation | convolution fusion | flops 134610944 | bytes 526336 | tf_op jit(solution)/shard_map/dot_general | solution.py:87
  2.1 0.5 %collective-permute-start = (bf16[4,64,256]{2,1,0:T(8,128)(2,1)S(1)}, bf16[4,64,256]{2,1,0:T(8,128)(2,1)S(1)}, u32[]{:S(2)}, u32[]{:S(2)}) collective-permute-start(bf16[4,64,256]{2,1,0:T(8,128)(2,1)S(1)} %pad_maximum_fusion), channel_id=1, source_target_pairs={{0,1},{1,0},{2,3},{3,2},{4,5},{5,4},{6,7},{7,6},{8,9},{9,8},{10,11... | collective-permute-start | bytes 393224 | tf_op jit(solution)/shard_map/ppermute | solution.py:81
  2.6 0.8 %stack.50.vectors = f32[6,128]{1,0:T(8,128)S(1)} concatenate(f32[1,128]{1,0:T(1,128)} %bitcast.28, f32[1,128]{1,0:T(1,128)} %bitcast.29, f32[1,128]{1,0:T(1,128)} %bitcast.30, f32[1,128]{1,0:T(1,128)} %bitcast.31, f32[1,128]{1,0:T(1,128)} %bitcast.32, f32[1,128]{1,0:T(1,128)} %bitcast.33), dimensions={0} | concatenate | bytes 6144 | tf_op jit(solution)/shard_map/stack | solution.py:510
  3.4 0.2 collective-permute-done
  3.6 5.0 %collective-permute-start.1 = (bf16[2,64,256]{2,1,0:T(8,128)(2,1)S(1)}, bf16[2,64,256]{2,1,0:T(8,128)(2,1)S(1)}, u32[]{:S(2)}, u32[]{:S(2)}) collective-permute-start(bf16[2,64,256]{2,1,0:T(8,128)(2,1)S(1)} %pad_maximum_fusion.2), channel_id=1, source_target_pairs={{0,12},{4,8},{8,4},{12,0},{1,13},{5,9},{9,5},{13,1},{2,14},{6,10},... | collective-permute-start | bytes 196616 | tf_op jit(solution)/shard_map/ppermute | solution.py:76
  8.6 0.1 collective-permute-start.2
  8.7 0.6 %collective-permute-start.3 = (bf16[2,64,256]{2,1,0:T(8,128)(2,1)S(1)}, bf16[2,64,256]{2,1,0:T(8,128)(2,1)S(1)}, u32[]{:S(2)}, u32[]{:S(2)}) collective-permute-start(bf16[2,64,256]{2,1,0:T(8,128)(2,1)S(1)} %pad_maximum_fusion.4), channel_id=1, source_target_pairs={{0,8},{4,12},{8,0},{12,4},{1,9},{5,13},{9,1},{13,5},{2,10},{6,14},... | collective-permute-start | bytes 196616 | tf_op jit(solution)/shard_map/ppermute | solution.py:76
  9.4 1.7 %collective-permute-start.4 = (bf16[2,64,256]{2,1,0:T(8,128)(2,1)S(1)}, bf16[2,64,256]{2,1,0:T(8,128)(2,1)S(1)}, u32[]{:S(2)}, u32[]{:S(2)}) collective-permute-start(bf16[2,64,256]{2,1,0:T(8,128)(2,1)S(1)} %pad_maximum_fusion.1.refs_0_), channel_id=1, source_target_pairs={{2,0},{0,2},{3,1},{1,3},{6,4},{4,6},{7,5},{5,7},{10,8},{8,10},{11,... | collective-permute-start | bytes 196616 | tf_op jit(solution)/shard_map/ppermute | solution.py:65
  11.1 0.4 collective-permute-done.1.refs_1_
  11.5 1.8 %collective-permute-start.5 = (bf16[2,64,256]{2,1,0:T(8,128)(2,1)S(1)}, bf16[2,64,256]{2,1,0:T(8,128)(2,1)S(1)}, u32[]{:S(2)}, u32[]{:S(2)}) collective-permute-start(bf16[2,64,256]{2,1,0:T(8,128)(2,1)S(1)} %collective-permute-done.1.refs_1_), channel_id=1, source_target_pairs={{2,0},{0,2},{3,1},{1,3},{6,4},{4,6},{7,5},{5,7},{10,8},{8,10},{11,... | collective-permute-start | bytes 196616 | tf_op jit(solution)/shard_map/ppermute | solution.py:65
  13.3 0.4 collective-permute-done.2.refs_2_
  13.7 1.5 %collective-permute-start.6 = (bf16[2,64,256]{2,1,0:T(8,128)(2,1)S(1)}, bf16[2,64,256]{2,1,0:T(8,128)(2,1)S(1)}, u32[]{:S(2)}, u32[]{:S(2)}) collective-permute-start(bf16[2,64,256]{2,1,0:T(8,128)(2,1)S(1)} %collective-permute-done.2.refs_2_), channel_id=1, source_target_pairs={{2,0},{0,2},{3,1},{1,3},{6,4},{4,6},{7,5},{5,7},{10,8},{8,10},{11,... | collective-permute-start | bytes 196616 | tf_op jit(solution)/shard_map/ppermute | solution.py:65
  15.2 0.9 %collective-permute-start.7 = (bf16[2,64,256]{2,1,0:T(8,128)(2,1)S(1)}, bf16[2,64,256]{2,1,0:T(8,128)(2,1)S(1)}, u32[]{:S(2)}, u32[]{:S(2)}) collective-permute-start(bf16[2,64,256]{2,1,0:T(8,128)(2,1)S(1)} %collective-permute-done.3.refs_3_), channel_id=1, source_target_pairs={{2,0},{0,2},{3,1},{1,3},{6,4},{4,6},{7,5},{5,7},{10,8},{8,10},{11,... | collective-permute-start | bytes 196616 | tf_op jit(solution)/shard_map/ppermute | solution.py:65
  16.2 1.9 %pieces_first.2.refs_4_ = f32[16,64,128]{2,1,0:T(8,128)S(1)} custom-call(s32[16,27]{1,0:T(8,128)S(1)} %get-tuple-element.29.table_near, bf16[27,128,256]{2,1,0:T(8,128)(2,1)S(1)} %copy-done.6, bf16[2,64,256]{2,1,0:T(8,128)(2,1)S(1)} %pad_maximum_fusion.1.refs_0_, bf16[2,64,256]{2,1,0:T(8,128)(2,1)S(1)} %collective-permute-done.1.refs_1_, ...), custom_call_target="tpu_custom_call" | custom-call | flops 1811939328 | tf_op jit(solution)/shard_map/pieces_first/pallas_call | solution.py:245
  18.1 1.3 %collective-permute-done.7.refs_7_.refs_3_ = bf16[2,64,256]{2,1,0:T(8,128)(2,1)S(1)} collective-permute-done((bf16[2,64,256]{2,1,0:T(8,128)(2,1)S(1)}, bf16[2,64,256]{2,1,0:T(8,128)(2,1)S(1)}, u32[]{:S(2)}, u32[]{:S(2)}) %collective-permute-start.7) | collective-permute-done | bytes 65568 | tf_op jit(solution)/shard_map/ppermute | solution.py:65
  19.5 0.6 %assemble.1 = (bf16[16,64,256]{2,1,0:T(8,128)(2,1)S(1)}, bf16[2,64,256]{2,1,0:T(8,128)(2,1)S(1)}, bf16[2,64,256]{2,1,0:T(8,128)(2,1)S(1)}) custom-call(s32[2,2]{1,0:T(2,128)S(1)} %copy-done.4, bf16[2,64,256]{2,1,0:T(8,128)(2,1)S(1)} %pad_maximum_fusion.1.refs_0_, bf16[2,64,256]{2,1,0:T(8,128)(2,1)S(1)} %collective-permute-done.1.refs_1_, ...), custom_call_target="tpu_custom_call" | custom-call | tf_op jit(solution)/shard_map/assemble/pallas_call | solution.py:113
  20.1 0.1 collective-permute-start.8
  20.1 1.3 %collective-permute-start.9 = (bf16[2,64,256]{2,1,0:T(8,128)(2,1)S(1)}, bf16[2,64,256]{2,1,0:T(8,128)(2,1)S(1)}, u32[]{:S(2)}, u32[]{:S(2)}) collective-permute-start(bf16[2,64,256]{2,1,0:T(8,128)(2,1)S(1)} %get-tuple-element.13), channel_id=1, source_target_pairs={{0,1},{4,5},{8,9},{12,13},{1,0},{5,4},{9,8},{13,12},{2,3},{6,7},{1... | collective-permute-start | bytes 196616 | tf_op jit(solution)/shard_map/ppermute | solution.py:53
  21.4 1.9 %pieces_first.3.own = f32[16,64,128]{2,1,0:T(8,128)S(1)} custom-call(s32[16,27]{1,0:T(8,128)S(1)} %get-tuple-element.31.table_near, bf16[27,128,256]{2,1,0:T(8,128)(2,1)S(1)} %copy-done.6, bf16[2,64,256]{2,1,0:T(8,128)(2,1)S(1)} %collective-permute-done.4.refs_4_.refs_0_, bf16[2,64,256]{2,1,0:T(8,128)(2,1)S(1)} %collective-permute-done.5.refs_5_.refs_1_, ...), custom_call_target="tpu_custom_call" | custom-call | flops 1811939328 | tf_op jit(solution)/shard_map/pieces_first/pallas_call | solution.py:245
  23.4 2.3 %collective-permute-done.8.odd = bf16[2,64,256]{2,1,0:T(8,128)(2,1)S(1)} collective-permute-done((bf16[2,64,256]{2,1,0:T(8,128)(2,1)S(1)}, bf16[2,64,256]{2,1,0:T(8,128)(2,1)S(1)}, u32[]{:S(2)}, u32[]{:S(2)}) %collective-permute-start.8) | collective-permute-done | bytes 65568 | tf_op jit(solution)/shard_map/ppermute | solution.py:53
  25.6 1.5 %rim_first.1 = (bf16[16,64,128]{2,1,0:T(8,128)(2,1)S(1)}, bf16[2,64,128]{2,1,0:T(8,128)(2,1)S(1)}, bf16[2,64,128]{2,1,0:T(8,128)(2,1)S(1)}) custom-call(bf16[2,64,256]{2,1,0:T(8,128)(2,1)S(1)} %collective-permute-done.8.odd, bf16[2,64,256]{2,1,0:T(8,128)(2,1)S(1)} %collective-permute-done.9.even, s32[2,2]{1,0:T(2,128)S(1)} %copy-done.4, ...), custom_call_target="tpu_custom_call" | custom-call | flops 905969664 | tf_op jit(solution)/shard_map/rim_first/pallas_call | solution.py:287
  27.1 1.2 %collective-permute-start.12 = (bf16[16,64,128]{2,1,0:T(8,128)(2,1)S(1)}, bf16[16,64,128]{2,1,0:T(8,128)(2,1)S(1)}, u32[]{:S(2)}, u32[]{:S(2)}) collective-permute-start(bf16[16,64,128]{2,1,0:T(8,128)(2,1)S(1)} %get-tuple-element.16.refs_0_), channel_id=1, source_target_pairs={{2,0},{0,2},{3,1},{1,3},{6,4},{4,6},{7,5},{5,7},{10,8},{8,10},{11,... | collective-permute-start | bytes 786440 | tf_op jit(solution)/shard_map/ppermute | solution.py:65
  28.3 1.6 %collective-permute-start.11 = (bf16[2,64,128]{2,1,0:T(8,128)(2,1)S(1)}, bf16[2,64,128]{2,1,0:T(8,128)(2,1)S(1)}, u32[]{:S(2)}, u32[]{:S(2)}) collective-permute-start(bf16[2,64,128]{2,1,0:T(8,128)(2,1)S(1)} %get-tuple-element.15), channel_id=1, source_target_pairs={{1,4},{5,8},{9,12},{0,13},{4,1},{8,5},{12,9},{13,0},{3,6},{7,10},{... | collective-permute-start | bytes 98312 | tf_op jit(solution)/shard_map/ppermute | solution.py:53
  29.9 2.7 %own_second.2.refs_0_.refs_2_ = f32[16,64,128]{2,1,0:T(8,128)S(1)} custom-call(s32[16,27]{1,0:T(8,128)S(1)} %copy-done.3, bf16[27,128,256]{2,1,0:T(8,128)(2,1)S(1)} %copy-done.1, bf16[16,64,128]{2,1,0:T(8,128)(2,1)S(1)} %get-tuple-element.16.refs_0_), custom_call_target="tpu_custom_call" | custom-call | flops 1811939328 | tf_op jit(solution)/shard_map/own_second/pallas_call | solution.py:347
  32.5 0.9 %collective-permute-done.11.odd.refs_1_ = bf16[2,64,128]{2,1,0:T(8,128)(2,1)S(1)} collective-permute-done((bf16[2,64,128]{2,1,0:T(8,128)(2,1)S(1)}, bf16[2,64,128]{2,1,0:T(8,128)(2,1)S(1)}, u32[]{:S(2)}, u32[]{:S(2)}) %collective-permute-start.11) | collective-permute-done | bytes 32800 | tf_op jit(solution)/shard_map/ppermute | solution.py:53
  33.5 1.0 %collective-permute-start.13 = (bf16[4,64,128]{2,1,0:T(8,128)(2,1)S(1)}, bf16[4,64,128]{2,1,0:T(8,128)(2,1)S(1)}, u32[]{:S(2)}, u32[]{:S(2)}) collective-permute-start(bf16[4,64,128]{2,1,0:T(8,128)(2,1)S(1)} %pack.1), channel_id=1, source_target_pairs={{2,0},{0,2},{3,1},{1,3},{6,4},{4,6},{7,5},{5,7},{10,8},{8,10},{11,... | collective-permute-start | bytes 196616 | tf_op jit(solution)/shard_map/ppermute | solution.py:65
  34.4 2.7 %own_second.3.refs_3_ = f32[16,64,128]{2,1,0:T(8,128)S(1)} custom-call(s32[16,27]{1,0:T(8,128)S(1)} %copy-done.3, bf16[27,128,256]{2,1,0:T(8,128)(2,1)S(1)} %copy-done.1, bf16[16,64,128]{2,1,0:T(8,128)(2,1)S(1)} %collective-permute-done.12.refs_0_), custom_call_target="tpu_custom_call" | custom-call | flops 1811939328 | tf_op jit(solution)/shard_map/own_second/pallas_call | solution.py:347
  37.1 0.7 %collective-permute-done.13.refs_4_ = bf16[4,64,128]{2,1,0:T(8,128)(2,1)S(1)} collective-permute-done((bf16[4,64,128]{2,1,0:T(8,128)(2,1)S(1)}, bf16[4,64,128]{2,1,0:T(8,128)(2,1)S(1)}, u32[]{:S(2)}, u32[]{:S(2)}) %collective-permute-start.13) | collective-permute-done | bytes 65568 | tf_op jit(solution)/shard_map/ppermute | solution.py:65
  37.8 2.1 %rim_second.1 = bf16[16,32,128]{2,1,0:T(8,128)(2,1)S(1)} custom-call(s32[1,16]{1,0:T(1,128)S(1)} %bitcast.26, s32[16,27]{1,0:T(8,128)S(1)} %get-tuple-element.30.table_near, f32[6,128]{1,0:T(8,128)S(1)} %stack.50.vectors, bf16[16,64,256]{2,1,0:T(8,128)(2,1)S(1)} %get-tuple-element.11.rows, bf16[27,128,256]{2,1,0:T(8,128)(2,1)S(1)} %copy-done.1, ...), custom_call_target="tpu_custom_call" | custom-call | flops 905969664 | tf_op jit(solution)/shard_map/rim_second/pallas_call | solution.py:417
  39.9 11.0 %all_to_all.5.parts = bf16[16,32,128]{2,1,0:T(8,128)(2,1)S(1)} all-to-all(bf16[16,32,128]{2,1,0:T(8,128)(2,1)S(1)} %rim_second.1), channel_id=1, replica_groups=mesh['groups'=2,'brick'=4,'chan'=2,'sub'=2] {'brick','chan','sub'}, dimensions={0} | all-to-all | bytes 262144 | tf_op jit(solution)/shard_map/all_to_all | solution.py:551
  50.9 0.7 %arrived_tiles.1 = bf16[1,128,256]{2,1,0:T(8,128)(2,1)} custom-call(f32[6,128]{1,0:T(8,128)S(1)} %stack.50.vectors, bf16[16,32,128]{2,1,0:T(8,128)(2,1)S(1)} %all_to_all.5.parts), custom_call_target="tpu_custom_call" | custom-call | tf_op jit(solution)/shard_map/arrived_tiles/pallas_call | solution.py:448
  (30 shorter events, 0.2 us)
Async XLA Ops:
  0.0 1.0 %copy-start = (bf16[512,256]{1,0:T(8,128)(2,1)S(1)}, bf16[512,256]{1,0:T(8,128)(2,1)}, u32[]{:S(2)}) copy-start(bf16[512,256]{1,0:T(8,128)(2,1)} %param.14) | copy-start | bytes 786436
  0.0 3.3 %copy-start.3 = (s32[16,27]{1,0:T(8,128)S(1)}, s32[16,27]{1,0:T(8,128)}, u32[]{:S(2)}) copy-start(s32[16,27]{1,0:T(8,128)} %table_near.3) | copy-start | bytes 5188
  0.0 16.1 %copy-start.6 = (bf16[27,128,256]{2,1,0:T(8,128)(2,1)S(1)}, bf16[27,128,256]{2,1,0:T(8,128)(2,1)}, u32[]{:S(2)}) copy-start(bf16[27,128,256]{2,1,0:T(8,128)(2,1)} %weight.8) | copy-start | bytes 5308420
  2.1 1.5 %collective-permute-start = (bf16[4,64,256]{2,1,0:T(8,128)(2,1)S(1)}, bf16[4,64,256]{2,1,0:T(8,128)(2,1)S(1)}, u32[]{:S(2)}, u32[]{:S(2)}) collective-permute-start(bf16[4,64,256]{2,1,0:T(8,128)(2,1)S(1)} %pad_maximum_fusion), channel_id=1, source_target_pairs={{0,1},{1,0},{2,3},{3,2},{4,5},{5,4},{6,7},{7,6},{8,9},{9,8},{10,11... | collective-permute-start | bytes 393224 | tf_op jit(solution)/shard_map/ppermute | solution.py:81
  3.6 7.9 %collective-permute-start.1 = (bf16[2,64,256]{2,1,0:T(8,128)(2,1)S(1)}, bf16[2,64,256]{2,1,0:T(8,128)(2,1)S(1)}, u32[]{:S(2)}, u32[]{:S(2)}) collective-permute-start(bf16[2,64,256]{2,1,0:T(8,128)(2,1)S(1)} %pad_maximum_fusion.2), channel_id=1, source_target_pairs={{0,12},{4,8},{8,4},{12,0},{1,13},{5,9},{9,5},{13,1},{2,14},{6,10},... | collective-permute-start | bytes 196616 | tf_op jit(solution)/shard_map/ppermute | solution.py:76
  8.6 5.1 %collective-permute-start.2 = (bf16[2,64,256]{2,1,0:T(8,128)(2,1)S(1)}, bf16[2,64,256]{2,1,0:T(8,128)(2,1)S(1)}, u32[]{:S(2)}, u32[]{:S(2)}) collective-permute-start(bf16[2,64,256]{2,1,0:T(8,128)(2,1)S(1)} %pad_maximum_fusion.3), channel_id=1, source_target_pairs={{0,4},{4,0},{8,12},{12,8},{1,5},{5,1},{9,13},{13,9},{2,6},{6,2},{1... | collective-permute-start | bytes 196616 | tf_op jit(solution)/shard_map/ppermute | solution.py:76
  8.7 6.5 %collective-permute-start.3 = (bf16[2,64,256]{2,1,0:T(8,128)(2,1)S(1)}, bf16[2,64,256]{2,1,0:T(8,128)(2,1)S(1)}, u32[]{:S(2)}, u32[]{:S(2)}) collective-permute-start(bf16[2,64,256]{2,1,0:T(8,128)(2,1)S(1)} %pad_maximum_fusion.4), channel_id=1, source_target_pairs={{0,8},{4,12},{8,0},{12,4},{1,9},{5,13},{9,1},{13,5},{2,10},{6,14},... | collective-permute-start | bytes 196616 | tf_op jit(solution)/shard_map/ppermute | solution.py:76
  9.4 8.7 %collective-permute-start.4 = (bf16[2,64,256]{2,1,0:T(8,128)(2,1)S(1)}, bf16[2,64,256]{2,1,0:T(8,128)(2,1)S(1)}, u32[]{:S(2)}, u32[]{:S(2)}) collective-permute-start(bf16[2,64,256]{2,1,0:T(8,128)(2,1)S(1)} %pad_maximum_fusion.1.refs_0_), channel_id=1, source_target_pairs={{2,0},{0,2},{3,1},{1,3},{6,4},{4,6},{7,5},{5,7},{10,8},{8,10},{11,... | collective-permute-start | bytes 196616 | tf_op jit(solution)/shard_map/ppermute | solution.py:65
  11.5 6.6 %collective-permute-start.5 = (bf16[2,64,256]{2,1,0:T(8,128)(2,1)S(1)}, bf16[2,64,256]{2,1,0:T(8,128)(2,1)S(1)}, u32[]{:S(2)}, u32[]{:S(2)}) collective-permute-start(bf16[2,64,256]{2,1,0:T(8,128)(2,1)S(1)} %collective-permute-done.1.refs_1_), channel_id=1, source_target_pairs={{2,0},{0,2},{3,1},{1,3},{6,4},{4,6},{7,5},{5,7},{10,8},{8,10},{11,... | collective-permute-start | bytes 196616 | tf_op jit(solution)/shard_map/ppermute | solution.py:65
  13.7 4.4 %collective-permute-start.6 = (bf16[2,64,256]{2,1,0:T(8,128)(2,1)S(1)}, bf16[2,64,256]{2,1,0:T(8,128)(2,1)S(1)}, u32[]{:S(2)}, u32[]{:S(2)}) collective-permute-start(bf16[2,64,256]{2,1,0:T(8,128)(2,1)S(1)} %collective-permute-done.2.refs_2_), channel_id=1, source_target_pairs={{2,0},{0,2},{3,1},{1,3},{6,4},{4,6},{7,5},{5,7},{10,8},{8,10},{11,... | collective-permute-start | bytes 196616 | tf_op jit(solution)/shard_map/ppermute | solution.py:65
  15.2 4.3 %collective-permute-start.7 = (bf16[2,64,256]{2,1,0:T(8,128)(2,1)S(1)}, bf16[2,64,256]{2,1,0:T(8,128)(2,1)S(1)}, u32[]{:S(2)}, u32[]{:S(2)}) collective-permute-start(bf16[2,64,256]{2,1,0:T(8,128)(2,1)S(1)} %collective-permute-done.3.refs_3_), channel_id=1, source_target_pairs={{2,0},{0,2},{3,1},{1,3},{6,4},{4,6},{7,5},{5,7},{10,8},{8,10},{11,... | collective-permute-start | bytes 196616 | tf_op jit(solution)/shard_map/ppermute | solution.py:65
  16.2 3.3 %copy-start.4 = (s32[2,2]{1,0:T(2,128)S(1)}, s32[2,2]{1,0:T(2,128)}, u32[]{:S(2)}) copy-start(s32[2,2]{1,0:T(2,128)} %halo_near.3) | copy-start | bytes 52
  20.1 5.6 %collective-permute-start.8 = (bf16[2,64,256]{2,1,0:T(8,128)(2,1)S(1)}, bf16[2,64,256]{2,1,0:T(8,128)(2,1)S(1)}, u32[]{:S(2)}, u32[]{:S(2)}) collective-permute-start(bf16[2,64,256]{2,1,0:T(8,128)(2,1)S(1)} %get-tuple-element.12), channel_id=1, source_target_pairs={{1,4},{5,8},{9,12},{0,13},{4,1},{8,5},{12,9},{13,0},{3,6},{7,10},{... | collective-permute-start | bytes 196616 | tf_op jit(solution)/shard_map/ppermute | solution.py:53
  20.1 5.5 %collective-permute-start.9 = (bf16[2,64,256]{2,1,0:T(8,128)(2,1)S(1)}, bf16[2,64,256]{2,1,0:T(8,128)(2,1)S(1)}, u32[]{:S(2)}, u32[]{:S(2)}) collective-permute-start(bf16[2,64,256]{2,1,0:T(8,128)(2,1)S(1)} %get-tuple-element.13), channel_id=1, source_target_pairs={{0,1},{4,5},{8,9},{12,13},{1,0},{5,4},{9,8},{13,12},{2,3},{6,7},{1... | collective-permute-start | bytes 196616 | tf_op jit(solution)/shard_map/ppermute | solution.py:53
  23.3 6.5 %copy-start.1 = (bf16[27,128,256]{2,1,0:T(8,128)(2,1)S(1)}, bf16[27,128,256]{2,1,0:T(8,128)(2,1)}, u32[]{:S(2)}) copy-start(bf16[27,128,256]{2,1,0:T(8,128)(2,1)} %weight.11) | copy-start | bytes 5308420
  27.1 7.3 %collective-permute-start.12 = (bf16[16,64,128]{2,1,0:T(8,128)(2,1)S(1)}, bf16[16,64,128]{2,1,0:T(8,128)(2,1)S(1)}, u32[]{:S(2)}, u32[]{:S(2)}) collective-permute-start(bf16[16,64,128]{2,1,0:T(8,128)(2,1)S(1)} %get-tuple-element.16.refs_0_), channel_id=1, source_target_pairs={{2,0},{0,2},{3,1},{1,3},{6,4},{4,6},{7,5},{5,7},{10,8},{8,10},{11,... | collective-permute-start | bytes 786440 | tf_op jit(solution)/shard_map/ppermute | solution.py:65
  28.3 4.2 %collective-permute-start.10 = (bf16[2,64,128]{2,1,0:T(8,128)(2,1)S(1)}, bf16[2,64,128]{2,1,0:T(8,128)(2,1)S(1)}, u32[]{:S(2)}, u32[]{:S(2)}) collective-permute-start(bf16[2,64,128]{2,1,0:T(8,128)(2,1)S(1)} %get-tuple-element.14), channel_id=1, source_target_pairs={{0,1},{4,5},{8,9},{12,13},{1,0},{5,4},{9,8},{13,12},{2,3},{6,7},{1... | collective-permute-start | bytes 98312 | tf_op jit(solution)/shard_map/ppermute | solution.py:53
  28.3 5.1 %collective-permute-start.11 = (bf16[2,64,128]{2,1,0:T(8,128)(2,1)S(1)}, bf16[2,64,128]{2,1,0:T(8,128)(2,1)S(1)}, u32[]{:S(2)}, u32[]{:S(2)}) collective-permute-start(bf16[2,64,128]{2,1,0:T(8,128)(2,1)S(1)} %get-tuple-element.15), channel_id=1, source_target_pairs={{1,4},{5,8},{9,12},{0,13},{4,1},{8,5},{12,9},{13,0},{3,6},{7,10},{... | collective-permute-start | bytes 98312 | tf_op jit(solution)/shard_map/ppermute | solution.py:53
  33.4 4.4 %copy-start.2 = (bf16[8,128,256]{2,1,0:T(8,128)(2,1)S(1)}, bf16[8,128,256]{2,1,0:T(8,128)(2,1)}, u32[]{:S(2)}) copy-start(bf16[8,128,256]{2,1,0:T(8,128)(2,1)} %down_weight.1) | copy-start | bytes 1572868
  33.4 4.3 %copy-start.5 = (s32[16,1]{0,1:T(1,128)S(1)}, s32[16,1]{0,1:T(1,128)}, u32[]{:S(2)}) copy-start(s32[16,1]{0,1:T(1,128)} %param.18) | copy-start | bytes 196
  33.5 4.3 %collective-permute-start.13 = (bf16[4,64,128]{2,1,0:T(8,128)(2,1)S(1)}, bf16[4,64,128]{2,1,0:T(8,128)(2,1)S(1)}, u32[]{:S(2)}, u32[]{:S(2)}) collective-permute-start(bf16[4,64,128]{2,1,0:T(8,128)(2,1)S(1)} %pack.1), channel_id=1, source_target_pairs={{2,0},{0,2},{3,1},{1,3},{6,4},{4,6},{7,5},{5,7},{10,8},{8,10},{11,... | collective-permute-start | bytes 196616 | tf_op jit(solution)/shard_map/ppermute | solution.py:65

commit v6 on v5

--- a/solution.py
+++ b/solution.py
@@ -88,9 +88,8 @@
 
 
 def assemble_kernel(bricks, subs, chans, keys, halo_near, *refs):
-    parts, (rows, even, odd, halo, semaphore) = dict(zip(keys, refs[:-5])), refs[-5:]
-    reach = halo.shape[1]
-    scalars = Scalars([halo_near], [halo], semaphore)
+    parts, (rows, even, odd) = dict(zip(keys, refs[:-3])), refs[-3:]
+    lists, reach = halo_near[...], halo_near.shape[1]
     place = Place()
     split = BLK // parts[0, 0].shape[1]
     for (jb, j), part in parts.items():
@@ -99,10 +98,12 @@
         for js in range(subs):
             sub = lax.rem(place.sub + js, subs)
             rows[(source * subs + sub) * chans + chan] = part[js]
-    scalars.wait()
     for j in range(reach):
-        even[pl.ds(j * split, split)] = rows[pl.ds(halo[place.parity, j] * split, split)]
-        odd[pl.ds(j * split, split)] = rows[pl.ds(halo[1 - place.parity, j] * split, split)]
+        up, down = lists[0, j], lists[1, j]
+        first = jnp.where(place.parity == 0, up, down)
+        second = jnp.where(place.parity == 0, down, up)
+        even[pl.ds(j * split, split)] = rows[pl.ds(first * split, split)]
+        odd[pl.ds(j * split, split)] = rows[pl.ds(second * split, split)]
 
 
 def assemble(halo, parts, bricks, subs, chans):
@@ -117,7 +118,6 @@
         ],
         in_specs=[VMEM] * (1 + len(parts)),
         out_specs=[VMEM] * 3,
-        scratch_shapes=scalar_scratch(halo),
         compiler_params=LIMIT,
         name="assemble",
     )(halo, *parts.values())
@@ -162,7 +162,7 @@
     rim[pl.ds(reach * place.parity, reach), :, lanes] = named(place, odd[...])
 
 
-def named_sums(table, scalars, given, weight, products, total):
+def named_sums(table, scalars, given, weight, products, begin, end):
     blocks, offsets = given.shape[0], table.shape[1]
     width, channels = weight.shape[1:]
     together = max(1, channels // width)
@@ -183,10 +183,10 @@
     scalars.wait()
 
     def one_block(n, carry):
-        running = total[n]
+        running = begin(n)
         for k in range(offsets):
             running = running + products[k, table[n, k]]
-        total[n] = running
+        end(n, running)
         return carry
 
     lax.fori_loop(0, table.shape[0], one_block, 0, unroll=min(table.shape[0], 16))
@@ -232,8 +232,14 @@
         source = other(place.brick, jb, bricks, -1)
         for js in range(subs):
             held[source * subs + lax.rem(place.sub + js, subs)] = part[js]
-    total[...] = before[...] if started else jnp.zeros(total.shape, F32)
-    named_sums(table, scalars, held, weight, products, total)
+
+    def begin(n):
+        return before[n] if started else jnp.zeros(total.shape[1:], F32)
+
+    def end(n, value):
+        total[n] = value
+
+    named_sums(table, scalars, held, weight, products, begin, end)
 
 
 def pieces_first(table, weight, parts, before, j, bricks, subs):
@@ -259,26 +265,27 @@
 
 
 def rim_first_kernel(odd, even, halo_near, table_near, vectors, own, weight, *refs):
-    hidden, even_out, odd_out, rim, products, total, halo, table, semaphore = refs
+    hidden, even_out, odd_out, rim, products, halo, table, semaphore = refs
     scalars = Scalars([halo_near, table_near], [halo, table], semaphore)
     reach = even.shape[0]
     place = Place()
     rim_blocks(place, even, odd, slice(None), rim)
-    total[...] = own[...]
-    named_sums(table, scalars, rim, weight, products, total)
-    value = total[...] * vectors[0:1][None] + vectors[1:2][None]
-    hidden[...] = jnp.maximum(value, 0.0).astype(BF16)
+    gain, bias = vectors[0:1], vectors[1:2]
+
+    def end(n, value):
+        hidden[n] = jnp.maximum(value * gain + bias, 0.0).astype(BF16)
+
+    named_sums(table, scalars, rim, weight, products, lambda n: own[n], end)
     for j in range(reach):
         even_out[j] = hidden[halo[place.parity, j]]
         odd_out[j] = hidden[halo[1 - place.parity, j]]
 
 
-def rim_scratch(count, reach, weight):
+def rim_scratch(reach, weight):
     offsets, width, channels = weight.shape
     return [
         pltpu.VMEM((2 * reach, BLK, channels), BF16),
         pltpu.VMEM((offsets, 2 * reach + 1, BLK, width), F32),
-        pltpu.VMEM((count, BLK, width), F32),
     ]
 
 
@@ -291,7 +298,7 @@
         ],
         in_specs=[VMEM] * 7,
         out_specs=[VMEM] * 3,
-        scratch_shapes=rim_scratch(count, reach, weight) + scalar_scratch(halo, table),
+        scratch_shapes=rim_scratch(reach, weight) + scalar_scratch(halo, table),
         compiler_params=LIMIT,
         cost_estimate=cost(2 * reach, weight),
         name="rim_first",
@@ -379,7 +386,11 @@
     total[...] = sums[0][...]
     for more in sums[1:]:
         total[...] += more[...]
-    named_sums(table, scalars, rim, weight, products, total)
+
+    def end(n, value):
+        total[n] = value
+
+    named_sums(table, scalars, rim, weight, products, lambda n: total[n], end)
     for c in range(chans):
 
         @pl.when(place.chan == c)
@@ -419,7 +430,8 @@
         out_shape=jax.ShapeDtypeStruct(slots, BF16),
         in_specs=[VMEM] * (8 + len(sums) + len(fars)),
         out_specs=VMEM,
-        scratch_shapes=rim_scratch(count, reach, weight)
+        scratch_shapes=rim_scratch(reach, weight)
+        + [pltpu.VMEM((count, BLK, width), F32)]
         + [pltpu.VMEM(slots, F32), pltpu.SMEM((bricks * subs,), jnp.int32)]
         + scalar_scratch(route, table),
         compiler_params=LIMIT,

time: 51.9 us -> 51.3 us (0.988)
  Pallas kernels: 14.1 us -> 13.4 us
where the time goes in v6:
time: 51.3 us; the launch traced here: 51.1 us
  starting transfers between devices  17.3 us (34%)
  Pallas kernels  13.4 us (26%)
  blocking collectives  11 us (21%)
  waiting for transfers between devices  6.29 us (12%)
  local copies, waits for them, and re-layouts  1.77 us (3%)
  matrix products  1.04 us (2%)
    all_to_all x1, blocking collectives, body(): lax.all_to_all(partial, ('brick', 'chan', 'sub'), split_axis=0, concat_ax...  11 us
    ppermute x6, starting transfers between devices, from_ahead(): lax.ppermute(block, axis, [((i + distance) % n, i) for i in range(n)])  8.15 us
    ppermute x3, starting transfers between devices, across(): lax.ppermute(block, 'brick', [(b, other(b, step, bricks)) for b in range(...  5.72 us
    pallas_call x2, Pallas kernels, own_second(): pl.pallas_call(functools.partial(own_second_kernel, nearest, chans), out_...  5.33 us
    pallas_call x2, Pallas kernels, pieces_first(): pl.pallas_call(functools.partial(pieces_first_kernel, bricks, subs, behin...  3.79 us
    ppermute x4, waiting for transfers between devices, owner_pairs(): lax.ppermute(block, ('brick', 'sub'), pairs + [(b, a) for a, b in pairs])  3.16 us
    ppermute x4, starting transfers between devices, owner_pairs(): lax.ppermute(block, ('brick', 'sub'), pairs + [(b, a) for a, b in pairs])  2.9 us
    ppermute x6, waiting for transfers between devices, from_ahead(): lax.ppermute(block, axis, [((i + distance) % n, i) for i in range(n)])  2.13 us
  transfers between devices with their start and end apart: 14, of which 7 were waited for; matrix products, arithmetic and copies ran while one was open for 2% of the time, Pallas kernels for 18%

profile of v6, /device:TPU:0, one launch (start us, length us, event | category | flops | bytes accessed | tf_op | source)
XLA Modules:
  0.0 51.1 jit_solution(16850876798321019306)
XLA Ops:
  0.0 0.9 %copy-done = bf16[512,256]{1,0:T(8,128)(2,1)S(1)} copy-done((bf16[512,256]{1,0:T(8,128)(2,1)S(1)}, bf16[512,256]{1,0:T(8,128)(2,1)}, u32[]{:S(2)}) %copy-start) | copy-done | bytes 262168
  1.0 1.0 %convolution_convert_fusion = bf16[512,256]{1,0:T(8,128)(2,1)S(1)} fusion(bf16[512,256]{1,0:T(8,128)(2,1)S(1)} %copy-done, s32[512]{0:T(512)} %bitcast.34), kind=kOutput, calls=%fused_computation | convolution fusion | flops 134610944 | bytes 526336 | tf_op jit(solution)/shard_map/dot_general | solution.py:87
  2.1 0.5 %collective-permute-start = (bf16[4,64,256]{2,1,0:T(8,128)(2,1)S(1)}, bf16[4,64,256]{2,1,0:T(8,128)(2,1)S(1)}, u32[]{:S(2)}, u32[]{:S(2)}) collective-permute-start(bf16[4,64,256]{2,1,0:T(8,128)(2,1)S(1)} %pad_maximum_fusion), channel_id=1, source_target_pairs={{0,1},{1,0},{2,3},{3,2},{4,5},{5,4},{6,7},{7,6},{8,9},{9,8},{10,11... | collective-permute-start | bytes 393224 | tf_op jit(solution)/shard_map/ppermute | solution.py:81
  2.6 0.8 %stack.50.vectors = f32[6,128]{1,0:T(8,128)S(1)} concatenate(f32[1,128]{1,0:T(1,128)} %bitcast.28, f32[1,128]{1,0:T(1,128)} %bitcast.29, f32[1,128]{1,0:T(1,128)} %bitcast.30, f32[1,128]{1,0:T(1,128)} %bitcast.31, f32[1,128]{1,0:T(1,128)} %bitcast.32, f32[1,128]{1,0:T(1,128)} %bitcast.33), dimensions={0} | concatenate | bytes 6144 | tf_op jit(solution)/shard_map/stack | solution.py:522
  3.4 0.2 collective-permute-done
  3.6 5.0 %collective-permute-start.1 = (bf16[2,64,256]{2,1,0:T(8,128)(2,1)S(1)}, bf16[2,64,256]{2,1,0:T(8,128)(2,1)S(1)}, u32[]{:S(2)}, u32[]{:S(2)}) collective-permute-start(bf16[2,64,256]{2,1,0:T(8,128)(2,1)S(1)} %pad_maximum_fusion.2), channel_id=1, source_target_pairs={{0,12},{4,8},{8,4},{12,0},{1,13},{5,9},{9,5},{13,1},{2,14},{6,10},... | collective-permute-start | bytes 196616 | tf_op jit(solution)/shard_map/ppermute | solution.py:76
  8.6 0.1 collective-permute-start.2
  8.7 0.6 %collective-permute-start.3 = (bf16[2,64,256]{2,1,0:T(8,128)(2,1)S(1)}, bf16[2,64,256]{2,1,0:T(8,128)(2,1)S(1)}, u32[]{:S(2)}, u32[]{:S(2)}) collective-permute-start(bf16[2,64,256]{2,1,0:T(8,128)(2,1)S(1)} %pad_maximum_fusion.4), channel_id=1, source_target_pairs={{0,8},{4,12},{8,0},{12,4},{1,9},{5,13},{9,1},{13,5},{2,10},{6,14},... | collective-permute-start | bytes 196616 | tf_op jit(solution)/shard_map/ppermute | solution.py:76
  9.4 1.7 %collective-permute-start.4 = (bf16[2,64,256]{2,1,0:T(8,128)(2,1)S(1)}, bf16[2,64,256]{2,1,0:T(8,128)(2,1)S(1)}, u32[]{:S(2)}, u32[]{:S(2)}) collective-permute-start(bf16[2,64,256]{2,1,0:T(8,128)(2,1)S(1)} %pad_maximum_fusion.1.refs_0_), channel_id=1, source_target_pairs={{2,0},{0,2},{3,1},{1,3},{6,4},{4,6},{7,5},{5,7},{10,8},{8,10},{11,... | collective-permute-start | bytes 196616 | tf_op jit(solution)/shard_map/ppermute | solution.py:65
  11.1 0.4 collective-permute-done.1.refs_1_
  11.5 1.8 %collective-permute-start.5 = (bf16[2,64,256]{2,1,0:T(8,128)(2,1)S(1)}, bf16[2,64,256]{2,1,0:T(8,128)(2,1)S(1)}, u32[]{:S(2)}, u32[]{:S(2)}) collective-permute-start(bf16[2,64,256]{2,1,0:T(8,128)(2,1)S(1)} %collective-permute-done.1.refs_1_), channel_id=1, source_target_pairs={{2,0},{0,2},{3,1},{1,3},{6,4},{4,6},{7,5},{5,7},{10,8},{8,10},{11,... | collective-permute-start | bytes 196616 | tf_op jit(solution)/shard_map/ppermute | solution.py:65
  13.3 0.4 collective-permute-done.2.refs_2_
  13.7 1.5 %collective-permute-start.6 = (bf16[2,64,256]{2,1,0:T(8,128)(2,1)S(1)}, bf16[2,64,256]{2,1,0:T(8,128)(2,1)S(1)}, u32[]{:S(2)}, u32[]{:S(2)}) collective-permute-start(bf16[2,64,256]{2,1,0:T(8,128)(2,1)S(1)} %collective-permute-done.2.refs_2_), channel_id=1, source_target_pairs={{2,0},{0,2},{3,1},{1,3},{6,4},{4,6},{7,5},{5,7},{10,8},{8,10},{11,... | collective-permute-start | bytes 196616 | tf_op jit(solution)/shard_map/ppermute | solution.py:65
  15.2 0.9 %collective-permute-start.7 = (bf16[2,64,256]{2,1,0:T(8,128)(2,1)S(1)}, bf16[2,64,256]{2,1,0:T(8,128)(2,1)S(1)}, u32[]{:S(2)}, u32[]{:S(2)}) collective-permute-start(bf16[2,64,256]{2,1,0:T(8,128)(2,1)S(1)} %collective-permute-done.3.refs_3_), channel_id=1, source_target_pairs={{2,0},{0,2},{3,1},{1,3},{6,4},{4,6},{7,5},{5,7},{10,8},{8,10},{11,... | collective-permute-start | bytes 196616 | tf_op jit(solution)/shard_map/ppermute | solution.py:65
  16.2 1.9 %pieces_first.2.refs_4_ = f32[16,64,128]{2,1,0:T(8,128)S(1)} custom-call(s32[16,27]{1,0:T(8,128)S(1)} %get-tuple-element.29.table_near, bf16[27,128,256]{2,1,0:T(8,128)(2,1)S(1)} %copy-done.6, bf16[2,64,256]{2,1,0:T(8,128)(2,1)S(1)} %pad_maximum_fusion.1.refs_0_, bf16[2,64,256]{2,1,0:T(8,128)(2,1)S(1)} %collective-permute-done.1.refs_1_, ...), custom_call_target="tpu_custom_call" | custom-call | flops 1811939328 | tf_op jit(solution)/shard_map/pieces_first/pallas_call | solution.py:251
  18.1 1.4 %collective-permute-done.7.refs_7_.refs_3_ = bf16[2,64,256]{2,1,0:T(8,128)(2,1)S(1)} collective-permute-done((bf16[2,64,256]{2,1,0:T(8,128)(2,1)S(1)}, bf16[2,64,256]{2,1,0:T(8,128)(2,1)S(1)}, u32[]{:S(2)}, u32[]{:S(2)}) %collective-permute-start.7) | collective-permute-done | bytes 65568 | tf_op jit(solution)/shard_map/ppermute | solution.py:65
  19.5 0.1 assemble.1
  19.6 0.1 collective-permute-start.8
  19.7 1.3 %collective-permute-start.9 = (bf16[2,64,256]{2,1,0:T(8,128)(2,1)S(1)}, bf16[2,64,256]{2,1,0:T(8,128)(2,1)S(1)}, u32[]{:S(2)}, u32[]{:S(2)}) collective-permute-start(bf16[2,64,256]{2,1,0:T(8,128)(2,1)S(1)} %get-tuple-element.13), channel_id=1, source_target_pairs={{0,1},{4,5},{8,9},{12,13},{1,0},{5,4},{9,8},{13,12},{2,3},{6,7},{1... | collective-permute-start | bytes 196616 | tf_op jit(solution)/shard_map/ppermute | solution.py:53
  20.9 1.9 %pieces_first.3.own = f32[16,64,128]{2,1,0:T(8,128)S(1)} custom-call(s32[16,27]{1,0:T(8,128)S(1)} %get-tuple-element.31.table_near, bf16[27,128,256]{2,1,0:T(8,128)(2,1)S(1)} %copy-done.6, bf16[2,64,256]{2,1,0:T(8,128)(2,1)S(1)} %collective-permute-done.4.refs_4_.refs_0_, bf16[2,64,256]{2,1,0:T(8,128)(2,1)S(1)} %collective-permute-done.5.refs_5_.refs_1_, ...), custom_call_target="tpu_custom_call" | custom-call | flops 1811939328 | tf_op jit(solution)/shard_map/pieces_first/pallas_call | solution.py:251
  22.9 2.3 %collective-permute-done.8.odd = bf16[2,64,256]{2,1,0:T(8,128)(2,1)S(1)} collective-permute-done((bf16[2,64,256]{2,1,0:T(8,128)(2,1)S(1)}, bf16[2,64,256]{2,1,0:T(8,128)(2,1)S(1)}, u32[]{:S(2)}, u32[]{:S(2)}) %collective-permute-start.8) | collective-permute-done | bytes 65568 | tf_op jit(solution)/shard_map/ppermute | solution.py:53
  25.2 1.4 %rim_first.1 = (bf16[16,64,128]{2,1,0:T(8,128)(2,1)S(1)}, bf16[2,64,128]{2,1,0:T(8,128)(2,1)S(1)}, bf16[2,64,128]{2,1,0:T(8,128)(2,1)S(1)}) custom-call(bf16[2,64,256]{2,1,0:T(8,128)(2,1)S(1)} %collective-permute-done.8.odd, bf16[2,64,256]{2,1,0:T(8,128)(2,1)S(1)} %collective-permute-done.9.even, s32[2,2]{1,0:T(2,128)S(1)} %copy-done.4, ...), custom_call_target="tpu_custom_call" | custom-call | flops 905969664 | tf_op jit(solution)/shard_map/rim_first/pallas_call | solution.py:294
  26.6 1.2 %collective-permute-start.12 = (bf16[16,64,128]{2,1,0:T(8,128)(2,1)S(1)}, bf16[16,64,128]{2,1,0:T(8,128)(2,1)S(1)}, u32[]{:S(2)}, u32[]{:S(2)}) collective-permute-start(bf16[16,64,128]{2,1,0:T(8,128)(2,1)S(1)} %get-tuple-element.16.refs_0_), channel_id=1, source_target_pairs={{2,0},{0,2},{3,1},{1,3},{6,4},{4,6},{7,5},{5,7},{10,8},{8,10},{11,... | collective-permute-start | bytes 786440 | tf_op jit(solution)/shard_map/ppermute | solution.py:65
  27.8 1.6 %collective-permute-start.11 = (bf16[2,64,128]{2,1,0:T(8,128)(2,1)S(1)}, bf16[2,64,128]{2,1,0:T(8,128)(2,1)S(1)}, u32[]{:S(2)}, u32[]{:S(2)}) collective-permute-start(bf16[2,64,128]{2,1,0:T(8,128)(2,1)S(1)} %get-tuple-element.15), channel_id=1, source_target_pairs={{1,4},{5,8},{9,12},{0,13},{4,1},{8,5},{12,9},{13,0},{3,6},{7,10},{... | collective-permute-start | bytes 98312 | tf_op jit(solution)/shard_map/ppermute | solution.py:53
  29.3 2.7 %own_second.2.refs_0_.refs_2_ = f32[16,64,128]{2,1,0:T(8,128)S(1)} custom-call(s32[16,27]{1,0:T(8,128)S(1)} %copy-done.3, bf16[27,128,256]{2,1,0:T(8,128)(2,1)S(1)} %copy-done.1, bf16[16,64,128]{2,1,0:T(8,128)(2,1)S(1)} %get-tuple-element.16.refs_0_), custom_call_target="tpu_custom_call" | custom-call | flops 1811939328 | tf_op jit(solution)/shard_map/own_second/pallas_call | solution.py:354
  32.0 0.9 %collective-permute-done.11.odd.refs_1_ = bf16[2,64,128]{2,1,0:T(8,128)(2,1)S(1)} collective-permute-done((bf16[2,64,128]{2,1,0:T(8,128)(2,1)S(1)}, bf16[2,64,128]{2,1,0:T(8,128)(2,1)S(1)}, u32[]{:S(2)}, u32[]{:S(2)}) %collective-permute-start.11) | collective-permute-done | bytes 32800 | tf_op jit(solution)/shard_map/ppermute | solution.py:53
  32.9 1.0 %collective-permute-start.13 = (bf16[4,64,128]{2,1,0:T(8,128)(2,1)S(1)}, bf16[4,64,128]{2,1,0:T(8,128)(2,1)S(1)}, u32[]{:S(2)}, u32[]{:S(2)}) collective-permute-start(bf16[4,64,128]{2,1,0:T(8,128)(2,1)S(1)} %pack.1), channel_id=1, source_target_pairs={{2,0},{0,2},{3,1},{1,3},{6,4},{4,6},{7,5},{5,7},{10,8},{8,10},{11,... | collective-permute-start | bytes 196616 | tf_op jit(solution)/shard_map/ppermute | solution.py:65
  33.9 2.7 %own_second.3.refs_3_ = f32[16,64,128]{2,1,0:T(8,128)S(1)} custom-call(s32[16,27]{1,0:T(8,128)S(1)} %copy-done.3, bf16[27,128,256]{2,1,0:T(8,128)(2,1)S(1)} %copy-done.1, bf16[16,64,128]{2,1,0:T(8,128)(2,1)S(1)} %collective-permute-done.12.refs_0_), custom_call_target="tpu_custom_call" | custom-call | flops 1811939328 | tf_op jit(solution)/shard_map/own_second/pallas_call | solution.py:354
  36.6 0.7 %collective-permute-done.13.refs_4_ = bf16[4,64,128]{2,1,0:T(8,128)(2,1)S(1)} collective-permute-done((bf16[4,64,128]{2,1,0:T(8,128)(2,1)S(1)}, bf16[4,64,128]{2,1,0:T(8,128)(2,1)S(1)}, u32[]{:S(2)}, u32[]{:S(2)}) %collective-permute-start.13) | collective-permute-done | bytes 65568 | tf_op jit(solution)/shard_map/ppermute | solution.py:65
  37.3 2.1 %rim_second.1 = bf16[16,32,128]{2,1,0:T(8,128)(2,1)S(1)} custom-call(s32[1,16]{1,0:T(1,128)S(1)} %bitcast.26, s32[16,27]{1,0:T(8,128)S(1)} %get-tuple-element.30.table_near, f32[6,128]{1,0:T(8,128)S(1)} %stack.50.vectors, bf16[16,64,256]{2,1,0:T(8,128)(2,1)S(1)} %get-tuple-element.11.rows, bf16[27,128,256]{2,1,0:T(8,128)(2,1)S(1)} %copy-done.1, ...), custom_call_target="tpu_custom_call" | custom-call | flops 905969664 | tf_op jit(solution)/shard_map/rim_second/pallas_call | solution.py:428
  39.3 11.0 %all_to_all.5.parts = bf16[16,32,128]{2,1,0:T(8,128)(2,1)S(1)} all-to-all(bf16[16,32,128]{2,1,0:T(8,128)(2,1)S(1)} %rim_second.1), channel_id=1, replica_groups=mesh['groups'=2,'brick'=4,'chan'=2,'sub'=2] {'brick','chan','sub'}, dimensions={0} | all-to-all | bytes 262144 | tf_op jit(solution)/shard_map/all_to_all | solution.py:563
  50.4 0.7 %arrived_tiles.1 = bf16[1,128,256]{2,1,0:T(8,128)(2,1)} custom-call(f32[6,128]{1,0:T(8,128)S(1)} %stack.50.vectors, bf16[16,32,128]{2,1,0:T(8,128)(2,1)S(1)} %all_to_all.5.parts), custom_call_target="tpu_custom_call" | custom-call | tf_op jit(solution)/shard_map/arrived_tiles/pallas_call | solution.py:460
  (30 shorter events, 0.2 us)
Async XLA Ops:
  0.0 1.0 %copy-start = (bf16[512,256]{1,0:T(8,128)(2,1)S(1)}, bf16[512,256]{1,0:T(8,128)(2,1)}, u32[]{:S(2)}) copy-start(bf16[512,256]{1,0:T(8,128)(2,1)} %param.14) | copy-start | bytes 786436
  0.0 3.3 %copy-start.3 = (s32[16,27]{1,0:T(8,128)S(1)}, s32[16,27]{1,0:T(8,128)}, u32[]{:S(2)}) copy-start(s32[16,27]{1,0:T(8,128)} %table_near.3) | copy-start | bytes 5188
  0.0 16.1 %copy-start.6 = (bf16[27,128,256]{2,1,0:T(8,128)(2,1)S(1)}, bf16[27,128,256]{2,1,0:T(8,128)(2,1)}, u32[]{:S(2)}) copy-start(bf16[27,128,256]{2,1,0:T(8,128)(2,1)} %weight.8) | copy-start | bytes 5308420
  2.1 1.5 %collective-permute-start = (bf16[4,64,256]{2,1,0:T(8,128)(2,1)S(1)}, bf16[4,64,256]{2,1,0:T(8,128)(2,1)S(1)}, u32[]{:S(2)}, u32[]{:S(2)}) collective-permute-start(bf16[4,64,256]{2,1,0:T(8,128)(2,1)S(1)} %pad_maximum_fusion), channel_id=1, source_target_pairs={{0,1},{1,0},{2,3},{3,2},{4,5},{5,4},{6,7},{7,6},{8,9},{9,8},{10,11... | collective-permute-start | bytes 393224 | tf_op jit(solution)/shard_map/ppermute | solution.py:81
  3.6 7.9 %collective-permute-start.1 = (bf16[2,64,256]{2,1,0:T(8,128)(2,1)S(1)}, bf16[2,64,256]{2,1,0:T(8,128)(2,1)S(1)}, u32[]{:S(2)}, u32[]{:S(2)}) collective-permute-start(bf16[2,64,256]{2,1,0:T(8,128)(2,1)S(1)} %pad_maximum_fusion.2), channel_id=1, source_target_pairs={{0,12},{4,8},{8,4},{12,0},{1,13},{5,9},{9,5},{13,1},{2,14},{6,10},... | collective-permute-start | bytes 196616 | tf_op jit(solution)/shard_map/ppermute | solution.py:76
  8.6 5.1 %collective-permute-start.2 = (bf16[2,64,256]{2,1,0:T(8,128)(2,1)S(1)}, bf16[2,64,256]{2,1,0:T(8,128)(2,1)S(1)}, u32[]{:S(2)}, u32[]{:S(2)}) collective-permute-start(bf16[2,64,256]{2,1,0:T(8,128)(2,1)S(1)} %pad_maximum_fusion.3), channel_id=1, source_target_pairs={{0,4},{4,0},{8,12},{12,8},{1,5},{5,1},{9,13},{13,9},{2,6},{6,2},{1... | collective-permute-start | bytes 196616 | tf_op jit(solution)/shard_map/ppermute | solution.py:76
  8.7 6.5 %collective-permute-start.3 = (bf16[2,64,256]{2,1,0:T(8,128)(2,1)S(1)}, bf16[2,64,256]{2,1,0:T(8,128)(2,1)S(1)}, u32[]{:S(2)}, u32[]{:S(2)}) collective-permute-start(bf16[2,64,256]{2,1,0:T(8,128)(2,1)S(1)} %pad_maximum_fusion.4), channel_id=1, source_target_pairs={{0,8},{4,12},{8,0},{12,4},{1,9},{5,13},{9,1},{13,5},{2,10},{6,14},... | collective-permute-start | bytes 196616 | tf_op jit(solution)/shard_map/ppermute | solution.py:76
  9.4 8.7 %collective-permute-start.4 = (bf16[2,64,256]{2,1,0:T(8,128)(2,1)S(1)}, bf16[2,64,256]{2,1,0:T(8,128)(2,1)S(1)}, u32[]{:S(2)}, u32[]{:S(2)}) collective-permute-start(bf16[2,64,256]{2,1,0:T(8,128)(2,1)S(1)} %pad_maximum_fusion.1.refs_0_), channel_id=1, source_target_pairs={{2,0},{0,2},{3,1},{1,3},{6,4},{4,6},{7,5},{5,7},{10,8},{8,10},{11,... | collective-permute-start | bytes 196616 | tf_op jit(solution)/shard_map/ppermute | solution.py:65
  11.5 6.5 %collective-permute-start.5 = (bf16[2,64,256]{2,1,0:T(8,128)(2,1)S(1)}, bf16[2,64,256]{2,1,0:T(8,128)(2,1)S(1)}, u32[]{:S(2)}, u32[]{:S(2)}) collective-permute-start(bf16[2,64,256]{2,1,0:T(8,128)(2,1)S(1)} %collective-permute-done.1.refs_1_), channel_id=1, source_target_pairs={{2,0},{0,2},{3,1},{1,3},{6,4},{4,6},{7,5},{5,7},{10,8},{8,10},{11,... | collective-permute-start | bytes 196616 | tf_op jit(solution)/shard_map/ppermute | solution.py:65
  13.7 4.3 %collective-permute-start.6 = (bf16[2,64,256]{2,1,0:T(8,128)(2,1)S(1)}, bf16[2,64,256]{2,1,0:T(8,128)(2,1)S(1)}, u32[]{:S(2)}, u32[]{:S(2)}) collective-permute-start(bf16[2,64,256]{2,1,0:T(8,128)(2,1)S(1)} %collective-permute-done.2.refs_2_), channel_id=1, source_target_pairs={{2,0},{0,2},{3,1},{1,3},{6,4},{4,6},{7,5},{5,7},{10,8},{8,10},{11,... | collective-permute-start | bytes 196616 | tf_op jit(solution)/shard_map/ppermute | solution.py:65
  15.2 4.3 %collective-permute-start.7 = (bf16[2,64,256]{2,1,0:T(8,128)(2,1)S(1)}, bf16[2,64,256]{2,1,0:T(8,128)(2,1)S(1)}, u32[]{:S(2)}, u32[]{:S(2)}) collective-permute-start(bf16[2,64,256]{2,1,0:T(8,128)(2,1)S(1)} %collective-permute-done.3.refs_3_), channel_id=1, source_target_pairs={{2,0},{0,2},{3,1},{1,3},{6,4},{4,6},{7,5},{5,7},{10,8},{8,10},{11,... | collective-permute-start | bytes 196616 | tf_op jit(solution)/shard_map/ppermute | solution.py:65
  16.2 3.3 %copy-start.4 = (s32[2,2]{1,0:T(2,128)S(1)}, s32[2,2]{1,0:T(2,128)}, u32[]{:S(2)}) copy-start(s32[2,2]{1,0:T(2,128)} %halo_near.3) | copy-start | bytes 52
  19.6 5.6 %collective-permute-start.8 = (bf16[2,64,256]{2,1,0:T(8,128)(2,1)S(1)}, bf16[2,64,256]{2,1,0:T(8,128)(2,1)S(1)}, u32[]{:S(2)}, u32[]{:S(2)}) collective-permute-start(bf16[2,64,256]{2,1,0:T(8,128)(2,1)S(1)} %get-tuple-element.12), channel_id=1, source_target_pairs={{1,4},{5,8},{9,12},{0,13},{4,1},{8,5},{12,9},{13,0},{3,6},{7,10},{... | collective-permute-start | bytes 196616 | tf_op jit(solution)/shard_map/ppermute | solution.py:53
  19.7 5.5 %collective-permute-start.9 = (bf16[2,64,256]{2,1,0:T(8,128)(2,1)S(1)}, bf16[2,64,256]{2,1,0:T(8,128)(2,1)S(1)}, u32[]{:S(2)}, u32[]{:S(2)}) collective-permute-start(bf16[2,64,256]{2,1,0:T(8,128)(2,1)S(1)} %get-tuple-element.13), channel_id=1, source_target_pairs={{0,1},{4,5},{8,9},{12,13},{1,0},{5,4},{9,8},{13,12},{2,3},{6,7},{1... | collective-permute-start | bytes 196616 | tf_op jit(solution)/shard_map/ppermute | solution.py:53
  22.9 6.5 %copy-start.1 = (bf16[27,128,256]{2,1,0:T(8,128)(2,1)S(1)}, bf16[27,128,256]{2,1,0:T(8,128)(2,1)}, u32[]{:S(2)}) copy-start(bf16[27,128,256]{2,1,0:T(8,128)(2,1)} %weight.11) | copy-start | bytes 5308420
  26.6 7.3 %collective-permute-start.12 = (bf16[16,64,128]{2,1,0:T(8,128)(2,1)S(1)}, bf16[16,64,128]{2,1,0:T(8,128)(2,1)S(1)}, u32[]{:S(2)}, u32[]{:S(2)}) collective-permute-start(bf16[16,64,128]{2,1,0:T(8,128)(2,1)S(1)} %get-tuple-element.16.refs_0_), channel_id=1, source_target_pairs={{2,0},{0,2},{3,1},{1,3},{6,4},{4,6},{7,5},{5,7},{10,8},{8,10},{11,... | collective-permute-start | bytes 786440 | tf_op jit(solution)/shard_map/ppermute | solution.py:65
  27.8 4.2 %collective-permute-start.10 = (bf16[2,64,128]{2,1,0:T(8,128)(2,1)S(1)}, bf16[2,64,128]{2,1,0:T(8,128)(2,1)S(1)}, u32[]{:S(2)}, u32[]{:S(2)}) collective-permute-start(bf16[2,64,128]{2,1,0:T(8,128)(2,1)S(1)} %get-tuple-element.14), channel_id=1, source_target_pairs={{0,1},{4,5},{8,9},{12,13},{1,0},{5,4},{9,8},{13,12},{2,3},{6,7},{1... | collective-permute-start | bytes 98312 | tf_op jit(solution)/shard_map/ppermute | solution.py:53
  27.8 5.1 %collective-permute-start.11 = (bf16[2,64,128]{2,1,0:T(8,128)(2,1)S(1)}, bf16[2,64,128]{2,1,0:T(8,128)(2,1)S(1)}, u32[]{:S(2)}, u32[]{:S(2)}) collective-permute-start(bf16[2,64,128]{2,1,0:T(8,128)(2,1)S(1)} %get-tuple-element.15), channel_id=1, source_target_pairs={{1,4},{5,8},{9,12},{0,13},{4,1},{8,5},{12,9},{13,0},{3,6},{7,10},{... | collective-permute-start | bytes 98312 | tf_op jit(solution)/shard_map/ppermute | solution.py:53
  32.9 4.4 %copy-start.2 = (bf16[8,128,256]{2,1,0:T(8,128)(2,1)S(1)}, bf16[8,128,256]{2,1,0:T(8,128)(2,1)}, u32[]{:S(2)}) copy-start(bf16[8,128,256]{2,1,0:T(8,128)(2,1)} %down_weight.1) | copy-start | bytes 1572868
  32.9 4.3 %copy-start.5 = (s32[16,1]{0,1:T(1,128)S(1)}, s32[16,1]{0,1:T(1,128)}, u32[]{:S(2)}) copy-start(s32[16,1]{0,1:T(1,128)} %param.18) | copy-start | bytes 196
  32.9 4.3 %collective-permute-start.13 = (bf16[4,64,128]{2,1,0:T(8,128)(2,1)S(1)}, bf16[4,64,128]{2,1,0:T(8,128)(2,1)S(1)}, u32[]{:S(2)}, u32[]{:S(2)}) collective-permute-start(bf16[4,64,128]{2,1,0:T(8,128)(2,1)S(1)} %pack.1), channel_id=1, source_target_pairs={{2,0},{0,2},{3,1},{1,3},{6,4},{4,6},{7,5},{5,7},{10,8},{8,10},{11,... | collective-permute-start | bytes 196616 | tf_op jit(solution)/shard_map/ppermute | solution.py:65

commit v7 on v6

--- a/solution.py
+++ b/solution.py
@@ -402,11 +402,11 @@
             )
 
     refined = jnp.maximum(total[...], 0.0).reshape(count, CHILDREN, CELLS, width)
-    coarse = None
-    for o in range(CHILDREN):
-        child = refined[:, o].reshape(count * CELLS, width).astype(BF16)
-        product = lax.dot_general(child, down_weight[o], NN, preferred_element_type=F32)
-        coarse = product if coarse is None else coarse + product
+    beside = jnp.concatenate(
+        [refined[:, o].reshape(count * CELLS, width) for o in range(CHILDREN)], axis=1
+    ).astype(BF16)
+    down = down_weight[...].reshape(CHILDREN * width, down_weight.shape[2])
+    coarse = lax.dot_general(beside, down, NN, preferred_element_type=F32)
     slots[...] = jnp.full(slots.shape, ABSENT, F32)
     for owner in range(bricks * subs):
         seen[owner] = 0

time: 51.3 us -> 51.1 us (level)
  no operation moved by 1% of the time
where the time goes in v7:
time: 51.1 us; the launch traced here: 50.9 us
  starting transfers between devices  17.3 us (34%)
  Pallas kernels  13.3 us (26%)
  blocking collectives  11 us (22%)
  waiting for transfers between devices  6.29 us (12%)
  local copies, waits for them, and re-layouts  1.77 us (3%)
  matrix products  1.04 us (2%)
    all_to_all x1, blocking collectives, body(): lax.all_to_all(partial, ('brick', 'chan', 'sub'), split_axis=0, concat_ax...  11 us
    ppermute x6, starting transfers between devices, from_ahead(): lax.ppermute(block, axis, [((i + distance) % n, i) for i in range(n)])  8.15 us
    ppermute x3, starting transfers between devices, across(): lax.ppermute(block, 'brick', [(b, other(b, step, bricks)) for b in range(...  5.72 us
    pallas_call x2, Pallas kernels, own_second(): pl.pallas_call(functools.partial(own_second_kernel, nearest, chans), out_...  5.33 us
    pallas_call x2, Pallas kernels, pieces_first(): pl.pallas_call(functools.partial(pieces_first_kernel, bricks, subs, behin...  3.79 us
    ppermute x4, waiting for transfers between devices, owner_pairs(): lax.ppermute(block, ('brick', 'sub'), pairs + [(b, a) for a, b in pairs])  3.17 us
    ppermute x4, starting transfers between devices, owner_pairs(): lax.ppermute(block, ('brick', 'sub'), pairs + [(b, a) for a, b in pairs])  2.9 us
    ppermute x6, waiting for transfers between devices, from_ahead(): lax.ppermute(block, axis, [((i + distance) % n, i) for i in range(n)])  2.13 us
  transfers between devices with their start and end apart: 14, of which 7 were waited for; matrix products, arithmetic and copies ran while one was open for 2% of the time, Pallas kernels for 18%

profile of v7, /device:TPU:0, one launch (start us, length us, event | category | flops | bytes accessed | tf_op | source)
XLA Modules:
  0.0 50.9 jit_solution(10662526858553307322)
XLA Ops:
  0.0 0.9 %copy-done = bf16[512,256]{1,0:T(8,128)(2,1)S(1)} copy-done((bf16[512,256]{1,0:T(8,128)(2,1)S(1)}, bf16[512,256]{1,0:T(8,128)(2,1)}, u32[]{:S(2)}) %copy-start) | copy-done | bytes 262168
  1.0 1.0 %convolution_convert_fusion = bf16[512,256]{1,0:T(8,128)(2,1)S(1)} fusion(bf16[512,256]{1,0:T(8,128)(2,1)S(1)} %copy-done, s32[512]{0:T(512)} %bitcast.34), kind=kOutput, calls=%fused_computation | convolution fusion | flops 134610944 | bytes 526336 | tf_op jit(solution)/shard_map/dot_general | solution.py:87
  2.1 0.5 %collective-permute-start = (bf16[4,64,256]{2,1,0:T(8,128)(2,1)S(1)}, bf16[4,64,256]{2,1,0:T(8,128)(2,1)S(1)}, u32[]{:S(2)}, u32[]{:S(2)}) collective-permute-start(bf16[4,64,256]{2,1,0:T(8,128)(2,1)S(1)} %pad_maximum_fusion), channel_id=1, source_target_pairs={{0,1},{1,0},{2,3},{3,2},{4,5},{5,4},{6,7},{7,6},{8,9},{9,8},{10,11... | collective-permute-start | bytes 393224 | tf_op jit(solution)/shard_map/ppermute | solution.py:81
  2.6 0.8 %stack.50.vectors = f32[6,128]{1,0:T(8,128)S(1)} concatenate(f32[1,128]{1,0:T(1,128)} %bitcast.28, f32[1,128]{1,0:T(1,128)} %bitcast.29, f32[1,128]{1,0:T(1,128)} %bitcast.30, f32[1,128]{1,0:T(1,128)} %bitcast.31, f32[1,128]{1,0:T(1,128)} %bitcast.32, f32[1,128]{1,0:T(1,128)} %bitcast.33), dimensions={0} | concatenate | bytes 6144 | tf_op jit(solution)/shard_map/stack | solution.py:522
  3.4 0.2 collective-permute-done
  3.6 5.0 %collective-permute-start.1 = (bf16[2,64,256]{2,1,0:T(8,128)(2,1)S(1)}, bf16[2,64,256]{2,1,0:T(8,128)(2,1)S(1)}, u32[]{:S(2)}, u32[]{:S(2)}) collective-permute-start(bf16[2,64,256]{2,1,0:T(8,128)(2,1)S(1)} %pad_maximum_fusion.2), channel_id=1, source_target_pairs={{0,12},{4,8},{8,4},{12,0},{1,13},{5,9},{9,5},{13,1},{2,14},{6,10},... | collective-permute-start | bytes 196616 | tf_op jit(solution)/shard_map/ppermute | solution.py:76
  8.6 0.1 collective-permute-start.2
  8.7 0.6 %collective-permute-start.3 = (bf16[2,64,256]{2,1,0:T(8,128)(2,1)S(1)}, bf16[2,64,256]{2,1,0:T(8,128)(2,1)S(1)}, u32[]{:S(2)}, u32[]{:S(2)}) collective-permute-start(bf16[2,64,256]{2,1,0:T(8,128)(2,1)S(1)} %pad_maximum_fusion.4), channel_id=1, source_target_pairs={{0,8},{4,12},{8,0},{12,4},{1,9},{5,13},{9,1},{13,5},{2,10},{6,14},... | collective-permute-start | bytes 196616 | tf_op jit(solution)/shard_map/ppermute | solution.py:76
  9.4 1.7 %collective-permute-start.4 = (bf16[2,64,256]{2,1,0:T(8,128)(2,1)S(1)}, bf16[2,64,256]{2,1,0:T(8,128)(2,1)S(1)}, u32[]{:S(2)}, u32[]{:S(2)}) collective-permute-start(bf16[2,64,256]{2,1,0:T(8,128)(2,1)S(1)} %pad_maximum_fusion.1.refs_0_), channel_id=1, source_target_pairs={{2,0},{0,2},{3,1},{1,3},{6,4},{4,6},{7,5},{5,7},{10,8},{8,10},{11,... | collective-permute-start | bytes 196616 | tf_op jit(solution)/shard_map/ppermute | solution.py:65
  11.1 0.4 collective-permute-done.1.refs_1_
  11.5 1.8 %collective-permute-start.5 = (bf16[2,64,256]{2,1,0:T(8,128)(2,1)S(1)}, bf16[2,64,256]{2,1,0:T(8,128)(2,1)S(1)}, u32[]{:S(2)}, u32[]{:S(2)}) collective-permute-start(bf16[2,64,256]{2,1,0:T(8,128)(2,1)S(1)} %collective-permute-done.1.refs_1_), channel_id=1, source_target_pairs={{2,0},{0,2},{3,1},{1,3},{6,4},{4,6},{7,5},{5,7},{10,8},{8,10},{11,... | collective-permute-start | bytes 196616 | tf_op jit(solution)/shard_map/ppermute | solution.py:65
  13.3 0.4 collective-permute-done.2.refs_2_
  13.7 1.5 %collective-permute-start.6 = (bf16[2,64,256]{2,1,0:T(8,128)(2,1)S(1)}, bf16[2,64,256]{2,1,0:T(8,128)(2,1)S(1)}, u32[]{:S(2)}, u32[]{:S(2)}) collective-permute-start(bf16[2,64,256]{2,1,0:T(8,128)(2,1)S(1)} %collective-permute-done.2.refs_2_), channel_id=1, source_target_pairs={{2,0},{0,2},{3,1},{1,3},{6,4},{4,6},{7,5},{5,7},{10,8},{8,10},{11,... | collective-permute-start | bytes 196616 | tf_op jit(solution)/shard_map/ppermute | solution.py:65
  15.2 0.9 %collective-permute-start.7 = (bf16[2,64,256]{2,1,0:T(8,128)(2,1)S(1)}, bf16[2,64,256]{2,1,0:T(8,128)(2,1)S(1)}, u32[]{:S(2)}, u32[]{:S(2)}) collective-permute-start(bf16[2,64,256]{2,1,0:T(8,128)(2,1)S(1)} %collective-permute-done.3.refs_3_), channel_id=1, source_target_pairs={{2,0},{0,2},{3,1},{1,3},{6,4},{4,6},{7,5},{5,7},{10,8},{8,10},{11,... | collective-permute-start | bytes 196616 | tf_op jit(solution)/shard_map/ppermute | solution.py:65
  16.2 1.9 %pieces_first.2.refs_4_ = f32[16,64,128]{2,1,0:T(8,128)S(1)} custom-call(s32[16,27]{1,0:T(8,128)S(1)} %get-tuple-element.29.table_near, bf16[27,128,256]{2,1,0:T(8,128)(2,1)S(1)} %copy-done.6, bf16[2,64,256]{2,1,0:T(8,128)(2,1)S(1)} %pad_maximum_fusion.1.refs_0_, bf16[2,64,256]{2,1,0:T(8,128)(2,1)S(1)} %collective-permute-done.1.refs_1_, ...), custom_call_target="tpu_custom_call" | custom-call | flops 1811939328 | tf_op jit(solution)/shard_map/pieces_first/pallas_call | solution.py:251
  18.1 1.4 %collective-permute-done.7.refs_7_.refs_3_ = bf16[2,64,256]{2,1,0:T(8,128)(2,1)S(1)} collective-permute-done((bf16[2,64,256]{2,1,0:T(8,128)(2,1)S(1)}, bf16[2,64,256]{2,1,0:T(8,128)(2,1)S(1)}, u32[]{:S(2)}, u32[]{:S(2)}) %collective-permute-start.7) | collective-permute-done | bytes 65568 | tf_op jit(solution)/shard_map/ppermute | solution.py:65
  19.5 0.1 assemble.1
  19.6 0.1 collective-permute-start.8
  19.7 1.3 %collective-permute-start.9 = (bf16[2,64,256]{2,1,0:T(8,128)(2,1)S(1)}, bf16[2,64,256]{2,1,0:T(8,128)(2,1)S(1)}, u32[]{:S(2)}, u32[]{:S(2)}) collective-permute-start(bf16[2,64,256]{2,1,0:T(8,128)(2,1)S(1)} %get-tuple-element.13), channel_id=1, source_target_pairs={{0,1},{4,5},{8,9},{12,13},{1,0},{5,4},{9,8},{13,12},{2,3},{6,7},{1... | collective-permute-start | bytes 196616 | tf_op jit(solution)/shard_map/ppermute | solution.py:53
  20.9 1.9 %pieces_first.3.own = f32[16,64,128]{2,1,0:T(8,128)S(1)} custom-call(s32[16,27]{1,0:T(8,128)S(1)} %get-tuple-element.31.table_near, bf16[27,128,256]{2,1,0:T(8,128)(2,1)S(1)} %copy-done.6, bf16[2,64,256]{2,1,0:T(8,128)(2,1)S(1)} %collective-permute-done.4.refs_4_.refs_0_, bf16[2,64,256]{2,1,0:T(8,128)(2,1)S(1)} %collective-permute-done.5.refs_5_.refs_1_, ...), custom_call_target="tpu_custom_call" | custom-call | flops 1811939328 | tf_op jit(solution)/shard_map/pieces_first/pallas_call | solution.py:251
  22.9 2.3 %collective-permute-done.8.odd = bf16[2,64,256]{2,1,0:T(8,128)(2,1)S(1)} collective-permute-done((bf16[2,64,256]{2,1,0:T(8,128)(2,1)S(1)}, bf16[2,64,256]{2,1,0:T(8,128)(2,1)S(1)}, u32[]{:S(2)}, u32[]{:S(2)}) %collective-permute-start.8) | collective-permute-done | bytes 65568 | tf_op jit(solution)/shard_map/ppermute | solution.py:53
  25.2 1.4 %rim_first.1 = (bf16[16,64,128]{2,1,0:T(8,128)(2,1)S(1)}, bf16[2,64,128]{2,1,0:T(8,128)(2,1)S(1)}, bf16[2,64,128]{2,1,0:T(8,128)(2,1)S(1)}) custom-call(bf16[2,64,256]{2,1,0:T(8,128)(2,1)S(1)} %collective-permute-done.8.odd, bf16[2,64,256]{2,1,0:T(8,128)(2,1)S(1)} %collective-permute-done.9.even, s32[2,2]{1,0:T(2,128)S(1)} %copy-done.4, ...), custom_call_target="tpu_custom_call" | custom-call | flops 905969664 | tf_op jit(solution)/shard_map/rim_first/pallas_call | solution.py:294
  26.6 1.2 %collective-permute-start.12 = (bf16[16,64,128]{2,1,0:T(8,128)(2,1)S(1)}, bf16[16,64,128]{2,1,0:T(8,128)(2,1)S(1)}, u32[]{:S(2)}, u32[]{:S(2)}) collective-permute-start(bf16[16,64,128]{2,1,0:T(8,128)(2,1)S(1)} %get-tuple-element.16.refs_0_), channel_id=1, source_target_pairs={{2,0},{0,2},{3,1},{1,3},{6,4},{4,6},{7,5},{5,7},{10,8},{8,10},{11,... | collective-permute-start | bytes 786440 | tf_op jit(solution)/shard_map/ppermute | solution.py:65
  27.8 1.6 %collective-permute-start.11 = (bf16[2,64,128]{2,1,0:T(8,128)(2,1)S(1)}, bf16[2,64,128]{2,1,0:T(8,128)(2,1)S(1)}, u32[]{:S(2)}, u32[]{:S(2)}) collective-permute-start(bf16[2,64,128]{2,1,0:T(8,128)(2,1)S(1)} %get-tuple-element.15), channel_id=1, source_target_pairs={{1,4},{5,8},{9,12},{0,13},{4,1},{8,5},{12,9},{13,0},{3,6},{7,10},{... | collective-permute-start | bytes 98312 | tf_op jit(solution)/shard_map/ppermute | solution.py:53
  29.3 2.7 %own_second.2.refs_0_.refs_2_ = f32[16,64,128]{2,1,0:T(8,128)S(1)} custom-call(s32[16,27]{1,0:T(8,128)S(1)} %copy-done.3, bf16[27,128,256]{2,1,0:T(8,128)(2,1)S(1)} %copy-done.1, bf16[16,64,128]{2,1,0:T(8,128)(2,1)S(1)} %get-tuple-element.16.refs_0_), custom_call_target="tpu_custom_call" | custom-call | flops 1811939328 | tf_op jit(solution)/shard_map/own_second/pallas_call | solution.py:354
  32.0 0.9 %collective-permute-done.11.odd.refs_1_ = bf16[2,64,128]{2,1,0:T(8,128)(2,1)S(1)} collective-permute-done((bf16[2,64,128]{2,1,0:T(8,128)(2,1)S(1)}, bf16[2,64,128]{2,1,0:T(8,128)(2,1)S(1)}, u32[]{:S(2)}, u32[]{:S(2)}) %collective-permute-start.11) | collective-permute-done | bytes 32800 | tf_op jit(solution)/shard_map/ppermute | solution.py:53
  32.9 1.0 %collective-permute-start.13 = (bf16[4,64,128]{2,1,0:T(8,128)(2,1)S(1)}, bf16[4,64,128]{2,1,0:T(8,128)(2,1)S(1)}, u32[]{:S(2)}, u32[]{:S(2)}) collective-permute-start(bf16[4,64,128]{2,1,0:T(8,128)(2,1)S(1)} %pack.1), channel_id=1, source_target_pairs={{2,0},{0,2},{3,1},{1,3},{6,4},{4,6},{7,5},{5,7},{10,8},{8,10},{11,... | collective-permute-start | bytes 196616 | tf_op jit(solution)/shard_map/ppermute | solution.py:65
  33.9 2.7 %own_second.3.refs_3_ = f32[16,64,128]{2,1,0:T(8,128)S(1)} custom-call(s32[16,27]{1,0:T(8,128)S(1)} %copy-done.3, bf16[27,128,256]{2,1,0:T(8,128)(2,1)S(1)} %copy-done.1, bf16[16,64,128]{2,1,0:T(8,128)(2,1)S(1)} %collective-permute-done.12.refs_0_), custom_call_target="tpu_custom_call" | custom-call | flops 1811939328 | tf_op jit(solution)/shard_map/own_second/pallas_call | solution.py:354
  36.6 0.7 %collective-permute-done.13.refs_4_ = bf16[4,64,128]{2,1,0:T(8,128)(2,1)S(1)} collective-permute-done((bf16[4,64,128]{2,1,0:T(8,128)(2,1)S(1)}, bf16[4,64,128]{2,1,0:T(8,128)(2,1)S(1)}, u32[]{:S(2)}, u32[]{:S(2)}) %collective-permute-start.13) | collective-permute-done | bytes 65568 | tf_op jit(solution)/shard_map/ppermute | solution.py:65
  37.3 1.9 %rim_second.1 = bf16[16,32,128]{2,1,0:T(8,128)(2,1)S(1)} custom-call(s32[1,16]{1,0:T(1,128)S(1)} %bitcast.26, s32[16,27]{1,0:T(8,128)S(1)} %get-tuple-element.30.table_near, f32[6,128]{1,0:T(8,128)S(1)} %stack.50.vectors, bf16[16,64,256]{2,1,0:T(8,128)(2,1)S(1)} %get-tuple-element.11.rows, bf16[27,128,256]{2,1,0:T(8,128)(2,1)S(1)} %copy-done.1, ...), custom_call_target="tpu_custom_call" | custom-call | flops 905969664 | tf_op jit(solution)/shard_map/rim_second/pallas_call | solution.py:428
  39.2 11.0 %all_to_all.5.parts = bf16[16,32,128]{2,1,0:T(8,128)(2,1)S(1)} all-to-all(bf16[16,32,128]{2,1,0:T(8,128)(2,1)S(1)} %rim_second.1), channel_id=1, replica_groups=mesh['groups'=2,'brick'=4,'chan'=2,'sub'=2] {'brick','chan','sub'}, dimensions={0} | all-to-all | bytes 262144 | tf_op jit(solution)/shard_map/all_to_all | solution.py:563
  50.2 0.7 %arrived_tiles.1 = bf16[1,128,256]{2,1,0:T(8,128)(2,1)} custom-call(f32[6,128]{1,0:T(8,128)S(1)} %stack.50.vectors, bf16[16,32,128]{2,1,0:T(8,128)(2,1)S(1)} %all_to_all.5.parts), custom_call_target="tpu_custom_call" | custom-call | tf_op jit(solution)/shard_map/arrived_tiles/pallas_call | solution.py:460
  (30 shorter events, 0.2 us)
Async XLA Ops:
  0.0 1.0 %copy-start = (bf16[512,256]{1,0:T(8,128)(2,1)S(1)}, bf16[512,256]{1,0:T(8,128)(2,1)}, u32[]{:S(2)}) copy-start(bf16[512,256]{1,0:T(8,128)(2,1)} %param.14) | copy-start | bytes 786436
  0.0 3.3 %copy-start.3 = (s32[16,27]{1,0:T(8,128)S(1)}, s32[16,27]{1,0:T(8,128)}, u32[]{:S(2)}) copy-start(s32[16,27]{1,0:T(8,128)} %table_near.3) | copy-start | bytes 5188
  0.0 16.1 %copy-start.6 = (bf16[27,128,256]{2,1,0:T(8,128)(2,1)S(1)}, bf16[27,128,256]{2,1,0:T(8,128)(2,1)}, u32[]{:S(2)}) copy-start(bf16[27,128,256]{2,1,0:T(8,128)(2,1)} %weight.8) | copy-start | bytes 5308420
  2.1 1.5 %collective-permute-start = (bf16[4,64,256]{2,1,0:T(8,128)(2,1)S(1)}, bf16[4,64,256]{2,1,0:T(8,128)(2,1)S(1)}, u32[]{:S(2)}, u32[]{:S(2)}) collective-permute-start(bf16[4,64,256]{2,1,0:T(8,128)(2,1)S(1)} %pad_maximum_fusion), channel_id=1, source_target_pairs={{0,1},{1,0},{2,3},{3,2},{4,5},{5,4},{6,7},{7,6},{8,9},{9,8},{10,11... | collective-permute-start | bytes 393224 | tf_op jit(solution)/shard_map/ppermute | solution.py:81
  3.6 7.9 %collective-permute-start.1 = (bf16[2,64,256]{2,1,0:T(8,128)(2,1)S(1)}, bf16[2,64,256]{2,1,0:T(8,128)(2,1)S(1)}, u32[]{:S(2)}, u32[]{:S(2)}) collective-permute-start(bf16[2,64,256]{2,1,0:T(8,128)(2,1)S(1)} %pad_maximum_fusion.2), channel_id=1, source_target_pairs={{0,12},{4,8},{8,4},{12,0},{1,13},{5,9},{9,5},{13,1},{2,14},{6,10},... | collective-permute-start | bytes 196616 | tf_op jit(solution)/shard_map/ppermute | solution.py:76
  8.6 5.1 %collective-permute-start.2 = (bf16[2,64,256]{2,1,0:T(8,128)(2,1)S(1)}, bf16[2,64,256]{2,1,0:T(8,128)(2,1)S(1)}, u32[]{:S(2)}, u32[]{:S(2)}) collective-permute-start(bf16[2,64,256]{2,1,0:T(8,128)(2,1)S(1)} %pad_maximum_fusion.3), channel_id=1, source_target_pairs={{0,4},{4,0},{8,12},{12,8},{1,5},{5,1},{9,13},{13,9},{2,6},{6,2},{1... | collective-permute-start | bytes 196616 | tf_op jit(solution)/shard_map/ppermute | solution.py:76
  8.7 6.5 %collective-permute-start.3 = (bf16[2,64,256]{2,1,0:T(8,128)(2,1)S(1)}, bf16[2,64,256]{2,1,0:T(8,128)(2,1)S(1)}, u32[]{:S(2)}, u32[]{:S(2)}) collective-permute-start(bf16[2,64,256]{2,1,0:T(8,128)(2,1)S(1)} %pad_maximum_fusion.4), channel_id=1, source_target_pairs={{0,8},{4,12},{8,0},{12,4},{1,9},{5,13},{9,1},{13,5},{2,10},{6,14},... | collective-permute-start | bytes 196616 | tf_op jit(solution)/shard_map/ppermute | solution.py:76
  9.4 8.7 %collective-permute-start.4 = (bf16[2,64,256]{2,1,0:T(8,128)(2,1)S(1)}, bf16[2,64,256]{2,1,0:T(8,128)(2,1)S(1)}, u32[]{:S(2)}, u32[]{:S(2)}) collective-permute-start(bf16[2,64,256]{2,1,0:T(8,128)(2,1)S(1)} %pad_maximum_fusion.1.refs_0_), channel_id=1, source_target_pairs={{2,0},{0,2},{3,1},{1,3},{6,4},{4,6},{7,5},{5,7},{10,8},{8,10},{11,... | collective-permute-start | bytes 196616 | tf_op jit(solution)/shard_map/ppermute | solution.py:65
  11.5 6.5 %collective-permute-start.5 = (bf16[2,64,256]{2,1,0:T(8,128)(2,1)S(1)}, bf16[2,64,256]{2,1,0:T(8,128)(2,1)S(1)}, u32[]{:S(2)}, u32[]{:S(2)}) collective-permute-start(bf16[2,64,256]{2,1,0:T(8,128)(2,1)S(1)} %collective-permute-done.1.refs_1_), channel_id=1, source_target_pairs={{2,0},{0,2},{3,1},{1,3},{6,4},{4,6},{7,5},{5,7},{10,8},{8,10},{11,... | collective-permute-start | bytes 196616 | tf_op jit(solution)/shard_map/ppermute | solution.py:65
  13.7 4.3 %collective-permute-start.6 = (bf16[2,64,256]{2,1,0:T(8,128)(2,1)S(1)}, bf16[2,64,256]{2,1,0:T(8,128)(2,1)S(1)}, u32[]{:S(2)}, u32[]{:S(2)}) collective-permute-start(bf16[2,64,256]{2,1,0:T(8,128)(2,1)S(1)} %collective-permute-done.2.refs_2_), channel_id=1, source_target_pairs={{2,0},{0,2},{3,1},{1,3},{6,4},{4,6},{7,5},{5,7},{10,8},{8,10},{11,... | collective-permute-start | bytes 196616 | tf_op jit(solution)/shard_map/ppermute | solution.py:65
  15.2 4.3 %collective-permute-start.7 = (bf16[2,64,256]{2,1,0:T(8,128)(2,1)S(1)}, bf16[2,64,256]{2,1,0:T(8,128)(2,1)S(1)}, u32[]{:S(2)}, u32[]{:S(2)}) collective-permute-start(bf16[2,64,256]{2,1,0:T(8,128)(2,1)S(1)} %collective-permute-done.3.refs_3_), channel_id=1, source_target_pairs={{2,0},{0,2},{3,1},{1,3},{6,4},{4,6},{7,5},{5,7},{10,8},{8,10},{11,... | collective-permute-start | bytes 196616 | tf_op jit(solution)/shard_map/ppermute | solution.py:65
  16.2 3.3 %copy-start.4 = (s32[2,2]{1,0:T(2,128)S(1)}, s32[2,2]{1,0:T(2,128)}, u32[]{:S(2)}) copy-start(s32[2,2]{1,0:T(2,128)} %halo_near.3) | copy-start | bytes 52
  19.6 5.6 %collective-permute-start.8 = (bf16[2,64,256]{2,1,0:T(8,128)(2,1)S(1)}, bf16[2,64,256]{2,1,0:T(8,128)(2,1)S(1)}, u32[]{:S(2)}, u32[]{:S(2)}) collective-permute-start(bf16[2,64,256]{2,1,0:T(8,128)(2,1)S(1)} %get-tuple-element.12), channel_id=1, source_target_pairs={{1,4},{5,8},{9,12},{0,13},{4,1},{8,5},{12,9},{13,0},{3,6},{7,10},{... | collective-permute-start | bytes 196616 | tf_op jit(solution)/shard_map/ppermute | solution.py:53
  19.7 5.5 %collective-permute-start.9 = (bf16[2,64,256]{2,1,0:T(8,128)(2,1)S(1)}, bf16[2,64,256]{2,1,0:T(8,128)(2,1)S(1)}, u32[]{:S(2)}, u32[]{:S(2)}) collective-permute-start(bf16[2,64,256]{2,1,0:T(8,128)(2,1)S(1)} %get-tuple-element.13), channel_id=1, source_target_pairs={{0,1},{4,5},{8,9},{12,13},{1,0},{5,4},{9,8},{13,12},{2,3},{6,7},{1... | collective-permute-start | bytes 196616 | tf_op jit(solution)/shard_map/ppermute | solution.py:53
  22.9 6.5 %copy-start.1 = (bf16[27,128,256]{2,1,0:T(8,128)(2,1)S(1)}, bf16[27,128,256]{2,1,0:T(8,128)(2,1)}, u32[]{:S(2)}) copy-start(bf16[27,128,256]{2,1,0:T(8,128)(2,1)} %weight.11) | copy-start | bytes 5308420
  26.6 7.3 %collective-permute-start.12 = (bf16[16,64,128]{2,1,0:T(8,128)(2,1)S(1)}, bf16[16,64,128]{2,1,0:T(8,128)(2,1)S(1)}, u32[]{:S(2)}, u32[]{:S(2)}) collective-permute-start(bf16[16,64,128]{2,1,0:T(8,128)(2,1)S(1)} %get-tuple-element.16.refs_0_), channel_id=1, source_target_pairs={{2,0},{0,2},{3,1},{1,3},{6,4},{4,6},{7,5},{5,7},{10,8},{8,10},{11,... | collective-permute-start | bytes 786440 | tf_op jit(solution)/shard_map/ppermute | solution.py:65
  27.8 4.2 %collective-permute-start.10 = (bf16[2,64,128]{2,1,0:T(8,128)(2,1)S(1)}, bf16[2,64,128]{2,1,0:T(8,128)(2,1)S(1)}, u32[]{:S(2)}, u32[]{:S(2)}) collective-permute-start(bf16[2,64,128]{2,1,0:T(8,128)(2,1)S(1)} %get-tuple-element.14), channel_id=1, source_target_pairs={{0,1},{4,5},{8,9},{12,13},{1,0},{5,4},{9,8},{13,12},{2,3},{6,7},{1... | collective-permute-start | bytes 98312 | tf_op jit(solution)/shard_map/ppermute | solution.py:53
  27.8 5.1 %collective-permute-start.11 = (bf16[2,64,128]{2,1,0:T(8,128)(2,1)S(1)}, bf16[2,64,128]{2,1,0:T(8,128)(2,1)S(1)}, u32[]{:S(2)}, u32[]{:S(2)}) collective-permute-start(bf16[2,64,128]{2,1,0:T(8,128)(2,1)S(1)} %get-tuple-element.15), channel_id=1, source_target_pairs={{1,4},{5,8},{9,12},{0,13},{4,1},{8,5},{12,9},{13,0},{3,6},{7,10},{... | collective-permute-start | bytes 98312 | tf_op jit(solution)/shard_map/ppermute | solution.py:53
  32.9 4.4 %copy-start.2 = (bf16[8,128,256]{2,1,0:T(8,128)(2,1)S(1)}, bf16[8,128,256]{2,1,0:T(8,128)(2,1)}, u32[]{:S(2)}) copy-start(bf16[8,128,256]{2,1,0:T(8,128)(2,1)} %down_weight.1) | copy-start | bytes 1572868
  32.9 4.3 %copy-start.5 = (s32[16,1]{0,1:T(1,128)S(1)}, s32[16,1]{0,1:T(1,128)}, u32[]{:S(2)}) copy-start(s32[16,1]{0,1:T(1,128)} %param.18) | copy-start | bytes 196
  32.9 4.3 %collective-permute-start.13 = (bf16[4,64,128]{2,1,0:T(8,128)(2,1)S(1)}, bf16[4,64,128]{2,1,0:T(8,128)(2,1)S(1)}, u32[]{:S(2)}, u32[]{:S(2)}) collective-permute-start(bf16[4,64,128]{2,1,0:T(8,128)(2,1)S(1)} %pack.1), channel_id=1, source_target_pairs={{2,0},{0,2},{3,1},{1,3},{6,4},{4,6},{7,5},{5,7},{10,8},{8,10},{11,... | collective-permute-start | bytes 196616 | tf_op jit(solution)/shard_map/ppermute | solution.py:65
